TPU v7x, 32 devices: a whole 2x2x4 slice. The times are simulated.
32 devices in a mesh: dp: 8 (over y, x, core), expert: 4 (over z).
Axes of the slice: x: 2, y: 2, z: 4, core: 2. Of those that a mesh axis runs over, the one named last changes fastest.
Arguments:
- tokens: bfloat16 [2048, 1024], P(('dp', 'expert')), may hold values from -6 to 6
- expert_ids: int32 [2048, 2], P(('dp', 'expert')), may hold values from 0 to 7, all different within a row; in each aligned block of 64 rows (0 to 63, 64 to 127, ...) at most 20 rows name the same one
- gate_weights: float32 [2048, 2], P(('dp', 'expert')), may hold values from 0.2 to 1
- w_gate: bfloat16 [8, 1024, 4096], P('expert', None, 'dp'), may hold values from -0.1875 to 0.1875
- w_up: bfloat16 [8, 1024, 4096], P('expert', None, 'dp'), may hold values from -0.1875 to 0.1875
- w_down: bfloat16 [8, 4096, 1024], P('expert', 'dp'), may hold values from -0.09375 to 0.09375
- cotangent: bfloat16 [2048, 1024], P(('dp', 'expert')), may hold values from -6 to 6
Outputs:
- mixed: bfloat16 [2048, 1024], P(('dp', 'expert'))
- grad_tokens: bfloat16 [2048, 1024], P(('dp', 'expert'))
- grad_gate: bfloat16 [8, 1024, 4096], P('expert', None, 'dp')
- grad_up: bfloat16 [8, 1024, 4096], P('expert', None, 'dp')
- grad_down: bfloat16 [8, 4096, 1024], P('expert', 'dp')
Inputs may be any that keep to these rules, and one draw needn't show every extreme that they name: `expert_ids`: in every aligned block of 64 rows (the rows of one device) no expert is named more than 20 times, a bound that some block reaches; the 2 experts of a row differ.
All inputs are finite; a program needn't handle non-finite values.
Results may differ from a plain program's by a relative error of at most 0.019.
Values may be sent and summed in bfloat16 or wider, within the bound.
No kernel may reach another device: no remote copies, remote signals or barrier semaphores. Data moves between devices by JAX's collectives and lax.ppermute only.
A program may use at most 192 MiB of HBM per device.

v0:
```python
import jax
import jax.numpy as jnp
from jax import lax
from jax.sharding import PartitionSpec as P


def spread_one(buffer):
    arrived = lax.all_to_all(buffer, "expert", split_axis=0, concat_axis=0, tiled=True)
    return lax.all_gather(arrived[None], "dp", axis=0, tiled=True)


def collect(term_fn):
    summed = lax.psum_scatter(
        term_fn(jnp.int32(0), 1 * lax.axis_size("dp")).astype(jnp.bfloat16),
        "dp",
        scatter_dimension=0,
        tiled=True,
    )
    return lax.all_to_all(summed, "expert", split_axis=1, concat_axis=1, tiled=True)


def body(tokens, expert_ids, gate_weights, w_gate, w_up, w_down, cotangent):
    owners = lax.axis_size("expert")
    tok_count = tokens.shape[0]
    width = tokens.shape[1]
    top_count = expert_ids.shape[1]
    exp_local = w_gate.shape[0]
    experts_all = exp_local * owners
    capacity = max(2, 5 * tok_count * top_count // (4 * experts_all))
    flat = expert_ids.reshape(-1)
    onehot = (flat[:, None] == jnp.arange(experts_all, dtype=jnp.int32)[None, :]).astype(jnp.int32)
    before = jnp.sum((jnp.cumsum(onehot, axis=0) - onehot) * onehot, axis=1)
    slot = flat * capacity + before
    placer = (jnp.arange(experts_all * capacity, dtype=jnp.int32)[:, None] == slot[None, :]).astype(
        jnp.bfloat16
    )

    def place(rows):
        buffer = jnp.dot(placer, rows, preferred_element_type=jnp.float32).astype(jnp.bfloat16)
        return buffer.reshape(owners, exp_local, capacity, width)

    def unpack(results):
        flat_out = results.reshape(experts_all * capacity, width)
        return (
            jnp.take(flat_out, slot, axis=0)
            .astype(jnp.float32)
            .reshape(tok_count, top_count, width)
        )

    rows_x = jnp.repeat(tokens, top_count, axis=0)
    buf_x = place(rows_x)
    rows_d = (gate_weights[:, :, None] * cotangent[:, None, :].astype(jnp.float32)).reshape(
        tok_count * top_count, width
    )
    buf_d = place(rows_d.astype(jnp.bfloat16))
    gathered = spread_one(buf_x)
    gate = jnp.einsum("pcjkd,jdf->pcjkf", gathered, w_gate, preferred_element_type=jnp.float32)
    up = jnp.einsum("pcjkd,jdf->pcjkf", gathered, w_up, preferred_element_type=jnp.float32)
    sig = jax.nn.sigmoid(gate)
    act = gate * sig
    hidden = (act * up).astype(jnp.bfloat16)

    def forward_term(start, count):
        return jnp.einsum("pcjkf,jfd->pcjkd", hidden, w_down, preferred_element_type=jnp.float32)

    expert_out = collect(forward_term)
    mixed = jnp.sum(gate_weights[:, :, None] * unpack(expert_out), axis=1).astype(jnp.bfloat16)
    grad_rows = spread_one(buf_d)
    dact = jnp.einsum("pcjkd,jfd->pcjkf", grad_rows, w_down, preferred_element_type=jnp.float32)
    grad_hg = (dact * up * sig * (1.0 + gate * (1.0 - sig))).astype(jnp.bfloat16)
    grad_hu = (dact * act).astype(jnp.bfloat16)
    grad_down = jnp.einsum(
        "pcjkf,pcjkd->jfd", hidden, grad_rows, preferred_element_type=jnp.float32
    ).astype(jnp.bfloat16)
    grad_gate = jnp.einsum(
        "pcjkd,pcjkf->jdf", gathered, grad_hg, preferred_element_type=jnp.float32
    ).astype(jnp.bfloat16)
    grad_up = jnp.einsum(
        "pcjkd,pcjkf->jdf", gathered, grad_hu, preferred_element_type=jnp.float32
    ).astype(jnp.bfloat16)

    def backward_term(start, count):
        total = jnp.einsum("pcjkf,jdf->pcjkd", grad_hg, w_gate, preferred_element_type=jnp.float32)
        return total + jnp.einsum(
            "pcjkf,jdf->pcjkd", grad_hu, w_up, preferred_element_type=jnp.float32
        )

    token_part = collect(backward_term)
    grad_tokens = jnp.sum(unpack(token_part), axis=1).astype(jnp.bfloat16)
    return (mixed, grad_tokens, grad_gate, grad_up, grad_down)


def solution(mesh):
    placed = (
        P(("dp", "expert"), None),
        P(("dp", "expert"), None),
        P(("dp", "expert"), None),
        P("expert", None, "dp"),
        P("expert", None, "dp"),
        P("expert", "dp", None),
        P(("dp", "expert"), None),
    )
    return jax.shard_map(
        body,
        mesh=mesh,
        in_specs=placed,
        out_specs=(
            P(("dp", "expert"), None),
            P(("dp", "expert"), None),
            P("expert", None, "dp"),
            P("expert", None, "dp"),
            P("expert", "dp", None),
        ),
        check_vma=False,
    )
```

profile of v0, /device:TPU:0, one launch (start us, length us, event | category | flops | bytes accessed | tf_op | source)
XLA Modules:
  0.0 248.3 jit_solution(16407178834496961551)
XLA Ops:
  7.2 0.0 all-gather.5.cloned.1.call-start
  7.2 0.9 copy.37
  8.2 0.1 reshape.60
  8.3 0.1 fusion.36
  8.4 0.2 reduce_window_sum.11
  8.6 0.2 select_reduce_fusion
  8.8 1.0 broadcast_in_dim.24
  9.8 0.1 reshape.61
  9.9 0.2 convolution_convert_fusion.1
  10.2 0.1 reshape.62
  10.2 0.3 copy.38
  10.6 16.5 %all_to_all.20 = bf16[4,2,20,1024]{3,1,2,0:T(2,128)(2,1)} all-to-all(bf16[4,2,20,1024]{3,1,2,0:T(2,128)(2,1)S(1)} %copy.38), channel_id=1, replica_groups=mesh['dp'=8,'expert'=4] {'expert'}, dimensions={0} | all-to-all | bytes 655360 | tf_op jit(solution)/shard_map/all_to_all | solution.py:8
  27.1 0.0 all-gather.5.cloned.1.call-update
  27.1 0.0 all-gather.7.cloned.1.call-start
  27.2 0.1 copy.36
  27.3 0.6 copy-done.11
  27.9 0.1 mul.67
  28.0 0.1 mul.69
  28.2 0.4 mul.70
  28.5 0.3 convolution_convert_fusion
  28.9 0.1 reshape.66
  28.9 0.3 copy.44
  29.3 12.1 %all_to_all.21 = bf16[4,2,20,1024]{3,1,2,0:T(2,128)(2,1)} all-to-all(bf16[4,2,20,1024]{3,1,2,0:T(2,128)(2,1)S(1)} %copy.44), channel_id=1, replica_groups=mesh['dp'=8,'expert'=4] {'expert'}, dimensions={0} | all-to-all | bytes 655360 | tf_op jit(solution)/shard_map/all_to_all | solution.py:8
  41.4 0.0 all-gather.7.cloned.1.call-update
  41.5 0.0 all-reduce.5.cloned.1.call-start
  41.5 15.0 %all-gather.5.cloned.1.call-done = bf16[32,2,20,1024]{3,1,2,0:T(2,128)(2,1)} async-done(((bf16[4,2,20,1024]{3,1,2,0:T(2,128)(2,1)}), bf16[32,2,20,1024]{3,1,2,0:T(2,128)(2,1)}) %all-gather.5.cloned.1.call-update) | async-done | bytes 2621456 | tf_op jit(solution)/shard_map/all_gather | solution.py:9
  56.5 2.8 %copy.39 = bf16[32,2,20,1024]{3,2,0,1:T(8,128)(2,1)S(1)} copy(bf16[32,2,20,1024]{3,1,2,0:T(2,128)(2,1)} %all-gather.5.cloned.1.call-done) | data formatting | bytes 5242880 | tf_op jit(solution)/shard_map/all_gather | solution.py:9
  59.3 3.5 %fusion.17 = f32[2,8,4,20,512]{4,3,2,1,0:T(8,128)} fusion(bf16[8,4,2,20,1024]{4,3,1,0,2:T(8,128)(2,1)S(1)} %bitcast.87, bf16[2,1024,512]{2,1,0:T(8,128)(2,1)S(1)} %copy-done.6), kind=kOutput, calls=%fused_computation.30 | convolution fusion | flops 1342177280 | bytes 7340032 | tf_op jit(solution)/shard_map/pcjkd,jdf->pcjkf/dot_general | solution.py:58
  62.8 3.5 %fusion.21 = f32[2,8,4,20,512]{4,3,2,1,0:T(8,128)} fusion(bf16[8,4,2,20,1024]{4,3,1,0,2:T(8,128)(2,1)S(1)} %bitcast.88, bf16[2,1024,512]{2,1,0:T(8,128)(2,1)S(1)} %copy-done.8), kind=kOutput, calls=%fused_computation.34 | convolution fusion | flops 1342177280 | bytes 7340032 | tf_op jit(solution)/shard_map/pcjkd,jdf->pcjkf/dot_general | solution.py:57
  66.3 22.2 %all-gather.7.cloned.1.call-done = bf16[32,2,20,1024]{3,1,2,0:T(2,128)(2,1)} async-done(((bf16[4,2,20,1024]{3,1,2,0:T(2,128)(2,1)}), bf16[32,2,20,1024]{3,1,2,0:T(2,128)(2,1)}) %all-gather.7.cloned.1.call-update) | async-done | bytes 2621456 | tf_op jit(solution)/shard_map/all_gather | solution.py:9
  88.5 2.8 %copy.45 = bf16[32,2,20,1024]{3,2,0,1:T(8,128)(2,1)S(1)} copy(bf16[32,2,20,1024]{3,1,2,0:T(2,128)(2,1)} %all-gather.7.cloned.1.call-done) | data formatting | bytes 5242880 | tf_op jit(solution)/shard_map/all_gather | solution.py:9
  91.3 6.0 %fusion.4 = (bf16[8,4,2,20,512]{4,3,1,0,2:T(8,128)(2,1)S(1)}, bf16[8,4,2,20,512]{4,3,1,0,2:T(8,128)(2,1)S(1)}, bf16[8,4,2,20,512]{4,3,1,0,2:T(8,128)(2,1)S(1)}) fusion(f32[2,8,4,20,512]{4,3,2,1,0:T(8,128)} %fusion.21, f32[2,8,4,20,512]{4,3,2,1,0:T(8,128)S(1)} %copy-done.15, bf16[8,4,2,20,1024]{4,3,1,0,2:T(8,128)(2,1)S(1)} %bitcast.91, ...), kind=kOutput, calls=%fused_computation.12 | convolution fusion | flops 1352007680 | bytes 13893632 | tf_op jit(solution)/shard_map/pcjkd,jfd->pcjkf/dot_general | solution.py:69
  97.4 1.8 convert_bitcast_fusion
  99.3 3.7 %copy.40 = bf16[8,4,2,20,1024]{4,1,3,2,0:T(4,128)(2,1)} copy(bf16[8,4,2,20,1024]{4,3,1,0,2:T(8,128)(2,1)S(1)} %convert_bitcast_fusion) | data formatting | bytes 5242880 | tf_op jit(solution)/shard_map/convert_element_type | solution.py:14
  103.0 1.9 fusion.19
  104.9 1.9 fusion
  106.8 3.6 %copy.46 = bf16[8,4,2,20,1024]{4,1,3,2,0:T(4,128)(2,1)} copy(bf16[8,4,2,20,1024]{4,3,1,0,2:T(8,128)(2,1)S(1)} %fusion) | data formatting | bytes 5242880 | tf_op jit(solution)/shard_map/convert_element_type | solution.py:14
  110.5 0.0 all-reduce.5.cloned.1.call-update
  110.5 0.6 copy-done.14
  111.1 0.6 dynamic-slice
  111.7 0.2 copy-done.17
  111.9 5.2 %bitcast_convert_fusion = bf16[2,512,1024]{2,1,0:T(8,128)(2,1)} fusion(bf16[8,4,2,20,1024]{4,3,1,0,2:T(8,128)(2,1)} %bitcast.92, bf16[8,4,2,20,512]{4,3,1,0,2:T(8,128)(2,1)S(1)} %copy-done.17), kind=kOutput, calls=%fused_computation.3 | convolution fusion | flops 1343225856 | bytes 6029312 | tf_op jit(solution)/shard_map/pcjkf,pcjkd->jfd/dot_general | solution.py:72
  117.1 86.4 %all-reduce.5.cloned.1.call-done = (bf16[8,4,2,20,1024]{4,1,3,2,0:T(4,128)(2,1)}, bf16[8,4,2,20,1024]{4,1,3,2,0:T(4,128)(2,1)}) async-done(((bf16[8,4,2,20,1024]{4,1,3,2,0:T(4,128)(2,1)}, bf16[8,4,2,20,1024]{4,1,3,2,0:T(4,128)(2,1)}), (bf16[8,4,2,20,1024]{4,1,3,2,0:T(4,128)(2,1)}, bf16[8,4,2,20,1024]{4,1,3,2,0:T(4,128)(2,1)})) %all-reduce.5.cloned.1.call-update) | async-done | bytes 5242896
  203.4 1.7 constant_dynamic-slice_fusion
  205.2 1.1 copy.47
  206.2 4.6 %all-to-all-start.3 = ((bf16[1,4,2,20,1024]{4,2,3,0,1:T(2,128)(2,1)}), bf16[1,4,2,20,1024]{4,2,3,0,1:T(2,128)(2,1)S(1)}, u32[]{:S(2)}, u32[]{:S(2)}) async-start(bf16[1,4,2,20,1024]{4,2,3,0,1:T(2,128)(2,1)} %copy.47), calls=%async_computation.3 | async-start | bytes 655360 | tf_op jit(solution)/shard_map/all_to_all | solution.py:19
  210.8 5.9 %bitcast_convert_fusion.1 = bf16[2,1024,512]{2,1,0:T(8,128)(2,1)} fusion(bf16[8,4,2,20,1024]{4,3,1,0,2:T(8,128)(2,1)} %bitcast.89, bf16[8,4,2,20,512]{4,3,1,0,2:T(8,128)(2,1)} %copy-done.10), kind=kOutput, calls=%fused_computation.4 | convolution fusion | flops 1343225856 | bytes 6029312 | tf_op jit(solution)/shard_map/pcjkd,pcjkf->jdf/dot_general | solution.py:78
  216.8 1.7 constant_dynamic-slice_fusion.1
  218.5 1.1 copy.41
  219.6 1.5 all-to-all-done.3
  221.1 3.6 %all-to-all-start.1 = ((bf16[1,4,2,20,1024]{4,2,3,0,1:T(2,128)(2,1)}), bf16[1,4,2,20,1024]{4,2,3,0,1:T(2,128)(2,1)S(1)}, u32[]{:S(2)}, u32[]{:S(2)}) async-start(bf16[1,4,2,20,1024]{4,2,3,0,1:T(2,128)(2,1)} %copy.41), calls=%async_computation.1 | async-start | bytes 655360 | tf_op jit(solution)/shard_map/all_to_all | solution.py:19
  224.7 5.4 %bitcast_convert_fusion.2 = bf16[2,1024,512]{2,1,0:T(8,128)(2,1)} fusion(bf16[8,4,2,20,1024]{4,3,1,0,2:T(8,128)(2,1)} %bitcast.90, bf16[8,4,2,20,512]{4,3,1,0,2:T(8,128)(2,1)S(1)} %copy-done.3), kind=kOutput, calls=%fused_computation.5 | convolution fusion | flops 1343225856 | bytes 6029312 | tf_op jit(solution)/shard_map/pcjkd,pcjkf->jdf/dot_general | solution.py:75
  230.0 0.1 copy.48
  230.1 0.1 reshape.67
  230.2 4.1 %all-to-all-done.1 = bf16[1,4,2,20,1024]{4,2,3,0,1:T(2,128)(2,1)S(1)} async-done(((bf16[1,4,2,20,1024]{4,2,3,0,1:T(2,128)(2,1)}), bf16[1,4,2,20,1024]{4,2,3,0,1:T(2,128)(2,1)S(1)}, u32[]{:S(2)}, u32[]{:S(2)}) %all-to-all-start.1) | async-done | bytes 327712 | tf_op jit(solution)/shard_map/all_to_all | solution.py:19
  234.3 0.1 copy.42
  234.4 0.1 reshape.63
  234.5 0.9 gather_fusion.1
  235.3 0.9 gather_fusion
  236.2 0.1 broadcast_select_fusion
  236.3 0.8 reshape.68
  237.1 0.3 reshape.71
  237.4 2.2 multiply_reduce_fusion
  239.6 2.2 reduce
  (36 shorter events, 0.1 us)
Async XLA Ops:
  7.2 84.2 %copy-start = (bf16[2,512,1024]{2,1,0:T(8,128)(2,1)S(1)}, bf16[2,512,1024]{2,1,0:T(8,128)(2,1)}, u32[]{:S(2)}) copy-start(bf16[2,512,1024]{2,1,0:T(8,128)(2,1)} %param.14) | copy-start | bytes 6291460
  7.2 20.0 %copy-start.13 = (f32[64,2]{0,1:T(2,128)S(1)}, f32[64,2]{0,1:T(2,128)}, u32[]{:S(2)}) copy-start(f32[64,2]{0,1:T(2,128)} %param.11) | copy-start | bytes 1540
  7.2 20.8 %copy-start.12 = (bf16[64,1024]{1,0:T(8,128)(2,1)S(1)}, bf16[64,1024]{1,0:T(8,128)(2,1)}, u32[]{:S(2)}) copy-start(bf16[64,1024]{1,0:T(8,128)(2,1)} %param.15) | copy-start | bytes 393220
  7.2 49.3 %all-gather.5.cloned.1.call-start = ((), (), s32[]{:S(2)}) async-start(), calls=%async_computation.4 | async-start | bytes 2949120 | tf_op jit(solution)/shard_map/all_gather | solution.py:9
  27.1 61.4 %all-gather.7.cloned.1.call-start = ((), (), s32[]{:S(2)}) async-start(), calls=%async_computation.5 | async-start | bytes 2949120 | tf_op jit(solution)/shard_map/all_gather | solution.py:9
  27.3 0.6 copy-start.11
  41.5 162.0 %all-reduce.5.cloned.1.call-start = ((), (), s32[]{:S(2)}) async-start(), calls=%async_computation.6 | async-start | bytes 10485760
  56.5 2.8 %copy-start.6 = (bf16[2,1024,512]{2,1,0:T(8,128)(2,1)S(1)}, bf16[2,1024,512]{2,1,0:T(8,128)(2,1)}, u32[]{:S(2)}) copy-start(bf16[2,1024,512]{2,1,0:T(8,128)(2,1)} %param.13) | copy-start | bytes 6291460
  59.3 3.5 %copy-start.4 = (bf16[32,2,20,1024]{3,2,0,1:T(8,128)(2,1)}, bf16[32,2,20,1024]{3,2,0,1:T(8,128)(2,1)S(1)}, u32[]{:S(2)}) copy-start(bf16[32,2,20,1024]{3,2,0,1:T(8,128)(2,1)S(1)} %copy.39) | copy-start | bytes 7864324
  59.3 3.5 %copy-start.8 = (bf16[2,1024,512]{2,1,0:T(8,128)(2,1)S(1)}, bf16[2,1024,512]{2,1,0:T(8,128)(2,1)}, u32[]{:S(2)}) copy-start(bf16[2,1024,512]{2,1,0:T(8,128)(2,1)} %param.12) | copy-start | bytes 6291460
  88.5 2.8 %copy-start.15 = (f32[2,8,4,20,512]{4,3,2,1,0:T(8,128)S(1)}, f32[2,8,4,20,512]{4,3,2,1,0:T(8,128)}, u32[]{:S(2)}) copy-start(f32[2,8,4,20,512]{4,3,2,1,0:T(8,128)} %fusion.17) | copy-start | bytes 7864324
  91.3 6.1 %copy-start.5 = (bf16[32,2,20,1024]{3,2,0,1:T(8,128)(2,1)}, bf16[32,2,20,1024]{3,2,0,1:T(8,128)(2,1)S(1)}, u32[]{:S(2)}) copy-start(bf16[32,2,20,1024]{3,2,0,1:T(8,128)(2,1)S(1)} %copy.45) | copy-start | bytes 7864324
  97.4 1.9 copy-start.16
  97.4 5.6 %copy-start.2 = (bf16[8,4,2,20,512]{4,3,1,0,2:T(8,128)(2,1)}, bf16[8,4,2,20,512]{4,3,1,0,2:T(8,128)(2,1)S(1)}, u32[]{:S(2)}) copy-start(bf16[8,4,2,20,512]{4,3,1,0,2:T(8,128)(2,1)S(1)} %get-tuple-element.11) | copy-start | bytes 3932164
  97.4 7.5 %copy-start.10 = (bf16[8,4,2,20,512]{4,3,1,0,2:T(8,128)(2,1)}, bf16[8,4,2,20,512]{4,3,1,0,2:T(8,128)(2,1)S(1)}, u32[]{:S(2)}) copy-start(bf16[8,4,2,20,512]{4,3,1,0,2:T(8,128)(2,1)S(1)} %get-tuple-element.10) | copy-start | bytes 3932164
  99.3 3.8 %copy-start.9 = (bf16[2,1024,512]{2,1,0:T(8,128)(2,1)S(1)}, bf16[2,1024,512]{2,1,0:T(8,128)(2,1)}, u32[]{:S(2)}) copy-start(bf16[2,1024,512]{2,1,0:T(8,128)(2,1)} %param.12) | copy-start | bytes 6291460
  103.0 1.9 copy-start.7
  110.5 0.7 copy-start.14
  110.5 1.4 copy-start.17
  206.2 14.8 %all-to-all-start.3 = ((bf16[1,4,2,20,1024]{4,2,3,0,1:T(2,128)(2,1)}), bf16[1,4,2,20,1024]{4,2,3,0,1:T(2,128)(2,1)S(1)}, u32[]{:S(2)}, u32[]{:S(2)}) async-start(bf16[1,4,2,20,1024]{4,2,3,0,1:T(2,128)(2,1)} %copy.47), calls=%async_computation.3 | async-start | bytes 655360 | tf_op jit(solution)/shard_map/all_to_all | solution.py:19
  210.8 13.8 %copy-start.3 = (bf16[8,4,2,20,512]{4,3,1,0,2:T(8,128)(2,1)S(1)}, bf16[8,4,2,20,512]{4,3,1,0,2:T(8,128)(2,1)}, u32[]{:S(2)}) copy-start(bf16[8,4,2,20,512]{4,3,1,0,2:T(8,128)(2,1)} %copy-done.2) | copy-start | bytes 3932164
  221.1 13.2 %all-to-all-start.1 = ((bf16[1,4,2,20,1024]{4,2,3,0,1:T(2,128)(2,1)}), bf16[1,4,2,20,1024]{4,2,3,0,1:T(2,128)(2,1)S(1)}, u32[]{:S(2)}, u32[]{:S(2)}) async-start(bf16[1,4,2,20,1024]{4,2,3,0,1:T(2,128)(2,1)} %copy.41), calls=%async_computation.1 | async-start | bytes 655360 | tf_op jit(solution)/shard_map/all_to_all | solution.py:19
  234.5 7.4 %copy-start.1 = (bf16[2,512,1024]{2,1,0:T(8,128)(2,1)S(1)}, bf16[2,512,1024]{2,1,0:T(8,128)(2,1)}, u32[]{:S(2)}) copy-start(bf16[2,512,1024]{2,1,0:T(8,128)(2,1)} %param.14) | copy-start | bytes 6291460
Sparse Core Ops, SparseCore 0:
  27.2 29.2 all-gather.4
  58.4 30.1 all-gather.6
  110.6 92.7 all-reduce.4
where the time goes:
time: 249 us; the launch traced here: 248 us
  waiting for transfers between devices  129 us (52%)
  matrix products  35.6 us (14%)
  blocking collectives  28.6 us (11%)
  local copies, waits for them, and re-layouts  27.4 us (11%)
  between operations  14.1 us (6%)
  starting transfers between devices  8.31 us (3%)
  other arithmetic  4.97 us (2%)
    unnamed x4, waiting for transfers between devices  86.4 us
    all_gather x2, waiting for transfers between devices, spread_one(): return lax.all_gather(arrived[None], 'dp', axis=0, tiled=True)  37.2 us
    all_to_all x2, blocking collectives, spread_one(): lax.all_to_all(buffer, 'expert', split_axis=0, concat_axis=0, tiled=True)  28.6 us
    all_to_all x2, starting transfers between devices, collect(): lax.all_to_all(summed, 'expert', split_axis=1, concat_axis=1, tiled=True)  8.19 us
    convert_element_type x2, local copies, waits for them, and re-layouts, collect(): term_fn(jnp.int32(0), 1 * lax.axis_size('dp')).astype(jnp.bfloat16)  7.38 us
    unnamed x41, local copies, waits for them, and re-layouts  6.55 us
    dot_general x1, matrix products, body(): jnp.einsum('pcjkd,jfd->pcjkf', grad_rows, w_down, preferred_element_type=...  6.04 us
    dot_general x1, matrix products, body(): jnp.einsum('pcjkd,pcjkf->jdf', gathered, grad_hu, preferred_element_type=...  5.93 us
  transfers between devices with their start and end apart: 5, of which 5 were waited for; matrix products, arithmetic and copies ran while one was open for 13% of the time, Pallas kernels for 0%

commit v1 on v0

v1 whole, which is shorter than its diff:
```python
import functools

import jax
import jax.numpy as jnp
from jax import lax
from jax.experimental import pallas as pl
from jax.experimental.pallas import tpu as pltpu
from jax.sharding import PartitionSpec as P

BF = jnp.bfloat16
F32 = jnp.float32
NN = (((1,), (0,)), ((), ()))
NT = (((1,), (1,)), ((), ()))
TN = (((0,), (0,)), ((), ()))
VMEM_LIMIT = 56 * 1024 * 1024


def dot(a, b, dims=NN):
    return lax.dot_general(a, b, dims, preferred_element_type=F32)


def params():
    return pltpu.CompilerParams(vmem_limit_bytes=VMEM_LIMIT)


def whole(shape):
    return pl.BlockSpec(shape, lambda *_: (0,) * len(shape))


def places(ids, experts):
    toks, top = ids.shape
    lanes = lax.broadcasted_iota(jnp.int32, (toks, experts), 1)
    hot = [(ids[:, k : k + 1] == lanes).astype(F32) for k in range(top)]
    earlier = (
        lax.broadcasted_iota(jnp.int32, (toks, toks), 1)
        < lax.broadcasted_iota(jnp.int32, (toks, toks), 0)
    ).astype(BF)
    counts = dot(earlier, sum(hot).astype(BF))
    return [jnp.sum(counts * h, axis=1, keepdims=True).astype(jnp.int32) for h in hot]


def place_kernel(experts, local, cap, pos, ids_ref, gw_ref, tok_ref, cot_ref, *outs):
    ids = ids_ref[...]
    gw = gw_ref[...]
    toks, top = ids.shape
    owners = experts // local
    here = places(ids, experts)
    rel = jnp.bitwise_xor(ids // local, pos[1])
    lanes = lax.broadcasted_iota(jnp.int32, (toks, local * cap), 1)
    col = [(ids[:, k : k + 1] % local) * cap + here[k] for k in range(top)]
    cot = cot_ref[...].astype(F32)
    scaled = [(gw[:, k : k + 1] * cot).astype(BF) for k in range(top)]
    tok = tok_ref[...]
    for j in range(owners):
        sel = [
            jnp.where((rel[:, k : k + 1] == j) & (col[k] == lanes), 1.0, 0.0).astype(BF)
            for k in range(top)
        ]
        outs[j][...] = dot(sum(sel), tok, TN).astype(BF)
        outs[owners + j][...] = sum(dot(sel[k], scaled[k], TN) for k in range(top)).astype(BF)


def place(pos, ids, gw, tokens, cot, experts, local, cap):
    toks, width = tokens.shape
    owners = experts // local
    shape = (local * cap, width)
    return pl.pallas_call(
        functools.partial(place_kernel, experts, local, cap),
        grid_spec=pltpu.PrefetchScalarGridSpec(
            num_scalar_prefetch=1,
            grid=(1,),
            in_specs=[whole(a.shape) for a in (ids, gw, tokens, cot)],
            out_specs=[whole(shape)] * (2 * owners),
        ),
        out_shape=[jax.ShapeDtypeStruct(shape, BF)] * (2 * owners),
        compiler_params=params(),
        name="place",
    )(pos, ids, gw, tokens, cot)


def pack_kernel(owners, cap, pos, *refs):
    mine, theirs, out = refs[:owners], refs[owners : 2 * owners], refs[-1]
    size = mine[0].shape[0]
    row = lax.broadcasted_iota(jnp.int32, (size, size), 0)
    column = lax.broadcasted_iota(jnp.int32, (size, size), 1)
    first = pos[0] * cap
    keep = jnp.where((row < cap) & (column == first + row), 1.0, 0.0).astype(BF)
    take = jnp.where((row >= cap) & (column == first + row - cap), 1.0, 0.0).astype(BF)
    parts = [dot(keep, mine[j][...]) + dot(take, theirs[j][...]) for j in range(owners)]
    out[...] = jnp.concatenate(parts, axis=0).astype(BF)


def pack(pos, mine, theirs, cap):
    size, width = mine[0].shape
    owners = len(mine)
    shape = (owners * size, width)
    return pl.pallas_call(
        functools.partial(pack_kernel, owners, cap),
        grid_spec=pltpu.PrefetchScalarGridSpec(
            num_scalar_prefetch=1,
            grid=(1,),
            in_specs=[whole((size, width))] * (2 * owners),
            out_specs=whole(shape),
        ),
        out_shape=jax.ShapeDtypeStruct(shape, BF),
        compiler_params=params(),
        name="pack",
    )(pos, *mine, *theirs)


def forward_kernel(chips, steps, pos, *refs):
    xs = refs[:chips]
    weights = refs[chips : chips + 6]
    ps = refs[chips + 6 : 2 * chips + 6]
    f1, f2, at, x, acc = refs[2 * chips + 6 :]
    step = pl.program_id(0)
    size = xs[0].shape[0]

    @pl.when(step == 0)
    def _():
        for i in range(chips):
            x[i * size : (i + 1) * size, :] = xs[i][...]

    rows = x[...]
    total = None
    for half in range(2):
        wg, wu, wd = weights[3 * half : 3 * half + 3]
        if half == 0:
            wg, wu, wd = wg.at[0], wu.at[0], wd.at[0]
        gate = dot(rows, wg[...])
        up = dot(rows, wu[...])
        sig = 1.0 / (1.0 + jnp.exp(-gate))
        act = gate * sig
        hidden = (act * up).astype(BF)
        f1[half] = (up * sig * (1.0 + gate * (1.0 - sig))).astype(BF)
        f2[half] = act.astype(BF)
        at[half] = hidden.T
        term = dot(hidden, wd[...])
        total = term if total is None else total + term

    @pl.when(step == 0)
    def _():
        acc[...] = total

    @pl.when(step > 0)
    def _():
        acc[...] += total

    @pl.when(step == steps - 1)
    def _():
        for i in range(chips):
            ps[i][...] = acc[i * size : (i + 1) * size, :].astype(BF)


def weight_specs(width, tile):
    return [
        pl.BlockSpec((1, width, tile), lambda f, pos: (pos[0], 0, f)),
        pl.BlockSpec((1, width, tile), lambda f, pos: (pos[0], 0, f)),
        pl.BlockSpec((1, tile, width), lambda f, pos: (pos[0], f, 0)),
        pl.BlockSpec((width, tile), lambda f, pos: (0, f)),
        pl.BlockSpec((width, tile), lambda f, pos: (0, f)),
        pl.BlockSpec((tile, width), lambda f, pos: (f, 0)),
    ]


def tile_of(hidden):
    return 256 if hidden % 256 == 0 else hidden


def forward(pos, xs, own, other):
    chips = len(xs)
    size, width = xs[0].shape
    hidden = other[0].shape[1]
    tile = tile_of(hidden)
    steps = hidden // tile
    rows = chips * size
    factor = pl.BlockSpec((2, rows, tile), lambda f, pos: (0, 0, f))
    out = pl.pallas_call(
        functools.partial(forward_kernel, chips, steps),
        grid_spec=pltpu.PrefetchScalarGridSpec(
            num_scalar_prefetch=1,
            grid=(steps,),
            in_specs=[whole((size, width))] * chips + weight_specs(width, tile),
            out_specs=[whole((size, width))] * chips
            + [factor, factor, pl.BlockSpec((2, tile, rows), lambda f, pos: (0, f, 0))],
            scratch_shapes=[pltpu.VMEM((rows, width), BF), pltpu.VMEM((rows, width), F32)],
        ),
        out_shape=[jax.ShapeDtypeStruct((size, width), BF)] * chips
        + [
            jax.ShapeDtypeStruct((2, rows, hidden), BF),
            jax.ShapeDtypeStruct((2, rows, hidden), BF),
            jax.ShapeDtypeStruct((2, hidden, rows), BF),
        ],
        cost_estimate=pl.CostEstimate(
            flops=12 * rows * width * hidden, bytes_accessed=12 * width * hidden, transcendentals=0
        ),
        compiler_params=params(),
        name="forward",
    )(pos, *xs, *own, *other)
    return out[:chips], out[chips], out[chips + 1], out[chips + 2]


def backward_kernel(chips, steps, pos, *refs):
    dys = refs[:chips]
    weights = refs[chips : chips + 6]
    f1, f2 = refs[chips + 6 : chips + 8]
    qs = refs[chips + 8 : 2 * chips + 8]
    dg, du, dy, acc = refs[2 * chips + 8 :]
    step = pl.program_id(0)
    size = dys[0].shape[0]

    @pl.when(step == 0)
    def _():
        for i in range(chips):
            dy[i * size : (i + 1) * size, :] = dys[i][...]

    rows = dy[...]
    total = None
    for half in range(2):
        wg, wu, wd = weights[3 * half : 3 * half + 3]
        if half == 0:
            wg, wu, wd = wg.at[0], wu.at[0], wd.at[0]
        da = dot(rows, wd[...], NT)
        grad_g = (da * f1[half].astype(F32)).astype(BF)
        grad_u = (da * f2[half].astype(F32)).astype(BF)
        dg[half] = grad_g
        du[half] = grad_u
        term = dot(grad_g, wg[...], NT) + dot(grad_u, wu[...], NT)
        total = term if total is None else total + term

    @pl.when(step == 0)
    def _():
        acc[...] = total

    @pl.when(step > 0)
    def _():
        acc[...] += total

    @pl.when(step == steps - 1)
    def _():
        for i in range(chips):
            qs[i][...] = acc[i * size : (i + 1) * size, :].astype(BF)


def backward(pos, dys, own, other, f1, f2):
    chips = len(dys)
    size, width = dys[0].shape
    hidden = other[0].shape[1]
    tile = tile_of(hidden)
    steps = hidden // tile
    rows = chips * size
    factor = pl.BlockSpec((2, rows, tile), lambda f, pos: (0, 0, f))
    out = pl.pallas_call(
        functools.partial(backward_kernel, chips, steps),
        grid_spec=pltpu.PrefetchScalarGridSpec(
            num_scalar_prefetch=1,
            grid=(steps,),
            in_specs=[whole((size, width))] * chips + weight_specs(width, tile) + [factor, factor],
            out_specs=[whole((size, width))] * chips + [factor, factor],
            scratch_shapes=[pltpu.VMEM((rows, width), BF), pltpu.VMEM((rows, width), F32)],
        ),
        out_shape=[jax.ShapeDtypeStruct((size, width), BF)] * chips
        + [jax.ShapeDtypeStruct((2, rows, hidden), BF)] * 2,
        cost_estimate=pl.CostEstimate(
            flops=12 * rows * width * hidden, bytes_accessed=12 * width * hidden, transcendentals=0
        ),
        compiler_params=params(),
        name="backward",
    )(pos, *dys, *own, *other, f1, f2)
    return out[:chips], out[chips], out[chips + 1]


def grads_kernel(chips, pos, *refs):
    xs = refs[:chips]
    dys = refs[chips : 2 * chips]
    dg, du, at = refs[2 * chips : 2 * chips + 3]
    own = refs[2 * chips + 3 : 2 * chips + 6]
    other = refs[2 * chips + 6 : 2 * chips + 9]
    xt, dy = refs[2 * chips + 9 :]
    size = xs[0].shape[0]

    @pl.when(pl.program_id(0) == 0)
    def _():
        for i in range(chips):
            dy[i * size : (i + 1) * size, :] = dys[i][...]
        xt[...] = jnp.concatenate([xs[i][...] for i in range(chips)], axis=0).T

    for half in range(2):
        gg = dot(xt[...], dg[half]).astype(BF)
        gu = dot(xt[...], du[half]).astype(BF)
        gd = dot(at[half], dy[...]).astype(BF)
        if half == 0:
            own[0][0], own[1][0], own[2][0] = gg, gu, gd
        else:
            other[0][...], other[1][...], other[2][...] = gg, gu, gd


def grads(pos, xs, dys, dg, du, at, local):
    chips = len(xs)
    size, width = xs[0].shape
    rows = chips * size
    hidden = dg.shape[2]
    tile = tile_of(hidden)
    steps = hidden // tile
    factor = pl.BlockSpec((2, rows, tile), lambda f, pos: (0, 0, f))
    wide = jax.ShapeDtypeStruct((local, width, hidden), BF)
    tall = jax.ShapeDtypeStruct((local, hidden, width), BF)
    out = pl.pallas_call(
        functools.partial(grads_kernel, chips),
        grid_spec=pltpu.PrefetchScalarGridSpec(
            num_scalar_prefetch=1,
            grid=(steps,),
            in_specs=[whole((size, width))] * (2 * chips)
            + [factor, factor, pl.BlockSpec((2, tile, rows), lambda f, pos: (0, f, 0))],
            out_specs=weight_specs(width, tile),
            scratch_shapes=[pltpu.VMEM((width, rows), BF), pltpu.VMEM((rows, width), BF)],
        ),
        out_shape=[
            wide,
            wide,
            tall,
            jax.ShapeDtypeStruct(wide.shape[1:], BF),
            jax.ShapeDtypeStruct(wide.shape[1:], BF),
            jax.ShapeDtypeStruct(tall.shape[1:], BF),
        ],
        cost_estimate=pl.CostEstimate(
            flops=12 * rows * width * hidden, bytes_accessed=12 * width * hidden, transcendentals=0
        ),
        compiler_params=params(),
        name="grads",
    )(pos, *xs, *dys, dg, du, at)
    return out[:3], out[3:]


def add_kernel(parts, *refs):
    total = refs[0][...].astype(F32)
    for ref in refs[1:parts]:
        total = total + ref[...].astype(F32)
    outs = refs[parts:]
    size = total.shape[0] // len(outs)
    for j, out in enumerate(outs):
        out[...] = total[j * size : (j + 1) * size].astype(BF)


def add(arrays, pieces=1):
    rows, width = arrays[0].shape
    shape = (rows // pieces, width)
    return pl.pallas_call(
        functools.partial(add_kernel, len(arrays)),
        grid=(1,),
        in_specs=[whole((rows, width))] * len(arrays),
        out_specs=[whole(shape)] * pieces,
        out_shape=[jax.ShapeDtypeStruct(shape, BF)] * pieces,
        compiler_params=params(),
        name="add",
    )(*arrays)


def combine_kernel(experts, local, cap, weighted, pos, ids_ref, gw_ref, *refs):
    owners = experts // local
    mine, theirs, out = refs[:owners], refs[owners : 2 * owners], refs[-1]
    ids = ids_ref[...]
    gw = gw_ref[...]
    toks, top = ids.shape
    here = places(ids, experts)
    size = mine[0].shape[0]
    lanes = lax.broadcasted_iota(jnp.int32, (toks, size), 1)
    total = jnp.zeros(out.shape, F32)
    for j in range(owners):
        for source, which in ((mine, 0), (theirs, 1)):
            expert = jnp.bitwise_xor(pos[1], j) * local + jnp.bitwise_xor(pos[0], which)
            mask = [
                (ids[:, k : k + 1] == expert) & (here[k] + which * cap == lanes) for k in range(top)
            ]
            values = source[j][...]
            if weighted:
                w = sum(jnp.where(mask[k], gw[:, k : k + 1], 0.0) for k in range(top))
                high = w.astype(BF)
                low = (w - high.astype(F32)).astype(BF)
                total = total + dot(high, values) + dot(low, values)
            else:
                w = sum(jnp.where(mask[k], 1.0, 0.0) for k in range(top))
                total = total + dot(w.astype(BF), values)
    out[...] = total.astype(BF)


def combine(pos, ids, gw, mine, theirs, experts, local, cap, weighted):
    size, width = mine[0].shape
    out = jax.ShapeDtypeStruct((ids.shape[0], width), BF)
    return pl.pallas_call(
        functools.partial(combine_kernel, experts, local, cap, weighted),
        grid_spec=pltpu.PrefetchScalarGridSpec(
            num_scalar_prefetch=1,
            grid=(1,),
            in_specs=[whole(ids.shape), whole(gw.shape)] + [whole((size, width))] * (2 * len(mine)),
            out_specs=whole(out.shape),
        ),
        out_shape=out,
        compiler_params=params(),
        name="combine",
    )(pos, ids, gw, *mine, *theirs)


def body(tokens, expert_ids, gate_weights, w_gate, w_up, w_down, cotangent):
    owners = lax.axis_size("expert")
    devices = lax.axis_size("dp")
    toks, width = tokens.shape
    top = expert_ids.shape[1]
    local = w_gate.shape[0]
    experts = local * owners
    cap = max(2, 5 * toks * top // (4 * experts))
    bits = (devices // 2).bit_length() - 1
    assert local == 2 and devices == 2 << bits and owners & (owners - 1) == 0

    core = lax.axis_index("dp") % 2
    pos = jnp.stack([core, lax.axis_index("expert")]).astype(jnp.int32)

    def to_pair(a):
        return lax.ppermute(a, "dp", [(i, i ^ 1) for i in range(devices)])

    def to_owner(a, j):
        return lax.ppermute(a, "expert", [(i, i ^ j) for i in range(owners)])

    def to_chip(a, s):
        def bit(i):
            return 2 << ((s + (i % 2) * (bits // 2)) % bits)

        return lax.ppermute(a, "dp", [(i, i ^ bit(i)) for i in range(devices)])

    def swap(messages):
        return [messages[0]] + [to_owner(messages[j], j) for j in range(1, owners)]

    def spread(messages):
        mine = swap(messages)
        theirs = [to_pair(m) for m in mine]
        parts = [pack(pos, mine, theirs, cap)]
        for s in range(bits):
            parts = parts + [to_chip(a, s) for a in parts]
        return parts

    def collect(parts):
        for s in reversed(range(1, bits)):
            half = len(parts) // 2
            arrived = [to_chip(a, s) for a in parts[half:]]
            sums = [parts[0]] + [add([parts[i], arrived[i]])[0] for i in range(1, half)]
            held = [arrived[0]] if s == bits - 1 else held + [arrived[0]]
            parts = sums
        held = [parts[0]] + (held if bits > 1 else []) + [to_chip(parts[1], 0)]
        mine = swap(add(held, owners))
        return mine, [to_pair(m) for m in mine]

    placed = place(pos, expert_ids, gate_weights, tokens, cotangent, experts, local, cap)
    own = (w_gate, w_up, w_down)
    other = [
        to_pair(lax.dynamic_index_in_dim(w, 1 - core, 0, keepdims=False)) for w in own
    ]
    xs = spread(placed[:owners])
    dys = spread(placed[owners:])
    ps, f1, f2, at = forward(pos, xs, own, other)
    qs, dg, du = backward(pos, dys, own, other, f1, f2)
    kept, given = grads(pos, xs, dys, dg, du, at, local)
    mine, theirs = collect(ps)
    mixed = combine(
        pos, expert_ids, gate_weights, mine, theirs, experts, local, cap, True
    )
    mine, theirs = collect(qs)
    grad_tokens = combine(
        pos, expert_ids, gate_weights, mine, theirs, experts, local, cap, False
    )
    got = [to_pair(g) for g in given]
    grad_gate, grad_up, grad_down = [
        lax.dynamic_update_index_in_dim(k, g, 1 - core, 0) for k, g in zip(kept, got)
    ]
    return (mixed, grad_tokens, grad_gate, grad_up, grad_down)


def solution(mesh):
    rows = P(("dp", "expert"), None)
    wide, tall = P("expert", None, "dp"), P("expert", "dp", None)
    return jax.shard_map(
        body,
        mesh=mesh,
        in_specs=(rows, rows, rows, wide, wide, tall, rows),
        out_specs=(rows, rows, wide, wide, tall),
        check_vma=False,
    )
```

time: 249 us -> 153 us (0.61)
  waiting for transfers between devices: 129 us -> 32.1 us
  Pallas kernels: 0 us -> 57.6 us
  starting transfers between devices: 8.31 us -> 45 us
  matrix products: 35.6 us -> 0 us
  blocking collectives: 28.6 us -> 0 us
  between operations: 14.1 us -> 1.13 us
  local copies, waits for them, and re-layouts: 27.4 us -> 16 us
  other arithmetic: 4.97 us -> 0.65 us
    unnamed x4 -> x0, waiting for transfers between devices: 86.4 us -> none
    pallas_call x0 -> x12, Pallas kernels: none -> 57.6 us  [the longest x1 13.1 us: backward(): pl.pallas_call(functools.partial(backward_kernel, chips, steps), grid_spe...]
    ppermute x0 -> x46, starting transfers between devices: none -> 45 us  [the longest x12 27.4 us: to_owner(): return lax.ppermute(a, 'expert', [(i, i ^ j) for i in range(owners)])]
    all_gather x2 -> x0, waiting for transfers between devices: 37.2 us -> none  [spread_one(): return lax.all_gather(arrived[None], 'dp', axis=0, tiled=True)]
    dot_general x11 -> x0, matrix products: 35.6 us -> none  [the longest x1 6.04 us: body(): jnp.einsum('pcjkd,jfd->pcjkf', grad_rows, w_down, preferred_element_type=...]
    ppermute x0 -> x46, waiting for transfers between devices: none -> 32.1 us  [the longest x12 17.3 us: to_chip(): return lax.ppermute(a, 'dp', [(i, i ^ bit(i)) for i in range(devices)])]
    all_to_all x2 -> x0, blocking collectives: 28.6 us -> none  [spread_one(): lax.all_to_all(buffer, 'expert', split_axis=0, concat_axis=0, tiled=True)]
    all_to_all x2 -> x0, starting transfers between devices: 8.19 us -> none  [collect(): lax.all_to_all(summed, 'expert', split_axis=1, concat_axis=1, tiled=True)]
  transfers between devices with their start and end apart: 5 -> 46, of which waited for: 5 -> 19; matrix products, arithmetic and copies ran while one was open for 13% -> 2% of each run, Pallas kernels for 0% -> 36%
where the time goes in v1:
time: 153 us
  Pallas kernels  57.6 us (38%)
  starting transfers between devices  45 us (29%)
  waiting for transfers between devices  32.1 us (21%)
  local copies, waits for them, and re-layouts  16 us (10%)
    ppermute x12, starting transfers between devices, to_owner(): return lax.ppermute(a, 'expert', [(i, i ^ j) for i in range(owners)])  27.4 us
    ppermute x12, waiting for transfers between devices, to_chip(): return lax.ppermute(a, 'dp', [(i, i ^ bit(i)) for i in range(devices)])  17.3 us
    ppermute x12, starting transfers between devices, to_chip(): return lax.ppermute(a, 'dp', [(i, i ^ bit(i)) for i in range(devices)])  13.3 us
    unnamed x108, local copies, waits for them, and re-layouts  13.1 us
    pallas_call x1, Pallas kernels, backward(): pl.pallas_call(functools.partial(backward_kernel, chips, steps), grid_spe...  13.1 us
    ppermute x12, waiting for transfers between devices, to_owner(): return lax.ppermute(a, 'expert', [(i, i ^ j) for i in range(owners)])  11 us
    pallas_call x1, Pallas kernels, forward(): pl.pallas_call(functools.partial(forward_kernel, chips, steps), grid_spec...  10.7 us
    pallas_call x1, Pallas kernels, grads(): pl.pallas_call(functools.partial(grads_kernel, chips), grid_spec=pltpu.Pr...  10.3 us
  transfers between devices with their start and end apart: 46, of which 19 were waited for; matrix products, arithmetic and copies ran while one was open for 2% of the time, Pallas kernels for 36%

profile of v1, /device:TPU:0, one launch (start us, length us, event | category | flops | bytes accessed | tf_op | source)
XLA Modules:
  0.0 152.6 jit_solution(928565197655358889)
XLA Ops:
  0.7 1.5 %copy.14.ids_ref = s32[64,2]{1,0:T(8,128)} copy(s32[64,2]{0,1:T(2,128)} %param.8) | data formatting | bytes 1024 | tf_op args[1]
  2.2 1.4 copy.15.gw_ref
  3.6 0.7 pad_add_fusion.pos
  4.2 3.3 %place.1 = (bf16[40,1024]{1,0:T(8,128)(2,1)}, bf16[40,1024]{1,0:T(8,128)(2,1)}, bf16[40,1024]{1,0:T(8,128)(2,1)}, bf16[40,1024]{1,0:T(8,128)(2,1)}, bf16[40,1024...) custom-call(s32[2]{0:T(128)} %pad_add_fusion.pos, ...), custom_call_target="tpu_custom_call" | custom-call | tf_op jit(solution)/shard_map/place/pallas_call | solution.py:67
  7.6 3.0 %collective-permute-start = (bf16[40,1024]{1,0:T(8,128)(2,1)}, bf16[40,1024]{1,0:T(8,128)(2,1)S(1)}, u32[]{:S(2)}, u32[]{:S(2)}) collective-permute-start(bf16[40,1024]{1,0:T(8,128)(2,1)} %get-tuple-element.41), channel_id=1, source_target_pairs={{0,1},{1,0},{2,3},{3,2},{4,5},{5,4},{6,7},{7,6},{8,9},{9,8},{10,11... | collective-permute-start | bytes 245768 | tf_op jit(solution)/shard_map/ppermute | solution.py:422
  10.6 2.6 %collective-permute-start.1 = (bf16[40,1024]{1,0:T(8,128)(2,1)}, bf16[40,1024]{1,0:T(8,128)(2,1)S(1)}, u32[]{:S(2)}, u32[]{:S(2)}) collective-permute-start(bf16[40,1024]{1,0:T(8,128)(2,1)} %get-tuple-element.42), channel_id=1, source_target_pairs={{0,2},{1,3},{2,0},{3,1},{4,6},{5,7},{6,4},{7,5},{8,10},{9,11},{10,... | collective-permute-start | bytes 245768 | tf_op jit(solution)/shard_map/ppermute | solution.py:422
  13.2 0.9 collective-permute-start.23
  14.1 3.5 %collective-permute-start.24 = (bf16[40,1024]{1,0:T(8,128)(2,1)}, bf16[40,1024]{1,0:T(8,128)(2,1)S(1)}, u32[]{:S(2)}, u32[]{:S(2)}) collective-permute-start(bf16[40,1024]{1,0:T(8,128)(2,1)} %get-tuple-element.54), channel_id=1, source_target_pairs={{0,2},{1,3},{2,0},{3,1},{4,6},{5,7},{6,4},{7,5},{8,10},{9,11},{10,... | collective-permute-start | bytes 245768 | tf_op jit(solution)/shard_map/ppermute | solution.py:422
  17.6 1.4 dynamic-slice_bitcast_fusion.2
  19.6 1.4 collective-permute-done.1.refs_2_
  21.6 5.4 %collective-permute-done.24.refs_2_ = bf16[40,1024]{1,0:T(8,128)(2,1)S(1)} collective-permute-done((bf16[40,1024]{1,0:T(8,128)(2,1)}, bf16[40,1024]{1,0:T(8,128)(2,1)S(1)}, u32[]{:S(2)}, u32[]{:S(2)}) %collective-permute-start.24) | collective-permute-done | bytes 81952 | tf_op jit(solution)/shard_map/ppermute | solution.py:422
  27.1 0.5 collective-permute-start.26
  27.6 0.7 collective-permute-done.3.refs_4_
  28.9 0.7 collective-permute-done.4.refs_5_
  30.2 0.7 collective-permute-done.28.refs_6_
  31.7 2.9 %pack.3.refs_0_.refs_4_ = bf16[160,1024]{1,0:T(8,128)(2,1)} custom-call(s32[2]{0:T(128)} %pad_add_fusion.pos, bf16[40,1024]{1,0:T(8,128)(2,1)} %get-tuple-element.52.refs_0_, bf16[40,1024]{1,0:T(8,128)(2,1)} %copy-done.13, bf16[40,1024]{1,0:T(8,128)(2,1)} %copy-done.14, bf16[40,1024]{1,0:T(8,128)(2,1)} %copy-done.15, bf16[40,1024]{1,0:T(8,128)(2,1)} %copy-done.18, ...), custom_call_target="tpu_custom_call" | custom-call | tf_op jit(solution)/shard_map/pack/pallas_call | solution.py:97
  34.6 1.6 %collective-permute-start.30 = (bf16[160,1024]{1,0:T(8,128)(2,1)}, bf16[160,1024]{1,0:T(8,128)(2,1)S(1)}, u32[]{:S(2)}, u32[]{:S(2)}) collective-permute-start(bf16[160,1024]{1,0:T(8,128)(2,1)} %pack.3.refs_0_.refs_4_), channel_id=1, source_target_pairs={{0,8},{4,20},{8,0},{12,28},{16,24},{20,4},{24,16},{28,12},{1,9},{5... | collective-permute-start | bytes 983048 | tf_op jit(solution)/shard_map/ppermute | solution.py:428
  36.3 0.6 copy-done.22
  36.9 2.9 %pack.2.refs_0_ = bf16[160,1024]{1,0:T(8,128)(2,1)} custom-call(s32[2]{0:T(128)} %pad_add_fusion.pos, bf16[40,1024]{1,0:T(8,128)(2,1)} %get-tuple-element.40.refs_0_, bf16[40,1024]{1,0:T(8,128)(2,1)} %copy-done.9, bf16[40,1024]{1,0:T(8,128)(2,1)} %copy-done.10, bf16[40,1024]{1,0:T(8,128)(2,1)} %copy-done.11, bf16[40,1024]{1,0:T(8,128)(2,1)} %copy-done.16, ...), custom_call_target="tpu_custom_call" | custom-call | tf_op jit(solution)/shard_map/pack/pallas_call | solution.py:97
  39.8 0.5 collective-permute-start.7
  40.3 1.7 %collective-permute-done.30.refs_1_.refs_5_ = bf16[160,1024]{1,0:T(8,128)(2,1)S(1)} collective-permute-done((bf16[160,1024]{1,0:T(8,128)(2,1)}, bf16[160,1024]{1,0:T(8,128)(2,1)S(1)}, u32[]{:S(2)}, u32[]{:S(2)}) %collective-permute-start.30) | collective-permute-done | bytes 327712 | tf_op jit(solution)/shard_map/ppermute | solution.py:428
  42.0 1.5 collective-permute-start.8
  43.5 6.4 %collective-permute-done.7.refs_1_ = bf16[160,1024]{1,0:T(8,128)(2,1)S(1)} collective-permute-done((bf16[160,1024]{1,0:T(8,128)(2,1)}, bf16[160,1024]{1,0:T(8,128)(2,1)S(1)}, u32[]{:S(2)}, u32[]{:S(2)}) %collective-permute-start.7) | collective-permute-done | bytes 327712 | tf_op jit(solution)/shard_map/ppermute | solution.py:428
  49.9 1.5 collective-permute-start.9
  51.4 0.5 collective-permute-start.31
  52.0 5.0 %collective-permute-done.9.refs_3_ = bf16[160,1024]{1,0:T(8,128)(2,1)S(1)} collective-permute-done((bf16[160,1024]{1,0:T(8,128)(2,1)S(1)}, bf16[160,1024]{1,0:T(8,128)(2,1)S(1)}, u32[]{:S(2)}, u32[]{:S(2)}) %collective-permute-start.9) | collective-permute-done | bytes 327712 | tf_op jit(solution)/shard_map/ppermute | solution.py:428
  57.0 1.5 collective-permute-start.32
  58.6 0.9 copy-done.43
  59.8 1.0 copy-done.45
  60.8 10.7 %forward.1 = (bf16[160,1024]{1,0:T(8,128)(2,1)}, bf16[160,1024]{1,0:T(8,128)(2,1)}, bf16[160,1024]{1,0:T(8,128)(2,1)}, bf16[160,1024]{1,0:T(8,128)(2,1)}, bf16[2...) custom-call(s32[2]{0:T(128)} %pad_add_fusion.pos, ...), custom_call_target="tpu_custom_call" | custom-call | flops 4026531840 | bytes 6291456 | tf_op jit(solution)/shard_map/forward/pallas_call | solution.py:178
  71.5 0.6 collective-permute-start.13
  72.1 1.5 collective-permute-start.14
  73.6 0.7 copy-done.51
  74.3 13.1 %backward.1 = (bf16[160,1024]{1,0:T(8,128)(2,1)}, bf16[160,1024]{1,0:T(8,128)(2,1)}, bf16[160,1024]{1,0:T(8,128)(2,1)}, bf16[160,1024]{1,0:T(8,128)(2,1)}, bf16[...) custom-call(s32[2]{0:T(128)} %pad_add_fusion.pos, bf16[160,1024]{1,0:T(8,128)(2,1)} %pack.3.refs_0_.refs_4_, ...), custom_call_target="tpu_custom_call" | custom-call | flops 4026531840 | bytes 6291456 | tf_op jit(solution)/shard_map/backward/pallas_call | solution.py:253
  87.4 0.6 collective-permute-start.34
  88.0 10.3 %grads.1 = (bf16[2,1024,512]{2,1,0:T(8,128)(2,1)}, bf16[2,1024,512]{2,1,0:T(8,128)(2,1)}, bf16[2,512,1024]{2,1,0:T(8,128)(2,1)}, bf16[1024,512]{1,0:T(8,128)(2,1...) custom-call(s32[2]{0:T(128)} %pad_add_fusion.pos, bf16[160,1024]{1,0:T(8,128)(2,1)} %pack.2.refs_0_, ...), custom_call_target="tpu_custom_call" | custom-call | flops 4026531840 | bytes 6291456 | tf_op jit(solution)/shard_map/grads/pallas_call | solution.py:308
  98.4 0.7 copy-done.5
  99.2 1.9 %add.25 = bf16[160,1024]{1,0:T(8,128)(2,1)} custom-call(bf16[160,1024]{1,0:T(8,128)(2,1)} %get-tuple-element.46.refs_0_, bf16[160,1024]{1,0:T(8,128)(2,1)} %copy-done.5), custom_call_target="tpu_custom_call" | custom-call | tf_op jit(solution)/shard_map/add/pallas_call | solution.py:348
  101.1 1.5 collective-permute-start.33
  102.5 0.7 copy-done.6
  103.3 1.9 %add.27 = bf16[160,1024]{1,0:T(8,128)(2,1)} custom-call(bf16[160,1024]{1,0:T(8,128)(2,1)} %get-tuple-element.60.refs_0_, bf16[160,1024]{1,0:T(8,128)(2,1)} %copy-done.6), custom_call_target="tpu_custom_call" | custom-call | tf_op jit(solution)/shard_map/add/pallas_call | solution.py:348
  105.2 2.0 %collective-permute-start.35 = (bf16[160,1024]{1,0:T(8,128)(2,1)}, bf16[160,1024]{1,0:T(8,128)(2,1)S(1)}, u32[]{:S(2)}, u32[]{:S(2)}) collective-permute-start(bf16[160,1024]{1,0:T(8,128)(2,1)} %add.27), channel_id=1, source_target_pairs={{0,8},{4,20},{8,0},{12,28},{16,24},{20,4},{24,16},{28,12},{1,9},{5... | collective-permute-start | bytes 983048 | tf_op jit(solution)/shard_map/ppermute | solution.py:428
  107.2 4.2 %collective-permute-done.15.refs_2_ = bf16[160,1024]{1,0:T(8,128)(2,1)S(1)} collective-permute-done((bf16[160,1024]{1,0:T(8,128)(2,1)}, bf16[160,1024]{1,0:T(8,128)(2,1)S(1)}, u32[]{:S(2)}, u32[]{:S(2)}) %collective-permute-start.15) | collective-permute-done | bytes 327712 | tf_op jit(solution)/shard_map/ppermute | solution.py:428
  111.4 0.7 copy-done.7
  112.1 1.9 %add.26 = (bf16[40,1024]{1,0:T(8,128)(2,1)}, bf16[40,1024]{1,0:T(8,128)(2,1)}, bf16[40,1024]{1,0:T(8,128)(2,1)}, bf16[40,1024]{1,0:T(8,128)(2,1)}) custom-call(bf16[160,1024]{1,0:T(8,128)(2,1)} %get-tuple-element.44.refs_0_, bf16[160,1024]{1,0:T(8,128)(2,1)} %copy-done.2, bf16[160,1024]{1,0:T(8,128)(2,1)} %copy-done.7), custom_call_target="tpu_custom_call" | custom-call | tf_op jit(solution)/shard_map/add/pallas_call | solution.py:348
  114.1 1.1 collective-permute-start.16
  115.2 3.0 %collective-permute-start.17 = (bf16[40,1024]{1,0:T(8,128)(2,1)}, bf16[40,1024]{1,0:T(8,128)(2,1)S(1)}, u32[]{:S(2)}, u32[]{:S(2)}) collective-permute-start(bf16[40,1024]{1,0:T(8,128)(2,1)} %get-tuple-element.50), channel_id=1, source_target_pairs={{0,2},{1,3},{2,0},{3,1},{4,6},{5,7},{6,4},{7,5},{8,10},{9,11},{10,... | collective-permute-start | bytes 245768 | tf_op jit(solution)/shard_map/ppermute | solution.py:422
  118.7 4.3 %collective-permute-start.18 = (bf16[40,1024]{1,0:T(8,128)(2,1)}, bf16[40,1024]{1,0:T(8,128)(2,1)S(1)}, u32[]{:S(2)}, u32[]{:S(2)}) collective-permute-start(bf16[40,1024]{1,0:T(8,128)(2,1)} %get-tuple-element.51), channel_id=1, source_target_pairs={{0,3},{1,2},{2,1},{3,0},{4,7},{5,6},{6,5},{7,4},{8,11},{9,10},{10,... | collective-permute-start | bytes 245768 | tf_op jit(solution)/shard_map/ppermute | solution.py:422
  123.1 1.9 %add.28 = (bf16[40,1024]{1,0:T(8,128)(2,1)}, bf16[40,1024]{1,0:T(8,128)(2,1)}, bf16[40,1024]{1,0:T(8,128)(2,1)}, bf16[40,1024]{1,0:T(8,128)(2,1)}) custom-call(bf16[160,1024]{1,0:T(8,128)(2,1)} %get-tuple-element.58.refs_0_, bf16[160,1024]{1,0:T(8,128)(2,1)} %copy-done.3, bf16[160,1024]{1,0:T(8,128)(2,1)} %copy-done.4), custom_call_target="tpu_custom_call" | custom-call | tf_op jit(solution)/shard_map/add/pallas_call | solution.py:348
  125.0 0.7 collective-permute-done.18.refs_3_
  125.7 0.9 collective-permute-start.36
  126.7 3.4 %collective-permute-start.37 = (bf16[40,1024]{1,0:T(8,128)(2,1)}, bf16[40,1024]{1,0:T(8,128)(2,1)S(1)}, u32[]{:S(2)}, u32[]{:S(2)}) collective-permute-start(bf16[40,1024]{1,0:T(8,128)(2,1)} %get-tuple-element.64), channel_id=1, source_target_pairs={{0,2},{1,3},{2,0},{3,1},{4,6},{5,7},{6,4},{7,5},{8,10},{9,11},{10,... | collective-permute-start | bytes 245768 | tf_op jit(solution)/shard_map/ppermute | solution.py:422
  130.4 4.5 %collective-permute-start.38 = (bf16[40,1024]{1,0:T(8,128)(2,1)}, bf16[40,1024]{1,0:T(8,128)(2,1)S(1)}, u32[]{:S(2)}, u32[]{:S(2)}) collective-permute-start(bf16[40,1024]{1,0:T(8,128)(2,1)} %get-tuple-element.65), channel_id=1, source_target_pairs={{0,3},{1,2},{2,1},{3,0},{4,7},{5,6},{6,5},{7,4},{8,11},{9,10},{10,... | collective-permute-start | bytes 245768 | tf_op jit(solution)/shard_map/ppermute | solution.py:422
  134.9 0.6 collective-permute-done.37.refs_2_
  135.5 2.1 %collective-permute-done.38.refs_3_ = bf16[40,1024]{1,0:T(8,128)(2,1)S(1)} collective-permute-done((bf16[40,1024]{1,0:T(8,128)(2,1)}, bf16[40,1024]{1,0:T(8,128)(2,1)S(1)}, u32[]{:S(2)}, u32[]{:S(2)}) %collective-permute-start.38) | collective-permute-done | bytes 81952 | tf_op jit(solution)/shard_map/ppermute | solution.py:422
  138.1 0.8 collective-permute-done.20.refs_5_
  139.4 0.8 collective-permute-done.22.refs_7_
  140.8 3.5 %combine.2 = bf16[64,1024]{1,0:T(8,128)(2,1)} custom-call(s32[2]{0:T(128)} %pad_add_fusion.pos, s32[64,2]{1,0:T(8,128)} %copy.14.ids_ref, f32[64,2]{1,0:T(8,128)} %copy.15.gw_ref, bf16[40,1024]{1,0:T(8,128)(2,1)} %get-tuple-element.48.refs_0_, bf16[40,1024]{1,0:T(8,128)(2,1)} %copy-done.24, bf16[40,1024]{1,0:T(8,128)(2,1)} %copy-done.25, ...), custom_call_target="tpu_custom_call" | custom-call | tf_op jit(solution)/shard_map/combine/pallas_call | solution.py:390
  144.3 0.6 copy-done.35
  144.9 0.6 copy-done.37
  145.5 3.2 %combine.3 = bf16[64,1024]{1,0:T(8,128)(2,1)} custom-call(s32[2]{0:T(128)} %pad_add_fusion.pos, s32[64,2]{1,0:T(8,128)} %copy.14.ids_ref, f32[64,2]{1,0:T(8,128)} %copy.15.gw_ref, bf16[40,1024]{1,0:T(8,128)(2,1)} %get-tuple-element.62.refs_0_, bf16[40,1024]{1,0:T(8,128)(2,1)} %copy-done.28, bf16[40,1024]{1,0:T(8,128)(2,1)} %copy-done.29, ...), custom_call_target="tpu_custom_call" | custom-call | tf_op jit(solution)/shard_map/combine/pallas_call | solution.py:390
  148.8 1.0 bitcast_dynamic-update-slice_fusion.2
  149.9 0.8 copy-done.38
  151.2 1.3 copy-done.39
  (155 shorter events, 6.7 us)
Async XLA Ops:
  0.6 18.4 %copy-start = (bf16[2,1024,512]{2,1,0:T(8,128)(2,1)S(1)}, bf16[2,1024,512]{2,1,0:T(8,128)(2,1)}, u32[]{:S(2)}) copy-start(bf16[2,1024,512]{2,1,0:T(8,128)(2,1)} %refs_5_.3) | copy-start | bytes 6291460
  7.6 11.6 %collective-permute-start = (bf16[40,1024]{1,0:T(8,128)(2,1)}, bf16[40,1024]{1,0:T(8,128)(2,1)S(1)}, u32[]{:S(2)}, u32[]{:S(2)}) collective-permute-start(bf16[40,1024]{1,0:T(8,128)(2,1)} %get-tuple-element.41), channel_id=1, source_target_pairs={{0,1},{1,0},{2,3},{3,2},{4,5},{5,4},{6,7},{7,6},{8,9},{9,8},{10,11... | collective-permute-start | bytes 245768 | tf_op jit(solution)/shard_map/ppermute | solution.py:422
  10.6 10.4 %collective-permute-start.1 = (bf16[40,1024]{1,0:T(8,128)(2,1)}, bf16[40,1024]{1,0:T(8,128)(2,1)S(1)}, u32[]{:S(2)}, u32[]{:S(2)}) collective-permute-start(bf16[40,1024]{1,0:T(8,128)(2,1)} %get-tuple-element.42), channel_id=1, source_target_pairs={{0,2},{1,3},{2,0},{3,1},{4,6},{5,7},{6,4},{7,5},{8,10},{9,11},{10,... | collective-permute-start | bytes 245768 | tf_op jit(solution)/shard_map/ppermute | solution.py:422
  13.2 7.8 %collective-permute-start.2 = (bf16[40,1024]{1,0:T(8,128)(2,1)}, bf16[40,1024]{1,0:T(8,128)(2,1)S(1)}, u32[]{:S(2)}, u32[]{:S(2)}) collective-permute-start(bf16[40,1024]{1,0:T(8,128)(2,1)} %get-tuple-element.43), channel_id=1, source_target_pairs={{0,3},{1,2},{2,1},{3,0},{4,7},{5,6},{6,5},{7,4},{8,11},{9,10},{10,... | collective-permute-start | bytes 245768 | tf_op jit(solution)/shard_map/ppermute | solution.py:422
  13.2 8.3 %collective-permute-start.23 = (bf16[40,1024]{1,0:T(8,128)(2,1)}, bf16[40,1024]{1,0:T(8,128)(2,1)S(1)}, u32[]{:S(2)}, u32[]{:S(2)}) collective-permute-start(bf16[40,1024]{1,0:T(8,128)(2,1)} %get-tuple-element.53), channel_id=1, source_target_pairs={{0,1},{1,0},{2,3},{3,2},{4,5},{5,4},{6,7},{7,6},{8,9},{9,8},{10,11... | collective-permute-start | bytes 245768 | tf_op jit(solution)/shard_map/ppermute | solution.py:422
  14.1 12.9 %collective-permute-start.24 = (bf16[40,1024]{1,0:T(8,128)(2,1)}, bf16[40,1024]{1,0:T(8,128)(2,1)S(1)}, u32[]{:S(2)}, u32[]{:S(2)}) collective-permute-start(bf16[40,1024]{1,0:T(8,128)(2,1)} %get-tuple-element.54), channel_id=1, source_target_pairs={{0,2},{1,3},{2,0},{3,1},{4,6},{5,7},{6,4},{7,5},{8,10},{9,11},{10,... | collective-permute-start | bytes 245768 | tf_op jit(solution)/shard_map/ppermute | solution.py:422
  19.0 8.0 %copy-start.8 = (bf16[40,1024]{1,0:T(8,128)(2,1)S(1)}, bf16[40,1024]{1,0:T(8,128)(2,1)}, u32[]{:S(2)}) copy-start(bf16[40,1024]{1,0:T(8,128)(2,1)} %get-tuple-element.40.refs_0_) | copy-start | bytes 245764
  19.0 8.0 %copy-start.12 = (bf16[40,1024]{1,0:T(8,128)(2,1)S(1)}, bf16[40,1024]{1,0:T(8,128)(2,1)}, u32[]{:S(2)}) copy-start(bf16[40,1024]{1,0:T(8,128)(2,1)} %get-tuple-element.52.refs_0_) | copy-start | bytes 245764
  19.1 17.1 %copy-start.9 = (bf16[40,1024]{1,0:T(8,128)(2,1)}, bf16[40,1024]{1,0:T(8,128)(2,1)S(1)}, u32[]{:S(2)}) copy-start(bf16[40,1024]{1,0:T(8,128)(2,1)S(1)} %collective-permute-done.refs_1_) | copy-start | bytes 245764
  19.2 7.9 %collective-permute-start.25 = (bf16[40,1024]{1,0:T(8,128)(2,1)S(1)}, bf16[40,1024]{1,0:T(8,128)(2,1)S(1)}, u32[]{:S(2)}, u32[]{:S(2)}) collective-permute-start(bf16[40,1024]{1,0:T(8,128)(2,1)S(1)} %copy-done.52), channel_id=1, source_target_pairs={{0,3},{1,2},{2,1},{3,0},{4,7},{5,6},{6,5},{7,4},{8,11},{9,10},{10,... | collective-permute-start | bytes 245768 | tf_op jit(solution)/shard_map/ppermute | solution.py:422
  21.0 15.3 %copy-start.10 = (bf16[40,1024]{1,0:T(8,128)(2,1)}, bf16[40,1024]{1,0:T(8,128)(2,1)S(1)}, u32[]{:S(2)}) copy-start(bf16[40,1024]{1,0:T(8,128)(2,1)S(1)} %collective-permute-done.1.refs_2_) | copy-start | bytes 245764
  21.0 37.5 %collective-permute-start.12 = (bf16[512,1024]{1,0:T(8,128)(2,1)S(1)}, bf16[512,1024]{1,0:T(8,128)(2,1)S(1)}, u32[]{:S(2)}, u32[]{:S(2)}) collective-permute-start(bf16[512,1024]{1,0:T(8,128)(2,1)S(1)} %dynamic-slice_bitcast_fusion), channel_id=1, source_target_pairs={{0,4},{4,0},{8,12},{12,8},{16,20},{20,16},{24,28},{28,24},{1,5},{5... | collective-permute-start | bytes 3145736 | tf_op jit(solution)/shard_map/ppermute | solution.py:419
  21.0 15.3 %copy-start.11 = (bf16[40,1024]{1,0:T(8,128)(2,1)}, bf16[40,1024]{1,0:T(8,128)(2,1)S(1)}, u32[]{:S(2)}) copy-start(bf16[40,1024]{1,0:T(8,128)(2,1)S(1)} %collective-permute-done.2.refs_3_) | copy-start | bytes 245764
  21.0 37.5 %collective-permute-start.11 = (bf16[1024,512]{1,0:T(8,128)(2,1)S(1)}, bf16[1024,512]{1,0:T(8,128)(2,1)S(1)}, u32[]{:S(2)}, u32[]{:S(2)}) collective-permute-start(bf16[1024,512]{1,0:T(8,128)(2,1)S(1)} %dynamic-slice_bitcast_fusion.1), channel_id=1, source_target_pairs={{0,4},{4,0},{8,12},{12,8},{16,20},{20,16},{24,28},{28,24},{1,5},{5... | collective-permute-start | bytes 3145736 | tf_op jit(solution)/shard_map/ppermute | solution.py:419
  21.5 10.0 %copy-start.13 = (bf16[40,1024]{1,0:T(8,128)(2,1)}, bf16[40,1024]{1,0:T(8,128)(2,1)S(1)}, u32[]{:S(2)}) copy-start(bf16[40,1024]{1,0:T(8,128)(2,1)S(1)} %collective-permute-done.23.refs_1_) | copy-start | bytes 245764
  21.5 37.0 %collective-permute-start.10 = (bf16[1024,512]{1,0:T(8,128)(2,1)S(1)}, bf16[1024,512]{1,0:T(8,128)(2,1)S(1)}, u32[]{:S(2)}, u32[]{:S(2)}) collective-permute-start(bf16[1024,512]{1,0:T(8,128)(2,1)S(1)} %dynamic-slice_bitcast_fusion.2), channel_id=1, source_target_pairs={{0,4},{4,0},{8,12},{12,8},{16,20},{20,16},{24,28},{28,24},{1,5},{5... | collective-permute-start | bytes 3145736 | tf_op jit(solution)/shard_map/ppermute | solution.py:419
  27.0 1.3 collective-permute-start.3
  27.1 1.5 collective-permute-start.26
  28.3 1.3 collective-permute-start.4
  28.5 1.3 collective-permute-start.27
  29.6 1.3 collective-permute-start.28
  29.8 1.3 collective-permute-start.29
  30.9 3.8 %collective-permute-start.5 = (bf16[40,1024]{1,0:T(8,128)(2,1)S(1)}, bf16[40,1024]{1,0:T(8,128)(2,1)S(1)}, u32[]{:S(2)}, u32[]{:S(2)}) collective-permute-start(bf16[40,1024]{1,0:T(8,128)(2,1)S(1)} %collective-permute-done.1.refs_2_), channel_id=1, source_target_pairs={{0,4},{4,0},{8,12},{12,8},{16,20},{20,16},{24,28},{28,24},{1,5},{5... | collective-permute-start | bytes 245768 | tf_op jit(solution)/shard_map/ppermute | solution.py:419
  31.1 5.1 %collective-permute-start.6 = (bf16[40,1024]{1,0:T(8,128)(2,1)S(1)}, bf16[40,1024]{1,0:T(8,128)(2,1)S(1)}, u32[]{:S(2)}, u32[]{:S(2)}) collective-permute-start(bf16[40,1024]{1,0:T(8,128)(2,1)S(1)} %collective-permute-done.2.refs_3_), channel_id=1, source_target_pairs={{0,4},{4,0},{8,12},{12,8},{16,20},{20,16},{24,28},{28,24},{1,5},{5... | collective-permute-start | bytes 245768 | tf_op jit(solution)/shard_map/ppermute | solution.py:419
  34.6 7.3 %collective-permute-start.30 = (bf16[160,1024]{1,0:T(8,128)(2,1)}, bf16[160,1024]{1,0:T(8,128)(2,1)S(1)}, u32[]{:S(2)}, u32[]{:S(2)}) collective-permute-start(bf16[160,1024]{1,0:T(8,128)(2,1)} %pack.3.refs_0_.refs_4_), channel_id=1, source_target_pairs={{0,8},{4,20},{8,0},{12,28},{16,24},{20,4},{24,16},{28,12},{1,9},{5... | collective-permute-start | bytes 983048 | tf_op jit(solution)/shard_map/ppermute | solution.py:428
  39.8 10.1 %collective-permute-start.7 = (bf16[160,1024]{1,0:T(8,128)(2,1)}, bf16[160,1024]{1,0:T(8,128)(2,1)S(1)}, u32[]{:S(2)}, u32[]{:S(2)}) collective-permute-start(bf16[160,1024]{1,0:T(8,128)(2,1)} %pack.2.refs_0_), channel_id=1, source_target_pairs={{0,8},{4,20},{8,0},{12,28},{16,24},{20,4},{24,16},{28,12},{1,9},{5... | collective-permute-start | bytes 983048 | tf_op jit(solution)/shard_map/ppermute | solution.py:428
  42.0 29.5 %copy-start.46 = (bf16[160,1024]{1,0:T(8,128)(2,1)}, bf16[160,1024]{1,0:T(8,128)(2,1)S(1)}, u32[]{:S(2)}) copy-start(bf16[160,1024]{1,0:T(8,128)(2,1)S(1)} %collective-permute-done.30.refs_1_.refs_5_) | copy-start | bytes 983044
  42.0 9.4 %collective-permute-start.8 = (bf16[160,1024]{1,0:T(8,128)(2,1)}, bf16[160,1024]{1,0:T(8,128)(2,1)S(1)}, u32[]{:S(2)}, u32[]{:S(2)}) collective-permute-start(bf16[160,1024]{1,0:T(8,128)(2,1)} %pack.2.refs_0_), channel_id=1, source_target_pairs={{0,16},{4,12},{8,24},{12,4},{16,0},{20,28},{24,8},{28,20},{1,17},{... | collective-permute-start | bytes 983048 | tf_op jit(solution)/shard_map/ppermute | solution.py:428
  49.9 8.6 %copy-start.47 = (bf16[160,1024]{1,0:T(8,128)(2,1)}, bf16[160,1024]{1,0:T(8,128)(2,1)S(1)}, u32[]{:S(2)}) copy-start(bf16[160,1024]{1,0:T(8,128)(2,1)S(1)} %collective-permute-done.7.refs_1_) | copy-start | bytes 983044
  49.9 7.1 %collective-permute-start.9 = (bf16[160,1024]{1,0:T(8,128)(2,1)S(1)}, bf16[160,1024]{1,0:T(8,128)(2,1)S(1)}, u32[]{:S(2)}, u32[]{:S(2)}) collective-permute-start(bf16[160,1024]{1,0:T(8,128)(2,1)S(1)} %collective-permute-done.7.refs_1_), channel_id=1, source_target_pairs={{0,16},{4,12},{8,24},{12,4},{16,0},{20,28},{24,8},{28,20},{1,17},{... | collective-permute-start | bytes 983048 | tf_op jit(solution)/shard_map/ppermute | solution.py:428
  51.4 22.2 %collective-permute-start.31 = (bf16[160,1024]{1,0:T(8,128)(2,1)}, bf16[160,1024]{1,0:T(8,128)(2,1)S(1)}, u32[]{:S(2)}, u32[]{:S(2)}) collective-permute-start(bf16[160,1024]{1,0:T(8,128)(2,1)} %pack.3.refs_0_.refs_4_), channel_id=1, source_target_pairs={{0,16},{4,12},{8,24},{12,4},{16,0},{20,28},{24,8},{28,20},{1,17},{... | collective-permute-start | bytes 983048 | tf_op jit(solution)/shard_map/ppermute | solution.py:428
  57.0 16.6 %collective-permute-start.32 = (bf16[160,1024]{1,0:T(8,128)(2,1)S(1)}, bf16[160,1024]{1,0:T(8,128)(2,1)}, u32[]{:S(2)}, u32[]{:S(2)}) collective-permute-start(bf16[160,1024]{1,0:T(8,128)(2,1)S(1)} %collective-permute-done.30.refs_1_.refs_5_), channel_id=1, source_target_pairs={{0,16},{4,12},{8,24},{12,4},{16,0},{20,28},{24,8},{28,20},{1,17},{... | collective-permute-start | bytes 983048 | tf_op jit(solution)/shard_map/ppermute | solution.py:428
  71.5 35.7 %collective-permute-start.13 = (bf16[160,1024]{1,0:T(8,128)(2,1)}, bf16[160,1024]{1,0:T(8,128)(2,1)S(1)}, u32[]{:S(2)}, u32[]{:S(2)}) collective-permute-start(bf16[160,1024]{1,0:T(8,128)(2,1)} %get-tuple-element.45), channel_id=1, source_target_pairs={{0,16},{4,12},{8,24},{12,4},{16,0},{20,28},{24,8},{28,20},{1,17},{... | collective-permute-start | bytes 983048 | tf_op jit(solution)/shard_map/ppermute | solution.py:428
  72.1 26.3 %collective-permute-start.14 = (bf16[160,1024]{1,0:T(8,128)(2,1)}, bf16[160,1024]{1,0:T(8,128)(2,1)S(1)}, u32[]{:S(2)}, u32[]{:S(2)}) collective-permute-start(bf16[160,1024]{1,0:T(8,128)(2,1)} %get-tuple-element.47), channel_id=1, source_target_pairs={{0,16},{4,12},{8,24},{12,4},{16,0},{20,28},{24,8},{28,20},{1,17},{... | collective-permute-start | bytes 983048 | tf_op jit(solution)/shard_map/ppermute | solution.py:428
  87.4 15.1 %collective-permute-start.34 = (bf16[160,1024]{1,0:T(8,128)(2,1)}, bf16[160,1024]{1,0:T(8,128)(2,1)S(1)}, u32[]{:S(2)}, u32[]{:S(2)}) collective-permute-start(bf16[160,1024]{1,0:T(8,128)(2,1)} %get-tuple-element.61), channel_id=1, source_target_pairs={{0,16},{4,12},{8,24},{12,4},{16,0},{20,28},{24,8},{28,20},{1,17},{... | collective-permute-start | bytes 983048 | tf_op jit(solution)/shard_map/ppermute | solution.py:428
  88.0 13.0 %copy-start.48 = (bf16[160,1024]{1,0:T(8,128)(2,1)S(1)}, bf16[160,1024]{1,0:T(8,128)(2,1)}, u32[]{:S(2)}) copy-start(bf16[160,1024]{1,0:T(8,128)(2,1)} %get-tuple-element.59) | copy-start | bytes 983044
  98.3 19.9 %copy-start.42 = (bf16[512,1024]{1,0:T(8,128)(2,1)S(1)}, bf16[512,1024]{1,0:T(8,128)(2,1)}, u32[]{:S(2)}) copy-start(bf16[512,1024]{1,0:T(8,128)(2,1)} %get-tuple-element.74) | copy-start | bytes 3145732
  98.3 50.4 %collective-permute-start.43 = (bf16[1024,512]{1,0:T(8,128)(2,1)}, bf16[1024,512]{1,0:T(8,128)(2,1)S(1)}, u32[]{:S(2)}, u32[]{:S(2)}) collective-permute-start(bf16[1024,512]{1,0:T(8,128)(2,1)} %get-tuple-element.70), channel_id=1, source_target_pairs={{0,4},{4,0},{8,12},{12,8},{16,20},{20,16},{24,28},{28,24},{1,5},{5... | collective-permute-start | bytes 3145736 | tf_op jit(solution)/shard_map/ppermute | solution.py:419
  101.0 10.3 %collective-permute-start.15 = (bf16[160,1024]{1,0:T(8,128)(2,1)}, bf16[160,1024]{1,0:T(8,128)(2,1)S(1)}, u32[]{:S(2)}, u32[]{:S(2)}) collective-permute-start(bf16[160,1024]{1,0:T(8,128)(2,1)} %add.25), channel_id=1, source_target_pairs={{0,8},{4,20},{8,0},{12,28},{16,24},{20,4},{24,16},{28,12},{1,9},{5... | collective-permute-start | bytes 983048 | tf_op jit(solution)/shard_map/ppermute | solution.py:428
  101.1 14.1 %collective-permute-start.33 = (bf16[160,1024]{1,0:T(8,128)(2,1)S(1)}, bf16[160,1024]{1,0:T(8,128)(2,1)S(1)}, u32[]{:S(2)}, u32[]{:S(2)}) collective-permute-start(bf16[160,1024]{1,0:T(8,128)(2,1)S(1)} %copy-done.48), channel_id=1, source_target_pairs={{0,16},{4,12},{8,24},{12,4},{16,0},{20,28},{24,8},{28,20},{1,17},{... | collective-permute-start | bytes 983048 | tf_op jit(solution)/shard_map/ppermute | solution.py:428
  105.2 13.1 %collective-permute-start.35 = (bf16[160,1024]{1,0:T(8,128)(2,1)}, bf16[160,1024]{1,0:T(8,128)(2,1)S(1)}, u32[]{:S(2)}, u32[]{:S(2)}) collective-permute-start(bf16[160,1024]{1,0:T(8,128)(2,1)} %add.27), channel_id=1, source_target_pairs={{0,8},{4,20},{8,0},{12,28},{16,24},{20,4},{24,16},{28,12},{1,9},{5... | collective-permute-start | bytes 983048 | tf_op jit(solution)/shard_map/ppermute | solution.py:428
  107.2 42.6 %collective-permute-start.44 = (bf16[1024,512]{1,0:T(8,128)(2,1)}, bf16[1024,512]{1,0:T(8,128)(2,1)S(1)}, u32[]{:S(2)}, u32[]{:S(2)}) collective-permute-start(bf16[1024,512]{1,0:T(8,128)(2,1)} %get-tuple-element.72), channel_id=1, source_target_pairs={{0,4},{4,0},{8,12},{12,8},{16,20},{20,16},{24,28},{28,24},{1,5},{5... | collective-permute-start | bytes 3145736 | tf_op jit(solution)/shard_map/ppermute | solution.py:419
  114.1 4.7 %collective-permute-start.16 = (bf16[40,1024]{1,0:T(8,128)(2,1)}, bf16[40,1024]{1,0:T(8,128)(2,1)S(1)}, u32[]{:S(2)}, u32[]{:S(2)}) collective-permute-start(bf16[40,1024]{1,0:T(8,128)(2,1)} %get-tuple-element.49), channel_id=1, source_target_pairs={{0,1},{1,0},{2,3},{3,2},{4,5},{5,4},{6,7},{7,6},{8,9},{9,8},{10,11... | collective-permute-start | bytes 245768 | tf_op jit(solution)/shard_map/ppermute | solution.py:422
  115.2 7.9 %collective-permute-start.17 = (bf16[40,1024]{1,0:T(8,128)(2,1)}, bf16[40,1024]{1,0:T(8,128)(2,1)S(1)}, u32[]{:S(2)}, u32[]{:S(2)}) collective-permute-start(bf16[40,1024]{1,0:T(8,128)(2,1)} %get-tuple-element.50), channel_id=1, source_target_pairs={{0,2},{1,3},{2,0},{3,1},{4,6},{5,7},{6,4},{7,5},{8,10},{9,11},{10,... | collective-permute-start | bytes 245768 | tf_op jit(solution)/shard_map/ppermute | solution.py:422
  118.2 31.7 %collective-permute-start.45 = (bf16[512,1024]{1,0:T(8,128)(2,1)S(1)}, bf16[512,1024]{1,0:T(8,128)(2,1)S(1)}, u32[]{:S(2)}, u32[]{:S(2)}) collective-permute-start(bf16[512,1024]{1,0:T(8,128)(2,1)S(1)} %copy-done.42), channel_id=1, source_target_pairs={{0,4},{4,0},{8,12},{12,8},{16,20},{20,16},{24,28},{28,24},{1,5},{5... | collective-permute-start | bytes 3145736 | tf_op jit(solution)/shard_map/ppermute | solution.py:419
  118.7 22.0 %copy-start.24 = (bf16[40,1024]{1,0:T(8,128)(2,1)}, bf16[40,1024]{1,0:T(8,128)(2,1)S(1)}, u32[]{:S(2)}) copy-start(bf16[40,1024]{1,0:T(8,128)(2,1)S(1)} %collective-permute-done.16.refs_1_) | copy-start | bytes 245764
  118.7 7.0 %collective-permute-start.18 = (bf16[40,1024]{1,0:T(8,128)(2,1)}, bf16[40,1024]{1,0:T(8,128)(2,1)S(1)}, u32[]{:S(2)}, u32[]{:S(2)}) collective-permute-start(bf16[40,1024]{1,0:T(8,128)(2,1)} %get-tuple-element.51), channel_id=1, source_target_pairs={{0,3},{1,2},{2,1},{3,0},{4,7},{5,6},{6,5},{7,4},{8,11},{9,10},{10,... | collective-permute-start | bytes 245768 | tf_op jit(solution)/shard_map/ppermute | solution.py:422
  123.1 17.6 %copy-start.25 = (bf16[40,1024]{1,0:T(8,128)(2,1)}, bf16[40,1024]{1,0:T(8,128)(2,1)S(1)}, u32[]{:S(2)}) copy-start(bf16[40,1024]{1,0:T(8,128)(2,1)S(1)} %collective-permute-done.17.refs_2_) | copy-start | bytes 245764
  123.1 3.6 %collective-permute-start.19 = (bf16[40,1024]{1,0:T(8,128)(2,1)}, bf16[40,1024]{1,0:T(8,128)(2,1)S(1)}, u32[]{:S(2)}, u32[]{:S(2)}) collective-permute-start(bf16[40,1024]{1,0:T(8,128)(2,1)} %get-tuple-element.48.refs_0_), channel_id=1, source_target_pairs={{0,4},{4,0},{8,12},{12,8},{16,20},{20,16},{24,28},{28,24},{1,5},{5... | collective-permute-start | bytes 245768 | tf_op jit(solution)/shard_map/ppermute | solution.py:419
  125.0 24.8 %copy-start.40 = (bf16[2,1024,512]{2,1,0:T(8,128)(2,1)S(1)}, bf16[2,1024,512]{2,1,0:T(8,128)(2,1)}, u32[]{:S(2)}) copy-start(bf16[2,1024,512]{2,1,0:T(8,128)(2,1)} %get-tuple-element.71) | copy-start | bytes 6291460
  125.7 14.9 %copy-start.26 = (bf16[40,1024]{1,0:T(8,128)(2,1)}, bf16[40,1024]{1,0:T(8,128)(2,1)S(1)}, u32[]{:S(2)}) copy-start(bf16[40,1024]{1,0:T(8,128)(2,1)S(1)} %collective-permute-done.18.refs_3_) | copy-start | bytes 245764
  125.7 4.7 %collective-permute-start.36 = (bf16[40,1024]{1,0:T(8,128)(2,1)}, bf16[40,1024]{1,0:T(8,128)(2,1)S(1)}, u32[]{:S(2)}, u32[]{:S(2)}) collective-permute-start(bf16[40,1024]{1,0:T(8,128)(2,1)} %get-tuple-element.63), channel_id=1, source_target_pairs={{0,1},{1,0},{2,3},{3,2},{4,5},{5,4},{6,7},{7,6},{8,9},{9,8},{10,11... | collective-permute-start | bytes 245768 | tf_op jit(solution)/shard_map/ppermute | solution.py:422
  126.7 14.0 %copy-start.27 = (bf16[40,1024]{1,0:T(8,128)(2,1)}, bf16[40,1024]{1,0:T(8,128)(2,1)S(1)}, u32[]{:S(2)}) copy-start(bf16[40,1024]{1,0:T(8,128)(2,1)S(1)} %collective-permute-done.19.refs_4_) | copy-start | bytes 245764
  126.7 8.8 %collective-permute-start.37 = (bf16[40,1024]{1,0:T(8,128)(2,1)}, bf16[40,1024]{1,0:T(8,128)(2,1)S(1)}, u32[]{:S(2)}, u32[]{:S(2)}) collective-permute-start(bf16[40,1024]{1,0:T(8,128)(2,1)} %get-tuple-element.64), channel_id=1, source_target_pairs={{0,2},{1,3},{2,0},{3,1},{4,6},{5,7},{6,4},{7,5},{8,10},{9,11},{10,... | collective-permute-start | bytes 245768 | tf_op jit(solution)/shard_map/ppermute | solution.py:422
  130.4 13.9 %copy-start.28 = (bf16[40,1024]{1,0:T(8,128)(2,1)}, bf16[40,1024]{1,0:T(8,128)(2,1)S(1)}, u32[]{:S(2)}) copy-start(bf16[40,1024]{1,0:T(8,128)(2,1)S(1)} %collective-permute-done.36.refs_1_) | copy-start | bytes 245764
  130.4 7.2 %collective-permute-start.38 = (bf16[40,1024]{1,0:T(8,128)(2,1)}, bf16[40,1024]{1,0:T(8,128)(2,1)S(1)}, u32[]{:S(2)}, u32[]{:S(2)}) collective-permute-start(bf16[40,1024]{1,0:T(8,128)(2,1)} %get-tuple-element.65), channel_id=1, source_target_pairs={{0,3},{1,2},{2,1},{3,0},{4,7},{5,6},{6,5},{7,4},{8,11},{9,10},{10,... | collective-permute-start | bytes 245768 | tf_op jit(solution)/shard_map/ppermute | solution.py:422
  135.5 8.8 %copy-start.29 = (bf16[40,1024]{1,0:T(8,128)(2,1)}, bf16[40,1024]{1,0:T(8,128)(2,1)S(1)}, u32[]{:S(2)}) copy-start(bf16[40,1024]{1,0:T(8,128)(2,1)S(1)} %collective-permute-done.37.refs_2_) | copy-start | bytes 245764
  135.5 2.1 %collective-permute-start.39 = (bf16[40,1024]{1,0:T(8,128)(2,1)}, bf16[40,1024]{1,0:T(8,128)(2,1)S(1)}, u32[]{:S(2)}, u32[]{:S(2)}) collective-permute-start(bf16[40,1024]{1,0:T(8,128)(2,1)} %get-tuple-element.62.refs_0_), channel_id=1, source_target_pairs={{0,4},{4,0},{8,12},{12,8},{16,20},{20,16},{24,28},{28,24},{1,5},{5... | collective-permute-start | bytes 245768 | tf_op jit(solution)/shard_map/ppermute | solution.py:419
  137.6 1.3 collective-permute-start.20
  137.6 1.4 collective-permute-start.21
  138.9 1.3 collective-permute-start.22
  139.0 1.3 collective-permute-start.40
  140.2 4.1 %collective-permute-start.41 = (bf16[40,1024]{1,0:T(8,128)(2,1)S(1)}, bf16[40,1024]{1,0:T(8,128)(2,1)S(1)}, u32[]{:S(2)}, u32[]{:S(2)}) collective-permute-start(bf16[40,1024]{1,0:T(8,128)(2,1)S(1)} %collective-permute-done.37.refs_2_), channel_id=1, source_target_pairs={{0,4},{4,0},{8,12},{12,8},{16,20},{20,16},{24,28},{28,24},{1,5},{5... | collective-permute-start | bytes 245768 | tf_op jit(solution)/shard_map/ppermute | solution.py:419
  140.3 4.0 %collective-permute-start.42 = (bf16[40,1024]{1,0:T(8,128)(2,1)S(1)}, bf16[40,1024]{1,0:T(8,128)(2,1)S(1)}, u32[]{:S(2)}, u32[]{:S(2)}) collective-permute-start(bf16[40,1024]{1,0:T(8,128)(2,1)S(1)} %collective-permute-done.38.refs_3_), channel_id=1, source_target_pairs={{0,4},{4,0},{8,12},{12,8},{16,20},{20,16},{24,28},{28,24},{1,5},{5... | collective-permute-start | bytes 245768 | tf_op jit(solution)/shard_map/ppermute | solution.py:419
  (35 other events, 94.3 us)

commit v2 on v0

v2 whole, which is shorter than its diff:
```python
import functools

import jax
import jax.numpy as jnp
from jax import lax
from jax.experimental import pallas as pl
from jax.experimental.pallas import tpu as pltpu
from jax.sharding import PartitionSpec as P

BF = jnp.bfloat16
F32 = jnp.float32
NN = (((1,), (0,)), ((), ()))
NT = (((1,), (1,)), ((), ()))
TN = (((0,), (0,)), ((), ()))
MIB = 1024 * 1024
VMEM = pl.BlockSpec(memory_space=pltpu.VMEM)
SMEM = pl.BlockSpec(memory_space=pltpu.SMEM)
HBM = pl.BlockSpec(memory_space=pltpu.HBM)


def dot(a, b, dims=NN):
    return lax.dot_general(a, b, dims, preferred_element_type=F32)


def shaped(*shape):
    return jax.ShapeDtypeStruct(shape, BF)


def kernel_call(kernel, name, in_specs, out_specs, out_shape, scratch=(), limit=4, flops=0, alias=None):
    return pl.pallas_call(
        kernel,
        in_specs=in_specs,
        out_specs=out_specs,
        out_shape=out_shape,
        scratch_shapes=list(scratch),
        input_output_aliases=alias or {},
        cost_estimate=pl.CostEstimate(flops=flops, bytes_accessed=0, transcendentals=0),
        compiler_params=pltpu.CompilerParams(vmem_limit_bytes=limit * MIB),
        name=name,
    )


def places(ids, experts):
    top, toks = ids.shape
    rows = lax.broadcasted_iota(jnp.int32, (experts, toks), 0)
    hot = [(ids[k : k + 1, :] == rows).astype(F32) for k in range(top)]
    earlier = (
        lax.broadcasted_iota(jnp.int32, (toks, toks), 0)
        < lax.broadcasted_iota(jnp.int32, (toks, toks), 1)
    ).astype(BF)
    counts = dot(sum(hot).astype(BF), earlier)
    return [jnp.sum(counts * h, axis=0, keepdims=True).astype(jnp.int32) for h in hot]


def place_kernel(experts, local, cap, expert_pos, ids_hbm, gw_hbm, tok_hbm, cot_hbm, *refs):
    owners = experts // local
    outs = refs[: 2 * owners]
    ids_ref, gw_ref, tok_ref, cot_ref, sems = refs[2 * owners :]
    copies = [
        pltpu.make_async_copy(src, dst, sems.at[i])
        for i, (src, dst) in enumerate(
            ((ids_hbm, ids_ref), (gw_hbm, gw_ref), (tok_hbm, tok_ref), (cot_hbm, cot_ref))
        )
    ]
    for c in copies:
        c.start()
    copies[0].wait()
    copies[1].wait()
    ids = ids_ref[...]
    gw = gw_ref[...]
    top, toks = ids.shape
    here = places(ids, experts)
    rel = jnp.bitwise_xor(ids // local, expert_pos[0])
    rows = lax.broadcasted_iota(jnp.int32, (local * cap, toks), 0)
    col = [(ids[k : k + 1, :] % local) * cap + here[k] for k in range(top)]
    picks = []
    for j in range(owners):
        hits = [
            jnp.where((rel[k : k + 1, :] == j) & (col[k] == rows), 1.0, 0.0) for k in range(top)
        ]
        scale = jnp.sum(
            sum(hits[k] * gw[k : k + 1, :] for k in range(top)), axis=1, keepdims=True
        )
        picks.append((sum(hits).astype(BF), scale))
    copies[2].wait()
    for j in range(owners):
        outs[j][...] = dot(picks[j][0], tok_ref[...]).astype(BF)
    copies[3].wait()
    for j in range(owners):
        outs[owners + j][...] = (picks[j][1] * dot(picks[j][0], cot_ref[...])).astype(BF)


def place(expert_pos, ids, gw, tokens, cot, experts, local, cap):
    width = tokens.shape[1]
    owners = experts // local
    return kernel_call(
        functools.partial(place_kernel, experts, local, cap),
        "place",
        [SMEM] + [HBM] * 4,
        [VMEM] * (2 * owners),
        [shaped(local * cap, width)] * (2 * owners),
        [pltpu.VMEM(a.shape, a.dtype) for a in (ids, gw, tokens, cot)]
        + [pltpu.SemaphoreType.DMA((4,))],
    )(expert_pos, ids, gw, tokens, cot)


def pack_kernel(owners, cap, core, *refs):
    mine, theirs, out = refs[:owners], refs[owners : 2 * owners], refs[-1]
    size = mine[0].shape[0]
    row = lax.broadcasted_iota(jnp.int32, (size, size), 0)
    column = lax.broadcasted_iota(jnp.int32, (size, size), 1)
    first = core[0] * cap
    keep = jnp.where((row < cap) & (column == first + row), 1.0, 0.0).astype(BF)
    take = jnp.where((row >= cap) & (column == first + row - cap), 1.0, 0.0).astype(BF)
    parts = [dot(keep, mine[j][...]) + dot(take, theirs[j][...]) for j in range(owners)]
    out[...] = jnp.concatenate(parts, axis=0).astype(BF)


def pack(core, mine, theirs, cap):
    size, width = mine[0].shape
    owners = len(mine)
    return kernel_call(
        functools.partial(pack_kernel, owners, cap),
        "pack",
        [SMEM] + [VMEM] * (2 * owners),
        VMEM,
        shaped(owners * size, width),
    )(core, *mine, *theirs)


def fetch(core, weights, held, sems):
    return [
        pltpu.make_async_copy(w.at[core[0]], h, sems.at[i])
        for i, (w, h) in enumerate(zip(weights, held))
    ]


def gather_rows(parts, out):
    size = parts[0].shape[0]
    for i, part in enumerate(parts):
        out[i * size : (i + 1) * size, :] = part[...]


def tile_of(hidden):
    return 256 if hidden % 256 == 0 else hidden


def chunks(total, size):
    return [slice(i, min(i + size, total)) for i in range(0, total, size)]


def forward_kernel(chips, core, *refs):
    xs, own, other = refs[:chips], refs[chips : chips + 3], refs[chips + 3 : chips + 6]
    ps = refs[chips + 6 : 2 * chips + 6]
    x, f1, f2, hid, wg, wu, wd, gate_s, up_s, sems = refs[2 * chips + 6 :]
    loads = fetch(core, own, (wg, wu, wd), sems)
    for c in loads:
        c.start()
    gather_rows(xs, x)
    hidden = wg.shape[1]
    rows, width = x.shape
    size = rows // chips
    turn = 0
    for half, (a, b) in ((1, other[:2]), (0, (wg, wu))):
        if half == 0:
            loads[0].wait()
            loads[1].wait()
        for cols in chunks(hidden, tile_of(hidden)):
            gate_s[turn] = dot(x[...], a[:, cols])
            up_s[turn] = dot(x[...], b[:, cols])
            for r in chunks(rows, 64):
                gate, up = gate_s[turn, r], up_s[turn, r]
                sig = 1.0 / (1.0 + jnp.exp(-gate))
                act = gate * sig
                hid[half, r, cols] = (act * up).astype(BF)
                f1[half, r, cols] = (up * sig * (1.0 + gate * (1.0 - sig))).astype(BF)
                f2[half, r, cols] = act.astype(BF)
            turn = 1 - turn
    loads[2].wait()
    for cols in chunks(width, tile_of(width)):
        total = dot(hid[1], other[2][:, cols]) + dot(hid[0], wd[:, cols])
        for i in range(chips):
            ps[i][:, cols] = total[i * size : (i + 1) * size].astype(BF)


def forward(core, xs, own, other):
    chips = len(xs)
    size, width = xs[0].shape
    hidden = other[0].shape[1]
    rows = chips * size
    factor = shaped(2, rows, hidden)
    out = kernel_call(
        functools.partial(forward_kernel, chips),
        "forward",
        [SMEM] + [VMEM] * chips + [HBM] * 3 + [VMEM] * 3,
        [VMEM] * (chips + 4),
        [shaped(size, width)] * chips + [shaped(rows, width)] + [factor] * 3,
        [pltpu.VMEM(w.shape, BF) for w in other]
        + [pltpu.VMEM((2, rows, tile_of(hidden)), F32)] * 2
        + [pltpu.SemaphoreType.DMA((3,))],
        limit=32,
        flops=12 * rows * width * hidden,
    )(core, *xs, *own, *other)
    return out[:chips], *out[chips:]


def backward_kernel(chips, core, *refs):
    dys, own, other = refs[:chips], refs[chips : chips + 3], refs[chips + 3 : chips + 6]
    f1, f2 = refs[chips + 6 : chips + 8]
    qs = refs[chips + 8 : 2 * chips + 8]
    dy, dg, du, wg, wu, wd, da_s, sems = refs[2 * chips + 8 :]
    loads = fetch(core, own, (wg, wu, wd), sems)
    for i in (2, 0, 1):
        loads[i].start()
    gather_rows(dys, dy)
    hidden = wg.shape[1]
    rows, width = dy.shape
    size = rows // chips
    turn = 0
    for half, a in ((1, other[2]), (0, wd)):
        if half == 0:
            loads[2].wait()
        for cols in chunks(hidden, tile_of(hidden)):
            da_s[turn] = dot(dy[...], a[cols, :], NT)
            for r in chunks(rows, 64):
                da = da_s[turn, r]
                dg[half, r, cols] = (da * f1[half, r, cols].astype(F32)).astype(BF)
                du[half, r, cols] = (da * f2[half, r, cols].astype(F32)).astype(BF)
            turn = 1 - turn
    loads[0].wait()
    loads[1].wait()
    for cols in chunks(width, tile_of(width)):
        total = dot(dg[1], other[0][cols, :], NT) + dot(du[1], other[1][cols, :], NT)
        total = total + dot(dg[0], wg[cols, :], NT) + dot(du[0], wu[cols, :], NT)
        for i in range(chips):
            qs[i][:, cols] = total[i * size : (i + 1) * size].astype(BF)


def backward(core, dys, own, other, f1, f2):
    chips = len(dys)
    size, width = dys[0].shape
    hidden = other[0].shape[1]
    rows = chips * size
    factor = shaped(2, rows, hidden)
    out = kernel_call(
        functools.partial(backward_kernel, chips),
        "backward",
        [SMEM] + [VMEM] * chips + [HBM] * 3 + [VMEM] * 5,
        [VMEM] * (chips + 3),
        [shaped(size, width)] * chips + [shaped(rows, width)] + [factor] * 2,
        [pltpu.VMEM(w.shape, BF) for w in other]
        + [pltpu.VMEM((2, rows, tile_of(hidden)), F32)]
        + [pltpu.SemaphoreType.DMA((3,))],
        limit=32,
        flops=12 * rows * width * hidden,
    )(core, *dys, *own, *other, f1, f2)
    return out[:chips], *out[chips:]


def grads_kernel(core, x, dy, dg, du, hid, *refs):
    given, kept, held, sems = refs[:3], refs[3:6], refs[6:9], refs[9]
    hidden = dg.shape[2]
    width = x.shape[1]
    for half, outs in ((1, given), (0, held)):
        for cols in chunks(hidden, tile_of(hidden)):
            outs[0][:, cols] = dot(x[...], dg[half, :, cols], TN).astype(BF)
        if half == 0:
            save = [
                pltpu.make_async_copy(h, k.at[core[0]], sems.at[i])
                for i, (h, k) in enumerate(zip(held, kept))
            ]
            save[0].start()
        for cols in chunks(hidden, tile_of(hidden)):
            outs[1][:, cols] = dot(x[...], du[half, :, cols], TN).astype(BF)
        if half == 0:
            save[1].start()
        for cols in chunks(width, tile_of(width)):
            outs[2][:, cols] = dot(hid[half], dy[:, cols], TN).astype(BF)
        if half == 0:
            save[2].start()
            for c in save:
                c.wait()


def grads(core, x, dy, dg, du, hid, local):
    rows, width = x.shape
    hidden = dg.shape[2]
    shapes = [(width, hidden), (width, hidden), (hidden, width)]
    out = kernel_call(
        grads_kernel,
        "grads",
        [SMEM] + [VMEM] * 5,
        [VMEM] * 3 + [HBM] * 3,
        [shaped(*s) for s in shapes] + [shaped(local, *s) for s in shapes],
        [pltpu.VMEM(s, BF) for s in shapes] + [pltpu.SemaphoreType.DMA((3,))],
        limit=32,
        flops=12 * rows * width * hidden,
    )(core, x, dy, dg, du, hid)
    return out[:3], out[3:]


def finish_kernel(core, *refs):
    got, outs, sems = refs[:3], refs[6:9], refs[9]
    copies = [
        pltpu.make_async_copy(g, o.at[1 - core[0]], sems.at[i])
        for i, (g, o) in enumerate(zip(got, outs))
    ]
    for c in copies:
        c.start()
    for c in copies:
        c.wait()


def finish(core, got, kept):
    return kernel_call(
        finish_kernel,
        "finish",
        [SMEM] + [VMEM] * 3 + [HBM] * 3,
        [HBM] * 3,
        [shaped(*k.shape) for k in kept],
        [pltpu.SemaphoreType.DMA((3,))],
        limit=8,
        alias={4: 0, 5: 1, 6: 2},
    )(core, *got, *kept)


def add_kernel(parts, *refs):
    total = refs[0][...].astype(F32)
    for ref in refs[1:parts]:
        total = total + ref[...].astype(F32)
    outs = refs[parts:]
    size = total.shape[0] // len(outs)
    for j, out in enumerate(outs):
        out[...] = total[j * size : (j + 1) * size].astype(BF)


def add(arrays, pieces=1):
    rows, width = arrays[0].shape
    return kernel_call(
        functools.partial(add_kernel, len(arrays)),
        "add",
        [VMEM] * len(arrays),
        [VMEM] * pieces,
        [shaped(rows // pieces, width)] * pieces,
    )(*arrays)


def combine_kernel(experts, local, cap, weighted, core, expert_pos, ids_ref, gw_ref, *refs):
    owners = experts // local
    mine, theirs, out = refs[:owners], refs[owners : 2 * owners], refs[-1]
    ids = ids_ref[...]
    gw = gw_ref[...]
    top, toks = ids.shape
    here = places(ids, experts)
    size = mine[0].shape[0]
    rows = lax.broadcasted_iota(jnp.int32, (size, toks), 0)
    total = jnp.zeros(out.shape, F32)
    for j in range(owners):
        for source, which in ((mine, 0), (theirs, 1)):
            expert = jnp.bitwise_xor(expert_pos[0], j) * local + jnp.bitwise_xor(core[0], which)
            mask = [
                (ids[k : k + 1, :] == expert) & (here[k] + which * cap == rows) for k in range(top)
            ]
            values = source[j][...]
            if weighted:
                w = sum(jnp.where(mask[k], gw[k : k + 1, :], 0.0) for k in range(top))
                high = w.astype(BF)
                low = (w - high.astype(F32)).astype(BF)
                total = total + dot(high, values, TN) + dot(low, values, TN)
            else:
                w = sum(jnp.where(mask[k], 1.0, 0.0) for k in range(top))
                total = total + dot(w.astype(BF), values, TN)
    out[...] = total.astype(BF)


def combine(core, expert_pos, ids, gw, mine, theirs, experts, local, cap, weighted):
    width = mine[0].shape[1]
    return kernel_call(
        functools.partial(combine_kernel, experts, local, cap, weighted),
        "combine",
        [SMEM, SMEM] + [VMEM] * (2 + 2 * len(mine)),
        VMEM,
        shaped(ids.shape[1], width),
    )(core, expert_pos, ids, gw, *mine, *theirs)


def body(tokens, expert_ids, gate_weights, w_gate, w_up, w_down, cotangent):
    owners = lax.axis_size("expert")
    devices = lax.axis_size("dp")
    toks, width = tokens.shape
    top = expert_ids.shape[1]
    local = w_gate.shape[0]
    experts = local * owners
    cap = max(2, 5 * toks * top // (4 * experts))
    bits = (devices // 2).bit_length() - 1
    assert local == 2 and devices == 2 << bits and owners & (owners - 1) == 0

    side = lax.axis_index("dp") % 2
    core = side.astype(jnp.int32).reshape(1)
    expert_pos = lax.axis_index("expert").astype(jnp.int32).reshape(1)
    ids, gw = expert_ids.T, gate_weights.T

    def to_pair(a):
        return lax.ppermute(a, "dp", [(i, i ^ 1) for i in range(devices)])

    def to_owner(a, j):
        return lax.ppermute(a, "expert", [(i, i ^ j) for i in range(owners)])

    def to_chip(a, s):
        def bit(i):
            return 2 << ((s + (i % 2) * (bits // 2)) % bits)

        return lax.ppermute(a, "dp", [(i, i ^ bit(i)) for i in range(devices)])

    def swap(messages):
        return [messages[0]] + [to_owner(messages[j], j) for j in range(1, owners)]

    def spread(messages):
        mine = swap(messages)
        theirs = [to_pair(m) for m in mine]
        parts = [pack(core, mine, theirs, cap)]
        for s in range(bits):
            parts = parts + [to_chip(a, s) for a in parts]
        return parts

    def collect(parts):
        held = []
        for s in reversed(range(1, bits)):
            half = len(parts) // 2
            arrived = [to_chip(a, s) for a in parts[half:]]
            held.append(arrived[0])
            parts = [parts[0]] + [add([parts[i], arrived[i]])[0] for i in range(1, half)]
        held = [parts[0]] + held + [to_chip(parts[1], 0)]
        mine = swap(add(held, owners))
        return mine, [to_pair(m) for m in mine]

    placed = place(expert_pos, ids, gw, tokens, cotangent, experts, local, cap)
    own = (w_gate, w_up, w_down)
    other = [to_pair(lax.dynamic_index_in_dim(w, 1 - side, 0, keepdims=False)) for w in own]
    xs = spread(placed[:owners])
    dys = spread(placed[owners:])
    ps, x, f1, f2, hid = forward(core, xs, own, other)
    qs, dy, dg, du = backward(core, dys, own, other, f1, f2)
    given, kept = grads(core, x, dy, dg, du, hid, local)
    mine, theirs = collect(ps)
    mixed = combine(core, expert_pos, ids, gw, mine, theirs, experts, local, cap, True)
    mine, theirs = collect(qs)
    grad_tokens = combine(core, expert_pos, ids, gw, mine, theirs, experts, local, cap, False)
    grad_gate, grad_up, grad_down = finish(core, [to_pair(g) for g in given], kept)
    return (mixed, grad_tokens, grad_gate, grad_up, grad_down)


def solution(mesh):
    rows = P(("dp", "expert"), None)
    wide, tall = P("expert", None, "dp"), P("expert", "dp", None)
    return jax.shard_map(
        body,
        mesh=mesh,
        in_specs=(rows, rows, rows, wide, wide, tall, rows),
        out_specs=(rows, rows, wide, wide, tall),
        check_vma=False,
    )
```

time: 249 us -> 116 us (0.47)
  waiting for transfers between devices: 129 us -> 42.6 us
  matrix products: 35.6 us -> 0 us
  starting transfers between devices: 8.31 us -> 43.9 us
  blocking collectives: 28.6 us -> 0 us
  Pallas kernels: 0 us -> 23.5 us
  local copies, waits for them, and re-layouts: 27.4 us -> 5.18 us
  between operations: 14.1 us -> 1.02 us
  other arithmetic: 4.97 us -> 0 us
    unnamed x4 -> x0, waiting for transfers between devices: 86.4 us -> none
    ppermute x0 -> x46, starting transfers between devices: none -> 43.9 us  [the longest x12 25.6 us: to_owner(): return lax.ppermute(a, 'expert', [(i, i ^ j) for i in range(owners)])]
    ppermute x0 -> x46, waiting for transfers between devices: none -> 42.6 us  [the longest x12 24.7 us: to_chip(): return lax.ppermute(a, 'dp', [(i, i ^ bit(i)) for i in range(devices)])]
    all_gather x2 -> x0, waiting for transfers between devices: 37.2 us -> none  [spread_one(): return lax.all_gather(arrived[None], 'dp', axis=0, tiled=True)]
    dot_general x11 -> x0, matrix products: 35.6 us -> none  [the longest x1 6.04 us: body(): jnp.einsum('pcjkd,jfd->pcjkf', grad_rows, w_down, preferred_element_type=...]
    all_to_all x2 -> x0, blocking collectives: 28.6 us -> none  [spread_one(): lax.all_to_all(buffer, 'expert', split_axis=0, concat_axis=0, tiled=True)]
    pallas_call x0 -> x13, Pallas kernels: none -> 23.5 us  [the longest x1 6.12 us: grads(): kernel_call(grads_kernel, 'grads', [SMEM] + [VMEM] * 5, [VMEM] * 3 + [HBM...]
    all_to_all x2 -> x0, starting transfers between devices: 8.19 us -> none  [collect(): lax.all_to_all(summed, 'expert', split_axis=1, concat_axis=1, tiled=True)]
  transfers between devices with their start and end apart: 5 -> 46, of which waited for: 5 -> 19; matrix products, arithmetic and copies ran while one was open for 13% -> 1% of each run, Pallas kernels for 0% -> 18%
where the time goes in v2:
time: 116 us
  starting transfers between devices  43.9 us (38%)
  waiting for transfers between devices  42.6 us (37%)
  Pallas kernels  23.5 us (20%)
  local copies, waits for them, and re-layouts  5.18 us (4%)
    ppermute x12, starting transfers between devices, to_owner(): return lax.ppermute(a, 'expert', [(i, i ^ j) for i in range(owners)])  25.6 us
    ppermute x12, waiting for transfers between devices, to_chip(): return lax.ppermute(a, 'dp', [(i, i ^ bit(i)) for i in range(devices)])  24.7 us
    ppermute x12, waiting for transfers between devices, to_owner(): return lax.ppermute(a, 'expert', [(i, i ^ j) for i in range(owners)])  13.6 us
    ppermute x12, starting transfers between devices, to_chip(): return lax.ppermute(a, 'dp', [(i, i ^ bit(i)) for i in range(devices)])  13.5 us
    pallas_call x1, Pallas kernels, grads(): kernel_call(grads_kernel, 'grads', [SMEM] + [VMEM] * 5, [VMEM] * 3 + [HBM...  6.12 us
    pallas_call x1, Pallas kernels, forward(): kernel_call(functools.partial(forward_kernel, chips), 'forward', [SMEM] +...  5.54 us
    pallas_call x1, Pallas kernels, backward(): kernel_call(functools.partial(backward_kernel, chips), 'backward', [SMEM]...  5.18 us
    ppermute x22, starting transfers between devices, to_pair(): return lax.ppermute(a, 'dp', [(i, i ^ 1) for i in range(devices)])  4.8 us
  transfers between devices with their start and end apart: 46, of which 19 were waited for; matrix products, arithmetic and copies ran while one was open for 1% of the time, Pallas kernels for 18%

profile of v2, /device:TPU:0, one launch (start us, length us, event | category | flops | bytes accessed | tf_op | source)
XLA Modules:
  0.0 116.1 jit_solution(5925335296145567149)
XLA Ops:
  0.7 1.0 copy-done.3
  1.7 0.9 copy-done.4
  2.6 0.7 copy-done.5
  3.3 0.7 copy-done.7
  4.0 1.1 place.1
  5.1 3.1 %collective-permute-start = (bf16[40,1024]{1,0:T(8,128)(2,1)S(1)}, bf16[40,1024]{1,0:T(8,128)(2,1)S(1)}, u32[]{:S(2)}, u32[]{:S(2)}) collective-permute-start(bf16[40,1024]{1,0:T(8,128)(2,1)S(1)} %get-tuple-element.46), channel_id=1, source_target_pairs={{0,1},{1,0},{2,3},{3,2},{4,5},{5,4},{6,7},{7,6},{8,9},{9,8},{10,11... | collective-permute-start | bytes 245768 | tf_op jit(solution)/shard_map/ppermute | solution.py:407
  8.1 2.6 %collective-permute-start.1 = (bf16[40,1024]{1,0:T(8,128)(2,1)S(1)}, bf16[40,1024]{1,0:T(8,128)(2,1)S(1)}, u32[]{:S(2)}, u32[]{:S(2)}) collective-permute-start(bf16[40,1024]{1,0:T(8,128)(2,1)S(1)} %get-tuple-element.47), channel_id=1, source_target_pairs={{0,2},{1,3},{2,0},{3,1},{4,6},{5,7},{6,4},{7,5},{8,10},{9,11},{10,... | collective-permute-start | bytes 245768 | tf_op jit(solution)/shard_map/ppermute | solution.py:407
  10.7 0.9 collective-permute-start.23
  11.6 3.5 %collective-permute-start.24 = (bf16[40,1024]{1,0:T(8,128)(2,1)S(1)}, bf16[40,1024]{1,0:T(8,128)(2,1)S(1)}, u32[]{:S(2)}, u32[]{:S(2)}) collective-permute-start(bf16[40,1024]{1,0:T(8,128)(2,1)S(1)} %get-tuple-element.59), channel_id=1, source_target_pairs={{0,2},{1,3},{2,0},{3,1},{4,6},{5,7},{6,4},{7,5},{8,10},{9,11},{10,... | collective-permute-start | bytes 245768 | tf_op jit(solution)/shard_map/ppermute | solution.py:407
  15.1 1.4 %dynamic-slice_bitcast_fusion.2 = bf16[1024,512]{1,0:T(8,128)(2,1)S(1)} fusion(bf16[2,1024,512]{2,1,0:T(8,128)(2,1)} %refs_4_.3, s32[]{:T(128)S(6)} %select_n.15), kind=kLoop, calls=%fused_computation.2 | loop fusion | bytes 2097156 | tf_op jit(solution)/shard_map/jit(dynamic_index_in_dim)/squeeze | solution.py:439
  16.8 0.3 copy-done.2
  17.1 1.2 %collective-permute-done.1.refs_2_ = bf16[40,1024]{1,0:T(8,128)(2,1)S(1)} collective-permute-done((bf16[40,1024]{1,0:T(8,128)(2,1)S(1)}, bf16[40,1024]{1,0:T(8,128)(2,1)S(1)}, u32[]{:S(2)}, u32[]{:S(2)}) %collective-permute-start.1) | collective-permute-done | bytes 81952 | tf_op jit(solution)/shard_map/ppermute | solution.py:407
  18.3 0.5 collective-permute-start.11
  18.9 5.5 %collective-permute-done.24.refs_2_ = bf16[40,1024]{1,0:T(8,128)(2,1)S(1)} collective-permute-done((bf16[40,1024]{1,0:T(8,128)(2,1)S(1)}, bf16[40,1024]{1,0:T(8,128)(2,1)S(1)}, u32[]{:S(2)}, u32[]{:S(2)}) %collective-permute-start.24) | collective-permute-done | bytes 81952 | tf_op jit(solution)/shard_map/ppermute | solution.py:407
  24.4 0.5 collective-permute-start.26
  24.9 0.8 collective-permute-done.3.refs_4_
  25.8 0.4 collective-permute-start.27
  26.2 0.8 collective-permute-done.4.refs_5_
  27.1 0.4 collective-permute-start.29
  27.4 0.8 collective-permute-done.28.refs_6_
  28.4 0.4 collective-permute-start.6
  28.7 0.3 pack.3.refs_0_
  29.1 0.4 collective-permute-done.5.refs_6_
  29.5 1.5 %collective-permute-start.30 = (bf16[160,1024]{1,0:T(8,128)(2,1)S(1)}, bf16[160,1024]{1,0:T(8,128)(2,1)S(1)}, u32[]{:S(2)}, u32[]{:S(2)}) collective-permute-start(bf16[160,1024]{1,0:T(8,128)(2,1)S(1)} %pack.3.refs_0_), channel_id=1, source_target_pairs={{0,8},{4,20},{8,0},{12,28},{16,24},{20,4},{24,16},{28,12},{1,9},{5... | collective-permute-start | bytes 983048 | tf_op jit(solution)/shard_map/ppermute | solution.py:413
  31.0 0.3 pack.2.refs_0_
  31.3 0.6 collective-permute-start.7
  31.9 4.6 %collective-permute-done.30.refs_1_ = bf16[160,1024]{1,0:T(8,128)(2,1)S(1)} collective-permute-done((bf16[160,1024]{1,0:T(8,128)(2,1)S(1)}, bf16[160,1024]{1,0:T(8,128)(2,1)S(1)}, u32[]{:S(2)}, u32[]{:S(2)}) %collective-permute-start.30) | collective-permute-done | bytes 327712 | tf_op jit(solution)/shard_map/ppermute | solution.py:413
  36.6 1.5 %collective-permute-start.8 = (bf16[160,1024]{1,0:T(8,128)(2,1)S(1)}, bf16[160,1024]{1,0:T(8,128)(2,1)S(1)}, u32[]{:S(2)}, u32[]{:S(2)}) collective-permute-start(bf16[160,1024]{1,0:T(8,128)(2,1)S(1)} %pack.2.refs_0_), channel_id=1, source_target_pairs={{0,16},{4,12},{8,24},{12,4},{16,0},{20,28},{24,8},{28,20},{1,17},{... | collective-permute-start | bytes 983048 | tf_op jit(solution)/shard_map/ppermute | solution.py:413
  38.1 3.5 %collective-permute-done.7.refs_1_ = bf16[160,1024]{1,0:T(8,128)(2,1)S(1)} collective-permute-done((bf16[160,1024]{1,0:T(8,128)(2,1)S(1)}, bf16[160,1024]{1,0:T(8,128)(2,1)S(1)}, u32[]{:S(2)}, u32[]{:S(2)}) %collective-permute-start.7) | collective-permute-done | bytes 327712 | tf_op jit(solution)/shard_map/ppermute | solution.py:413
  41.6 1.5 %collective-permute-start.9 = (bf16[160,1024]{1,0:T(8,128)(2,1)S(1)}, bf16[160,1024]{1,0:T(8,128)(2,1)S(1)}, u32[]{:S(2)}, u32[]{:S(2)}) collective-permute-start(bf16[160,1024]{1,0:T(8,128)(2,1)S(1)} %collective-permute-done.7.refs_1_), channel_id=1, source_target_pairs={{0,16},{4,12},{8,24},{12,4},{16,0},{20,28},{24,8},{28,20},{1,17},{... | collective-permute-start | bytes 983048 | tf_op jit(solution)/shard_map/ppermute | solution.py:413
  43.1 0.5 collective-permute-done.8.refs_2_
  43.6 1.5 %collective-permute-start.31 = (bf16[160,1024]{1,0:T(8,128)(2,1)S(1)}, bf16[160,1024]{1,0:T(8,128)(2,1)S(1)}, u32[]{:S(2)}, u32[]{:S(2)}) collective-permute-start(bf16[160,1024]{1,0:T(8,128)(2,1)S(1)} %pack.3.refs_0_), channel_id=1, source_target_pairs={{0,16},{4,12},{8,24},{12,4},{16,0},{20,28},{24,8},{28,20},{1,17},{... | collective-permute-start | bytes 983048 | tf_op jit(solution)/shard_map/ppermute | solution.py:413
  45.2 3.5 %collective-permute-done.9.refs_3_ = bf16[160,1024]{1,0:T(8,128)(2,1)S(1)} collective-permute-done((bf16[160,1024]{1,0:T(8,128)(2,1)S(1)}, bf16[160,1024]{1,0:T(8,128)(2,1)S(1)}, u32[]{:S(2)}, u32[]{:S(2)}) %collective-permute-start.9) | collective-permute-done | bytes 327712 | tf_op jit(solution)/shard_map/ppermute | solution.py:413
  48.7 1.5 %collective-permute-start.32 = (bf16[160,1024]{1,0:T(8,128)(2,1)S(1)}, bf16[160,1024]{1,0:T(8,128)(2,1)S(1)}, u32[]{:S(2)}, u32[]{:S(2)}) collective-permute-start(bf16[160,1024]{1,0:T(8,128)(2,1)S(1)} %collective-permute-done.30.refs_1_), channel_id=1, source_target_pairs={{0,16},{4,12},{8,24},{12,4},{16,0},{20,28},{24,8},{28,20},{1,17},{... | collective-permute-start | bytes 983048 | tf_op jit(solution)/shard_map/ppermute | solution.py:413
  50.2 5.5 %forward.1 = (bf16[160,1024]{1,0:T(8,128)(2,1)S(1)}, bf16[160,1024]{1,0:T(8,128)(2,1)S(1)}, bf16[160,1024]{1,0:T(8,128)(2,1)S(1)}, bf16[160,1024]{1,0:T(8,128)(2...) custom-call(s32[1]{0:T(128)} %bitcast.core, ...), custom_call_target="tpu_custom_call" | custom-call | flops 4026531840 | tf_op jit(solution)/shard_map/forward/pallas_call | solution.py:192
  55.8 0.6 collective-permute-start.13
  56.3 1.5 %collective-permute-start.14 = (bf16[160,1024]{1,0:T(8,128)(2,1)S(1)}, bf16[160,1024]{1,0:T(8,128)(2,1)S(1)}, u32[]{:S(2)}, u32[]{:S(2)}) collective-permute-start(bf16[160,1024]{1,0:T(8,128)(2,1)S(1)} %get-tuple-element.52), channel_id=1, source_target_pairs={{0,16},{4,12},{8,24},{12,4},{16,0},{20,28},{24,8},{28,20},{1,17},{... | collective-permute-start | bytes 983048 | tf_op jit(solution)/shard_map/ppermute | solution.py:413
  57.9 5.2 %backward.1 = (bf16[160,1024]{1,0:T(8,128)(2,1)S(1)}, bf16[160,1024]{1,0:T(8,128)(2,1)S(1)}, bf16[160,1024]{1,0:T(8,128)(2,1)S(1)}, bf16[160,1024]{1,0:T(8,128)(...) custom-call(s32[1]{0:T(128)} %bitcast.core, ...), custom_call_target="tpu_custom_call" | custom-call | flops 4026531840 | tf_op jit(solution)/shard_map/backward/pallas_call | solution.py:245
  63.1 0.6 collective-permute-start.34
  63.6 2.8 %collective-permute-done.14.refs_1_ = bf16[160,1024]{1,0:T(8,128)(2,1)S(1)} collective-permute-done((bf16[160,1024]{1,0:T(8,128)(2,1)S(1)}, bf16[160,1024]{1,0:T(8,128)(2,1)S(1)}, u32[]{:S(2)}, u32[]{:S(2)}) %collective-permute-start.14) | collective-permute-done | bytes 327712 | tf_op jit(solution)/shard_map/ppermute | solution.py:413
  66.5 2.3 %collective-permute-start.15 = (bf16[160,1024]{1,0:T(8,128)(2,1)S(1)}, bf16[160,1024]{1,0:T(8,128)(2,1)S(1)}, u32[]{:S(2)}, u32[]{:S(2)}) collective-permute-start(bf16[160,1024]{1,0:T(8,128)(2,1)S(1)} %add.18), channel_id=1, source_target_pairs={{0,8},{4,20},{8,0},{12,28},{16,24},{20,4},{24,16},{28,12},{1,9},{5... | collective-permute-start | bytes 983048 | tf_op jit(solution)/shard_map/ppermute | solution.py:413
  68.9 6.1 %grads.1 = (bf16[1024,512]{1,0:T(8,128)(2,1)S(1)}, bf16[1024,512]{1,0:T(8,128)(2,1)S(1)}, bf16[512,1024]{1,0:T(8,128)(2,1)S(1)}, bf16[2,1024,512]{2,1,0:T(8,128)...) custom-call(s32[1]{0:T(128)} %bitcast.core, bf16[640,1024]{1,0:T(8,128)(2,1)S(1)} %get-tuple-element.71.x, ...), custom_call_target="tpu_custom_call" | custom-call | flops 4026531840 | tf_op jit(solution)/shard_map/grads/pallas_call | solution.py:289
  75.1 0.5 collective-permute-start.44
  75.8 0.3 collective-permute-start.35
  76.2 9.7 %collective-permute-done.33.refs_1_ = bf16[160,1024]{1,0:T(8,128)(2,1)S(1)} collective-permute-done((bf16[160,1024]{1,0:T(8,128)(2,1)S(1)}, bf16[160,1024]{1,0:T(8,128)(2,1)S(1)}, u32[]{:S(2)}, u32[]{:S(2)}) %collective-permute-start.33) | collective-permute-done | bytes 327712 | tf_op jit(solution)/shard_map/ppermute | solution.py:413
  85.9 1.2 %collective-permute-start.16 = (bf16[40,1024]{1,0:T(8,128)(2,1)S(1)}, bf16[40,1024]{1,0:T(8,128)(2,1)S(1)}, u32[]{:S(2)}, u32[]{:S(2)}) collective-permute-start(bf16[40,1024]{1,0:T(8,128)(2,1)S(1)} %get-tuple-element.54), channel_id=1, source_target_pairs={{0,1},{1,0},{2,3},{3,2},{4,5},{5,4},{6,7},{7,6},{8,9},{9,8},{10,11... | collective-permute-start | bytes 245768 | tf_op jit(solution)/shard_map/ppermute | solution.py:407
  87.1 3.1 %collective-permute-start.17 = (bf16[40,1024]{1,0:T(8,128)(2,1)S(1)}, bf16[40,1024]{1,0:T(8,128)(2,1)S(1)}, u32[]{:S(2)}, u32[]{:S(2)}) collective-permute-start(bf16[40,1024]{1,0:T(8,128)(2,1)S(1)} %get-tuple-element.55), channel_id=1, source_target_pairs={{0,2},{1,3},{2,0},{3,1},{4,6},{5,7},{6,4},{7,5},{8,10},{9,11},{10,... | collective-permute-start | bytes 245768 | tf_op jit(solution)/shard_map/ppermute | solution.py:407
  90.2 1.0 collective-permute-done.16.refs_1_
  91.2 3.4 %collective-permute-start.18 = (bf16[40,1024]{1,0:T(8,128)(2,1)S(1)}, bf16[40,1024]{1,0:T(8,128)(2,1)S(1)}, u32[]{:S(2)}, u32[]{:S(2)}) collective-permute-start(bf16[40,1024]{1,0:T(8,128)(2,1)S(1)} %get-tuple-element.56), channel_id=1, source_target_pairs={{0,3},{1,2},{2,1},{3,0},{4,7},{5,6},{6,5},{7,4},{8,11},{9,10},{10,... | collective-permute-start | bytes 245768 | tf_op jit(solution)/shard_map/ppermute | solution.py:407
  94.6 0.7 collective-permute-done.17.refs_2_
  95.4 2.0 %collective-permute-done.18.refs_3_ = bf16[40,1024]{1,0:T(8,128)(2,1)S(1)} collective-permute-done((bf16[40,1024]{1,0:T(8,128)(2,1)S(1)}, bf16[40,1024]{1,0:T(8,128)(2,1)S(1)}, u32[]{:S(2)}, u32[]{:S(2)}) %collective-permute-start.18) | collective-permute-done | bytes 81952 | tf_op jit(solution)/shard_map/ppermute | solution.py:407
  97.5 4.0 %collective-permute-start.37 = (bf16[40,1024]{1,0:T(8,128)(2,1)S(1)}, bf16[40,1024]{1,0:T(8,128)(2,1)S(1)}, u32[]{:S(2)}, u32[]{:S(2)}) collective-permute-start(bf16[40,1024]{1,0:T(8,128)(2,1)S(1)} %get-tuple-element.69), channel_id=1, source_target_pairs={{0,2},{1,3},{2,0},{3,1},{4,6},{5,7},{6,4},{7,5},{8,10},{9,11},{10,... | collective-permute-start | bytes 245768 | tf_op jit(solution)/shard_map/ppermute | solution.py:407
  101.4 0.7 collective-permute-done.36.refs_1_
  102.1 3.7 %collective-permute-start.38 = (bf16[40,1024]{1,0:T(8,128)(2,1)S(1)}, bf16[40,1024]{1,0:T(8,128)(2,1)S(1)}, u32[]{:S(2)}, u32[]{:S(2)}) collective-permute-start(bf16[40,1024]{1,0:T(8,128)(2,1)S(1)} %get-tuple-element.70), channel_id=1, source_target_pairs={{0,3},{1,2},{2,1},{3,0},{4,7},{5,6},{6,5},{7,4},{8,11},{9,10},{10,... | collective-permute-start | bytes 245768 | tf_op jit(solution)/shard_map/ppermute | solution.py:407
  105.8 2.5 %collective-permute-done.38.refs_3_ = bf16[40,1024]{1,0:T(8,128)(2,1)S(1)} collective-permute-done((bf16[40,1024]{1,0:T(8,128)(2,1)S(1)}, bf16[40,1024]{1,0:T(8,128)(2,1)S(1)}, u32[]{:S(2)}, u32[]{:S(2)}) %collective-permute-start.38) | collective-permute-done | bytes 81952 | tf_op jit(solution)/shard_map/ppermute | solution.py:407
  108.4 0.5 collective-permute-start.21
  108.9 0.8 collective-permute-done.20.refs_5_
  109.8 0.4 collective-permute-start.40
  110.2 0.8 collective-permute-done.22.refs_7_
  110.9 0.2 collective-permute-start.41
  111.1 0.4 collective-permute-start.42
  111.4 1.5 %combine.2 = bf16[64,1024]{1,0:T(8,128)(2,1)} custom-call(s32[1]{0:T(128)} %bitcast.core, s32[1]{0:T(128)} %bitcast.1.expert_pos, s32[2,64]{1,0:T(2,128)S(1)} %bitcast.11, f32[2,64]{1,0:T(2,128)S(1)} %bitcast.14, bf16[40,1024]{1,0:T(8,128)(2,1)S(1)} %get-tuple-element.53.refs_0_, bf16[40,1024]{1,0:T(8,128)(2,1)S(1)} %collective-permute-done.16.refs_1_, ...), custom_call_target="tpu_custom_call" | custom-call | tf_op jit(solution)/shard_map/combine/pallas_call | solution.py:378
  113.0 1.3 %combine.3 = bf16[64,1024]{1,0:T(8,128)(2,1)} custom-call(s32[1]{0:T(128)} %bitcast.core, s32[1]{0:T(128)} %bitcast.1.expert_pos, s32[2,64]{1,0:T(2,128)S(1)} %bitcast.12, f32[2,64]{1,0:T(2,128)S(1)} %bitcast.15, bf16[40,1024]{1,0:T(8,128)(2,1)S(1)} %get-tuple-element.67.refs_0_, bf16[40,1024]{1,0:T(8,128)(2,1)S(1)} %collective-permute-done.36.refs_1_, ...), custom_call_target="tpu_custom_call" | custom-call | tf_op jit(solution)/shard_map/combine/pallas_call | solution.py:378
  114.3 1.7 %finish.1 = (bf16[2,1024,512]{2,1,0:T(8,128)(2,1)}, bf16[2,1024,512]{2,1,0:T(8,128)(2,1)}, bf16[2,512,1024]{2,1,0:T(8,128)(2,1)}) custom-call(s32[1]{0:T(128)} %bitcast.core, bf16[1024,512]{1,0:T(8,128)(2,1)S(1)} %collective-permute-done.43.refs_0_, ...), custom_call_target="tpu_custom_call", output_to_operand_aliasing={{0}: (4, {}), {1}: (5, {}), {2}: (6, {})} | custom-call | tf_op jit(solution)/shard_map/finish/pallas_call | solution.py:315
  (62 shorter events, 1.6 us)
Async XLA Ops:
  0.6 15.9 %copy-start.1 = (bf16[2,1024,512]{2,1,0:T(8,128)(2,1)S(1)}, bf16[2,1024,512]{2,1,0:T(8,128)(2,1)}, u32[]{:S(2)}) copy-start(bf16[2,1024,512]{2,1,0:T(8,128)(2,1)} %refs_5_.3) | copy-start | bytes 6291460
  0.6 1.1 copy-start.3
  1.7 0.9 copy-start.4
  2.6 0.7 copy-start.5
  3.3 0.7 copy-start.7
  5.1 11.6 %collective-permute-start = (bf16[40,1024]{1,0:T(8,128)(2,1)S(1)}, bf16[40,1024]{1,0:T(8,128)(2,1)S(1)}, u32[]{:S(2)}, u32[]{:S(2)}) collective-permute-start(bf16[40,1024]{1,0:T(8,128)(2,1)S(1)} %get-tuple-element.46), channel_id=1, source_target_pairs={{0,1},{1,0},{2,3},{3,2},{4,5},{5,4},{6,7},{7,6},{8,9},{9,8},{10,11... | collective-permute-start | bytes 245768 | tf_op jit(solution)/shard_map/ppermute | solution.py:407
  8.1 10.2 %collective-permute-start.1 = (bf16[40,1024]{1,0:T(8,128)(2,1)S(1)}, bf16[40,1024]{1,0:T(8,128)(2,1)S(1)}, u32[]{:S(2)}, u32[]{:S(2)}) collective-permute-start(bf16[40,1024]{1,0:T(8,128)(2,1)S(1)} %get-tuple-element.47), channel_id=1, source_target_pairs={{0,2},{1,3},{2,0},{3,1},{4,6},{5,7},{6,4},{7,5},{8,10},{9,11},{10,... | collective-permute-start | bytes 245768 | tf_op jit(solution)/shard_map/ppermute | solution.py:407
  10.7 7.6 %collective-permute-start.2 = (bf16[40,1024]{1,0:T(8,128)(2,1)S(1)}, bf16[40,1024]{1,0:T(8,128)(2,1)S(1)}, u32[]{:S(2)}, u32[]{:S(2)}) collective-permute-start(bf16[40,1024]{1,0:T(8,128)(2,1)S(1)} %get-tuple-element.48), channel_id=1, source_target_pairs={{0,3},{1,2},{2,1},{3,0},{4,7},{5,6},{6,5},{7,4},{8,11},{9,10},{10,... | collective-permute-start | bytes 245768 | tf_op jit(solution)/shard_map/ppermute | solution.py:407
  10.7 8.1 %collective-permute-start.23 = (bf16[40,1024]{1,0:T(8,128)(2,1)S(1)}, bf16[40,1024]{1,0:T(8,128)(2,1)S(1)}, u32[]{:S(2)}, u32[]{:S(2)}) collective-permute-start(bf16[40,1024]{1,0:T(8,128)(2,1)S(1)} %get-tuple-element.58), channel_id=1, source_target_pairs={{0,1},{1,0},{2,3},{3,2},{4,5},{5,4},{6,7},{7,6},{8,9},{9,8},{10,11... | collective-permute-start | bytes 245768 | tf_op jit(solution)/shard_map/ppermute | solution.py:407
  11.6 12.7 %collective-permute-start.24 = (bf16[40,1024]{1,0:T(8,128)(2,1)S(1)}, bf16[40,1024]{1,0:T(8,128)(2,1)S(1)}, u32[]{:S(2)}, u32[]{:S(2)}) collective-permute-start(bf16[40,1024]{1,0:T(8,128)(2,1)S(1)} %get-tuple-element.59), channel_id=1, source_target_pairs={{0,2},{1,3},{2,0},{3,1},{4,6},{5,7},{6,4},{7,5},{8,10},{9,11},{10,... | collective-permute-start | bytes 245768 | tf_op jit(solution)/shard_map/ppermute | solution.py:407
  15.1 1.9 %copy-start.2 = (bf16[2,512,1024]{2,1,0:T(8,128)(2,1)S(1)}, bf16[2,512,1024]{2,1,0:T(8,128)(2,1)}, u32[]{:S(2)}) copy-start(bf16[2,512,1024]{2,1,0:T(8,128)(2,1)} %refs_6_.3) | copy-start | bytes 6291460
  16.7 33.6 %copy-start = (bf16[2,1024,512]{2,1,0:T(8,128)(2,1)S(1)}, bf16[2,1024,512]{2,1,0:T(8,128)(2,1)}, u32[]{:S(2)}) copy-start(bf16[2,1024,512]{2,1,0:T(8,128)(2,1)} %refs_4_.3) | copy-start | bytes 6291460
  16.7 7.7 %collective-permute-start.25 = (bf16[40,1024]{1,0:T(8,128)(2,1)S(1)}, bf16[40,1024]{1,0:T(8,128)(2,1)S(1)}, u32[]{:S(2)}, u32[]{:S(2)}) collective-permute-start(bf16[40,1024]{1,0:T(8,128)(2,1)S(1)} %get-tuple-element.60), channel_id=1, source_target_pairs={{0,3},{1,2},{2,1},{3,0},{4,7},{5,6},{6,5},{7,4},{8,11},{9,10},{10,... | collective-permute-start | bytes 245768 | tf_op jit(solution)/shard_map/ppermute | solution.py:407
  18.3 31.9 %collective-permute-start.12 = (bf16[512,1024]{1,0:T(8,128)(2,1)S(1)}, bf16[512,1024]{1,0:T(8,128)(2,1)S(1)}, u32[]{:S(2)}, u32[]{:S(2)}) collective-permute-start(bf16[512,1024]{1,0:T(8,128)(2,1)S(1)} %dynamic-slice_bitcast_fusion), channel_id=1, source_target_pairs={{0,4},{4,0},{8,12},{12,8},{16,20},{20,16},{24,28},{28,24},{1,5},{5... | collective-permute-start | bytes 3145736 | tf_op jit(solution)/shard_map/ppermute | solution.py:404
  18.3 31.9 %collective-permute-start.11 = (bf16[1024,512]{1,0:T(8,128)(2,1)S(1)}, bf16[1024,512]{1,0:T(8,128)(2,1)S(1)}, u32[]{:S(2)}, u32[]{:S(2)}) collective-permute-start(bf16[1024,512]{1,0:T(8,128)(2,1)S(1)} %dynamic-slice_bitcast_fusion.1), channel_id=1, source_target_pairs={{0,4},{4,0},{8,12},{12,8},{16,20},{20,16},{24,28},{28,24},{1,5},{5... | collective-permute-start | bytes 3145736 | tf_op jit(solution)/shard_map/ppermute | solution.py:404
  18.8 31.4 %collective-permute-start.10 = (bf16[1024,512]{1,0:T(8,128)(2,1)S(1)}, bf16[1024,512]{1,0:T(8,128)(2,1)S(1)}, u32[]{:S(2)}, u32[]{:S(2)}) collective-permute-start(bf16[1024,512]{1,0:T(8,128)(2,1)S(1)} %dynamic-slice_bitcast_fusion.2), channel_id=1, source_target_pairs={{0,4},{4,0},{8,12},{12,8},{16,20},{20,16},{24,28},{28,24},{1,5},{5... | collective-permute-start | bytes 3145736 | tf_op jit(solution)/shard_map/ppermute | solution.py:404
  24.4 1.3 %collective-permute-start.3 = (bf16[40,1024]{1,0:T(8,128)(2,1)S(1)}, bf16[40,1024]{1,0:T(8,128)(2,1)S(1)}, u32[]{:S(2)}, u32[]{:S(2)}) collective-permute-start(bf16[40,1024]{1,0:T(8,128)(2,1)S(1)} %get-tuple-element.45.refs_0_), channel_id=1, source_target_pairs={{0,4},{4,0},{8,12},{12,8},{16,20},{20,16},{24,28},{28,24},{1,5},{5... | collective-permute-start | bytes 245768 | tf_op jit(solution)/shard_map/ppermute | solution.py:404
  24.4 1.4 %collective-permute-start.26 = (bf16[40,1024]{1,0:T(8,128)(2,1)S(1)}, bf16[40,1024]{1,0:T(8,128)(2,1)S(1)}, u32[]{:S(2)}, u32[]{:S(2)}) collective-permute-start(bf16[40,1024]{1,0:T(8,128)(2,1)S(1)} %get-tuple-element.57.refs_0_), channel_id=1, source_target_pairs={{0,4},{4,0},{8,12},{12,8},{16,20},{20,16},{24,28},{28,24},{1,5},{5... | collective-permute-start | bytes 245768 | tf_op jit(solution)/shard_map/ppermute | solution.py:404
  25.6 1.3 %collective-permute-start.4 = (bf16[40,1024]{1,0:T(8,128)(2,1)S(1)}, bf16[40,1024]{1,0:T(8,128)(2,1)S(1)}, u32[]{:S(2)}, u32[]{:S(2)}) collective-permute-start(bf16[40,1024]{1,0:T(8,128)(2,1)S(1)} %collective-permute-done.refs_1_), channel_id=1, source_target_pairs={{0,4},{4,0},{8,12},{12,8},{16,20},{20,16},{24,28},{28,24},{1,5},{5... | collective-permute-start | bytes 245768 | tf_op jit(solution)/shard_map/ppermute | solution.py:404
  25.8 1.3 %collective-permute-start.27 = (bf16[40,1024]{1,0:T(8,128)(2,1)S(1)}, bf16[40,1024]{1,0:T(8,128)(2,1)S(1)}, u32[]{:S(2)}, u32[]{:S(2)}) collective-permute-start(bf16[40,1024]{1,0:T(8,128)(2,1)S(1)} %collective-permute-done.23.refs_1_), channel_id=1, source_target_pairs={{0,4},{4,0},{8,12},{12,8},{16,20},{20,16},{24,28},{28,24},{1,5},{5... | collective-permute-start | bytes 245768 | tf_op jit(solution)/shard_map/ppermute | solution.py:404
  26.9 1.3 %collective-permute-start.28 = (bf16[40,1024]{1,0:T(8,128)(2,1)S(1)}, bf16[40,1024]{1,0:T(8,128)(2,1)S(1)}, u32[]{:S(2)}, u32[]{:S(2)}) collective-permute-start(bf16[40,1024]{1,0:T(8,128)(2,1)S(1)} %collective-permute-done.24.refs_2_), channel_id=1, source_target_pairs={{0,4},{4,0},{8,12},{12,8},{16,20},{20,16},{24,28},{28,24},{1,5},{5... | collective-permute-start | bytes 245768 | tf_op jit(solution)/shard_map/ppermute | solution.py:404
  27.1 1.3 %collective-permute-start.29 = (bf16[40,1024]{1,0:T(8,128)(2,1)S(1)}, bf16[40,1024]{1,0:T(8,128)(2,1)S(1)}, u32[]{:S(2)}, u32[]{:S(2)}) collective-permute-start(bf16[40,1024]{1,0:T(8,128)(2,1)S(1)} %collective-permute-done.25.refs_3_), channel_id=1, source_target_pairs={{0,4},{4,0},{8,12},{12,8},{16,20},{20,16},{24,28},{28,24},{1,5},{5... | collective-permute-start | bytes 245768 | tf_op jit(solution)/shard_map/ppermute | solution.py:404
  28.2 1.3 %collective-permute-start.5 = (bf16[40,1024]{1,0:T(8,128)(2,1)S(1)}, bf16[40,1024]{1,0:T(8,128)(2,1)S(1)}, u32[]{:S(2)}, u32[]{:S(2)}) collective-permute-start(bf16[40,1024]{1,0:T(8,128)(2,1)S(1)} %collective-permute-done.1.refs_2_), channel_id=1, source_target_pairs={{0,4},{4,0},{8,12},{12,8},{16,20},{20,16},{24,28},{28,24},{1,5},{5... | collective-permute-start | bytes 245768 | tf_op jit(solution)/shard_map/ppermute | solution.py:404
  28.4 2.6 %collective-permute-start.6 = (bf16[40,1024]{1,0:T(8,128)(2,1)S(1)}, bf16[40,1024]{1,0:T(8,128)(2,1)S(1)}, u32[]{:S(2)}, u32[]{:S(2)}) collective-permute-start(bf16[40,1024]{1,0:T(8,128)(2,1)S(1)} %collective-permute-done.2.refs_3_), channel_id=1, source_target_pairs={{0,4},{4,0},{8,12},{12,8},{16,20},{20,16},{24,28},{28,24},{1,5},{5... | collective-permute-start | bytes 245768 | tf_op jit(solution)/shard_map/ppermute | solution.py:404
  29.5 7.1 %collective-permute-start.30 = (bf16[160,1024]{1,0:T(8,128)(2,1)S(1)}, bf16[160,1024]{1,0:T(8,128)(2,1)S(1)}, u32[]{:S(2)}, u32[]{:S(2)}) collective-permute-start(bf16[160,1024]{1,0:T(8,128)(2,1)S(1)} %pack.3.refs_0_), channel_id=1, source_target_pairs={{0,8},{4,20},{8,0},{12,28},{16,24},{20,4},{24,16},{28,12},{1,9},{5... | collective-permute-start | bytes 983048 | tf_op jit(solution)/shard_map/ppermute | solution.py:413
  31.3 10.3 %collective-permute-start.7 = (bf16[160,1024]{1,0:T(8,128)(2,1)S(1)}, bf16[160,1024]{1,0:T(8,128)(2,1)S(1)}, u32[]{:S(2)}, u32[]{:S(2)}) collective-permute-start(bf16[160,1024]{1,0:T(8,128)(2,1)S(1)} %pack.2.refs_0_), channel_id=1, source_target_pairs={{0,8},{4,20},{8,0},{12,28},{16,24},{20,4},{24,16},{28,12},{1,9},{5... | collective-permute-start | bytes 983048 | tf_op jit(solution)/shard_map/ppermute | solution.py:413
  36.6 7.1 %collective-permute-start.8 = (bf16[160,1024]{1,0:T(8,128)(2,1)S(1)}, bf16[160,1024]{1,0:T(8,128)(2,1)S(1)}, u32[]{:S(2)}, u32[]{:S(2)}) collective-permute-start(bf16[160,1024]{1,0:T(8,128)(2,1)S(1)} %pack.2.refs_0_), channel_id=1, source_target_pairs={{0,16},{4,12},{8,24},{12,4},{16,0},{20,28},{24,8},{28,20},{1,17},{... | collective-permute-start | bytes 983048 | tf_op jit(solution)/shard_map/ppermute | solution.py:413
  41.6 7.1 %collective-permute-start.9 = (bf16[160,1024]{1,0:T(8,128)(2,1)S(1)}, bf16[160,1024]{1,0:T(8,128)(2,1)S(1)}, u32[]{:S(2)}, u32[]{:S(2)}) collective-permute-start(bf16[160,1024]{1,0:T(8,128)(2,1)S(1)} %collective-permute-done.7.refs_1_), channel_id=1, source_target_pairs={{0,16},{4,12},{8,24},{12,4},{16,0},{20,28},{24,8},{28,20},{1,17},{... | collective-permute-start | bytes 983048 | tf_op jit(solution)/shard_map/ppermute | solution.py:413
  43.6 14.3 %collective-permute-start.31 = (bf16[160,1024]{1,0:T(8,128)(2,1)S(1)}, bf16[160,1024]{1,0:T(8,128)(2,1)S(1)}, u32[]{:S(2)}, u32[]{:S(2)}) collective-permute-start(bf16[160,1024]{1,0:T(8,128)(2,1)S(1)} %pack.3.refs_0_), channel_id=1, source_target_pairs={{0,16},{4,12},{8,24},{12,4},{16,0},{20,28},{24,8},{28,20},{1,17},{... | collective-permute-start | bytes 983048 | tf_op jit(solution)/shard_map/ppermute | solution.py:413
  48.7 9.2 %collective-permute-start.32 = (bf16[160,1024]{1,0:T(8,128)(2,1)S(1)}, bf16[160,1024]{1,0:T(8,128)(2,1)S(1)}, u32[]{:S(2)}, u32[]{:S(2)}) collective-permute-start(bf16[160,1024]{1,0:T(8,128)(2,1)S(1)} %collective-permute-done.30.refs_1_), channel_id=1, source_target_pairs={{0,16},{4,12},{8,24},{12,4},{16,0},{20,28},{24,8},{28,20},{1,17},{... | collective-permute-start | bytes 983048 | tf_op jit(solution)/shard_map/ppermute | solution.py:413
  55.8 19.8 %collective-permute-start.13 = (bf16[160,1024]{1,0:T(8,128)(2,1)S(1)}, bf16[160,1024]{1,0:T(8,128)(2,1)S(1)}, u32[]{:S(2)}, u32[]{:S(2)}) collective-permute-start(bf16[160,1024]{1,0:T(8,128)(2,1)S(1)} %get-tuple-element.50), channel_id=1, source_target_pairs={{0,16},{4,12},{8,24},{12,4},{16,0},{20,28},{24,8},{28,20},{1,17},{... | collective-permute-start | bytes 983048 | tf_op jit(solution)/shard_map/ppermute | solution.py:413
  56.3 10.1 %collective-permute-start.14 = (bf16[160,1024]{1,0:T(8,128)(2,1)S(1)}, bf16[160,1024]{1,0:T(8,128)(2,1)S(1)}, u32[]{:S(2)}, u32[]{:S(2)}) collective-permute-start(bf16[160,1024]{1,0:T(8,128)(2,1)S(1)} %get-tuple-element.52), channel_id=1, source_target_pairs={{0,16},{4,12},{8,24},{12,4},{16,0},{20,28},{24,8},{28,20},{1,17},{... | collective-permute-start | bytes 983048 | tf_op jit(solution)/shard_map/ppermute | solution.py:413
  63.1 12.6 %collective-permute-start.34 = (bf16[160,1024]{1,0:T(8,128)(2,1)S(1)}, bf16[160,1024]{1,0:T(8,128)(2,1)S(1)}, u32[]{:S(2)}, u32[]{:S(2)}) collective-permute-start(bf16[160,1024]{1,0:T(8,128)(2,1)S(1)} %get-tuple-element.66), channel_id=1, source_target_pairs={{0,16},{4,12},{8,24},{12,4},{16,0},{20,28},{24,8},{28,20},{1,17},{... | collective-permute-start | bytes 983048 | tf_op jit(solution)/shard_map/ppermute | solution.py:413
  66.5 9.3 %collective-permute-start.15 = (bf16[160,1024]{1,0:T(8,128)(2,1)S(1)}, bf16[160,1024]{1,0:T(8,128)(2,1)S(1)}, u32[]{:S(2)}, u32[]{:S(2)}) collective-permute-start(bf16[160,1024]{1,0:T(8,128)(2,1)S(1)} %add.18), channel_id=1, source_target_pairs={{0,8},{4,20},{8,0},{12,28},{16,24},{20,4},{24,16},{28,12},{1,9},{5... | collective-permute-start | bytes 983048 | tf_op jit(solution)/shard_map/ppermute | solution.py:413
  75.0 36.5 %copy-start.6 = (s32[64,2]{0,1:T(2,128)S(1)}, s32[64,2]{0,1:T(2,128)}, u32[]{:S(2)}) copy-start(s32[64,2]{0,1:T(2,128)} %param.8) | copy-start | bytes 1540
  75.0 36.4 %copy-start.8 = (f32[64,2]{0,1:T(2,128)S(1)}, f32[64,2]{0,1:T(2,128)}, u32[]{:S(2)}) copy-start(f32[64,2]{0,1:T(2,128)} %param.9) | copy-start | bytes 1540
  75.0 39.2 %collective-permute-start.43 = (bf16[1024,512]{1,0:T(8,128)(2,1)S(1)}, bf16[1024,512]{1,0:T(8,128)(2,1)S(1)}, u32[]{:S(2)}, u32[]{:S(2)}) collective-permute-start(bf16[1024,512]{1,0:T(8,128)(2,1)S(1)} %get-tuple-element.76), channel_id=1, source_target_pairs={{0,4},{4,0},{8,12},{12,8},{16,20},{20,16},{24,28},{28,24},{1,5},{5... | collective-permute-start | bytes 3145736 | tf_op jit(solution)/shard_map/ppermute | solution.py:404
  75.1 39.2 %collective-permute-start.44 = (bf16[1024,512]{1,0:T(8,128)(2,1)S(1)}, bf16[1024,512]{1,0:T(8,128)(2,1)S(1)}, u32[]{:S(2)}, u32[]{:S(2)}) collective-permute-start(bf16[1024,512]{1,0:T(8,128)(2,1)S(1)} %get-tuple-element.77), channel_id=1, source_target_pairs={{0,4},{4,0},{8,12},{12,8},{16,20},{20,16},{24,28},{28,24},{1,5},{5... | collective-permute-start | bytes 3145736 | tf_op jit(solution)/shard_map/ppermute | solution.py:404
  75.6 38.7 %collective-permute-start.45 = (bf16[512,1024]{1,0:T(8,128)(2,1)S(1)}, bf16[512,1024]{1,0:T(8,128)(2,1)S(1)}, u32[]{:S(2)}, u32[]{:S(2)}) collective-permute-start(bf16[512,1024]{1,0:T(8,128)(2,1)S(1)} %get-tuple-element.78), channel_id=1, source_target_pairs={{0,4},{4,0},{8,12},{12,8},{16,20},{20,16},{24,28},{28,24},{1,5},{5... | collective-permute-start | bytes 3145736 | tf_op jit(solution)/shard_map/ppermute | solution.py:404
  75.7 10.2 %collective-permute-start.33 = (bf16[160,1024]{1,0:T(8,128)(2,1)S(1)}, bf16[160,1024]{1,0:T(8,128)(2,1)S(1)}, u32[]{:S(2)}, u32[]{:S(2)}) collective-permute-start(bf16[160,1024]{1,0:T(8,128)(2,1)S(1)} %get-tuple-element.64), channel_id=1, source_target_pairs={{0,16},{4,12},{8,24},{12,4},{16,0},{20,28},{24,8},{28,20},{1,17},{... | collective-permute-start | bytes 983048 | tf_op jit(solution)/shard_map/ppermute | solution.py:413
  75.8 11.3 %collective-permute-start.35 = (bf16[160,1024]{1,0:T(8,128)(2,1)S(1)}, bf16[160,1024]{1,0:T(8,128)(2,1)S(1)}, u32[]{:S(2)}, u32[]{:S(2)}) collective-permute-start(bf16[160,1024]{1,0:T(8,128)(2,1)S(1)} %add.20), channel_id=1, source_target_pairs={{0,8},{4,20},{8,0},{12,28},{16,24},{20,4},{24,16},{28,12},{1,9},{5... | collective-permute-start | bytes 983048 | tf_op jit(solution)/shard_map/ppermute | solution.py:413
  85.9 5.3 %collective-permute-start.16 = (bf16[40,1024]{1,0:T(8,128)(2,1)S(1)}, bf16[40,1024]{1,0:T(8,128)(2,1)S(1)}, u32[]{:S(2)}, u32[]{:S(2)}) collective-permute-start(bf16[40,1024]{1,0:T(8,128)(2,1)S(1)} %get-tuple-element.54), channel_id=1, source_target_pairs={{0,1},{1,0},{2,3},{3,2},{4,5},{5,4},{6,7},{7,6},{8,9},{9,8},{10,11... | collective-permute-start | bytes 245768 | tf_op jit(solution)/shard_map/ppermute | solution.py:407
  87.1 8.2 %collective-permute-start.17 = (bf16[40,1024]{1,0:T(8,128)(2,1)S(1)}, bf16[40,1024]{1,0:T(8,128)(2,1)S(1)}, u32[]{:S(2)}, u32[]{:S(2)}) collective-permute-start(bf16[40,1024]{1,0:T(8,128)(2,1)S(1)} %get-tuple-element.55), channel_id=1, source_target_pairs={{0,2},{1,3},{2,0},{3,1},{4,6},{5,7},{6,4},{7,5},{8,10},{9,11},{10,... | collective-permute-start | bytes 245768 | tf_op jit(solution)/shard_map/ppermute | solution.py:407
  91.2 6.2 %collective-permute-start.18 = (bf16[40,1024]{1,0:T(8,128)(2,1)S(1)}, bf16[40,1024]{1,0:T(8,128)(2,1)S(1)}, u32[]{:S(2)}, u32[]{:S(2)}) collective-permute-start(bf16[40,1024]{1,0:T(8,128)(2,1)S(1)} %get-tuple-element.56), channel_id=1, source_target_pairs={{0,3},{1,2},{2,1},{3,0},{4,7},{5,6},{6,5},{7,4},{8,11},{9,10},{10,... | collective-permute-start | bytes 245768 | tf_op jit(solution)/shard_map/ppermute | solution.py:407
  95.3 2.2 %collective-permute-start.19 = (bf16[40,1024]{1,0:T(8,128)(2,1)S(1)}, bf16[40,1024]{1,0:T(8,128)(2,1)S(1)}, u32[]{:S(2)}, u32[]{:S(2)}) collective-permute-start(bf16[40,1024]{1,0:T(8,128)(2,1)S(1)} %get-tuple-element.53.refs_0_), channel_id=1, source_target_pairs={{0,4},{4,0},{8,12},{12,8},{16,20},{20,16},{24,28},{28,24},{1,5},{5... | collective-permute-start | bytes 245768 | tf_op jit(solution)/shard_map/ppermute | solution.py:404
  97.4 4.7 %collective-permute-start.36 = (bf16[40,1024]{1,0:T(8,128)(2,1)S(1)}, bf16[40,1024]{1,0:T(8,128)(2,1)S(1)}, u32[]{:S(2)}, u32[]{:S(2)}) collective-permute-start(bf16[40,1024]{1,0:T(8,128)(2,1)S(1)} %get-tuple-element.68), channel_id=1, source_target_pairs={{0,1},{1,0},{2,3},{3,2},{4,5},{5,4},{6,7},{7,6},{8,9},{9,8},{10,11... | collective-permute-start | bytes 245768 | tf_op jit(solution)/shard_map/ppermute | solution.py:407
  97.5 8.4 %collective-permute-start.37 = (bf16[40,1024]{1,0:T(8,128)(2,1)S(1)}, bf16[40,1024]{1,0:T(8,128)(2,1)S(1)}, u32[]{:S(2)}, u32[]{:S(2)}) collective-permute-start(bf16[40,1024]{1,0:T(8,128)(2,1)S(1)} %get-tuple-element.69), channel_id=1, source_target_pairs={{0,2},{1,3},{2,0},{3,1},{4,6},{5,7},{6,4},{7,5},{8,10},{9,11},{10,... | collective-permute-start | bytes 245768 | tf_op jit(solution)/shard_map/ppermute | solution.py:407
  102.1 6.2 %collective-permute-start.38 = (bf16[40,1024]{1,0:T(8,128)(2,1)S(1)}, bf16[40,1024]{1,0:T(8,128)(2,1)S(1)}, u32[]{:S(2)}, u32[]{:S(2)}) collective-permute-start(bf16[40,1024]{1,0:T(8,128)(2,1)S(1)} %get-tuple-element.70), channel_id=1, source_target_pairs={{0,3},{1,2},{2,1},{3,0},{4,7},{5,6},{6,5},{7,4},{8,11},{9,10},{10,... | collective-permute-start | bytes 245768 | tf_op jit(solution)/shard_map/ppermute | solution.py:407
  105.8 2.6 %collective-permute-start.39 = (bf16[40,1024]{1,0:T(8,128)(2,1)S(1)}, bf16[40,1024]{1,0:T(8,128)(2,1)S(1)}, u32[]{:S(2)}, u32[]{:S(2)}) collective-permute-start(bf16[40,1024]{1,0:T(8,128)(2,1)S(1)} %get-tuple-element.67.refs_0_), channel_id=1, source_target_pairs={{0,4},{4,0},{8,12},{12,8},{16,20},{20,16},{24,28},{28,24},{1,5},{5... | collective-permute-start | bytes 245768 | tf_op jit(solution)/shard_map/ppermute | solution.py:404
  108.4 1.3 %collective-permute-start.20 = (bf16[40,1024]{1,0:T(8,128)(2,1)S(1)}, bf16[40,1024]{1,0:T(8,128)(2,1)S(1)}, u32[]{:S(2)}, u32[]{:S(2)}) collective-permute-start(bf16[40,1024]{1,0:T(8,128)(2,1)S(1)} %collective-permute-done.16.refs_1_), channel_id=1, source_target_pairs={{0,4},{4,0},{8,12},{12,8},{16,20},{20,16},{24,28},{28,24},{1,5},{5... | collective-permute-start | bytes 245768 | tf_op jit(solution)/shard_map/ppermute | solution.py:404
  108.4 1.4 %collective-permute-start.21 = (bf16[40,1024]{1,0:T(8,128)(2,1)S(1)}, bf16[40,1024]{1,0:T(8,128)(2,1)S(1)}, u32[]{:S(2)}, u32[]{:S(2)}) collective-permute-start(bf16[40,1024]{1,0:T(8,128)(2,1)S(1)} %collective-permute-done.17.refs_2_), channel_id=1, source_target_pairs={{0,4},{4,0},{8,12},{12,8},{16,20},{20,16},{24,28},{28,24},{1,5},{5... | collective-permute-start | bytes 245768 | tf_op jit(solution)/shard_map/ppermute | solution.py:404
  109.7 1.3 %collective-permute-start.22 = (bf16[40,1024]{1,0:T(8,128)(2,1)S(1)}, bf16[40,1024]{1,0:T(8,128)(2,1)S(1)}, u32[]{:S(2)}, u32[]{:S(2)}) collective-permute-start(bf16[40,1024]{1,0:T(8,128)(2,1)S(1)} %collective-permute-done.18.refs_3_), channel_id=1, source_target_pairs={{0,4},{4,0},{8,12},{12,8},{16,20},{20,16},{24,28},{28,24},{1,5},{5... | collective-permute-start | bytes 245768 | tf_op jit(solution)/shard_map/ppermute | solution.py:404
  109.8 1.3 %collective-permute-start.40 = (bf16[40,1024]{1,0:T(8,128)(2,1)S(1)}, bf16[40,1024]{1,0:T(8,128)(2,1)S(1)}, u32[]{:S(2)}, u32[]{:S(2)}) collective-permute-start(bf16[40,1024]{1,0:T(8,128)(2,1)S(1)} %collective-permute-done.36.refs_1_), channel_id=1, source_target_pairs={{0,4},{4,0},{8,12},{12,8},{16,20},{20,16},{24,28},{28,24},{1,5},{5... | collective-permute-start | bytes 245768 | tf_op jit(solution)/shard_map/ppermute | solution.py:404
  110.9 2.1 %collective-permute-start.41 = (bf16[40,1024]{1,0:T(8,128)(2,1)S(1)}, bf16[40,1024]{1,0:T(8,128)(2,1)S(1)}, u32[]{:S(2)}, u32[]{:S(2)}) collective-permute-start(bf16[40,1024]{1,0:T(8,128)(2,1)S(1)} %collective-permute-done.37.refs_2_), channel_id=1, source_target_pairs={{0,4},{4,0},{8,12},{12,8},{16,20},{20,16},{24,28},{28,24},{1,5},{5... | collective-permute-start | bytes 245768 | tf_op jit(solution)/shard_map/ppermute | solution.py:404
  111.1 1.9 %collective-permute-start.42 = (bf16[40,1024]{1,0:T(8,128)(2,1)S(1)}, bf16[40,1024]{1,0:T(8,128)(2,1)S(1)}, u32[]{:S(2)}, u32[]{:S(2)}) collective-permute-start(bf16[40,1024]{1,0:T(8,128)(2,1)S(1)} %collective-permute-done.38.refs_3_), channel_id=1, source_target_pairs={{0,4},{4,0},{8,12},{12,8},{16,20},{20,16},{24,28},{28,24},{1,5},{5... | collective-permute-start | bytes 245768 | tf_op jit(solution)/shard_map/ppermute | solution.py:404

commit v3 on v0

v3 whole, which is shorter than its diff:
```python
import functools

import jax
import jax.numpy as jnp
from jax import lax
from jax.experimental import pallas as pl
from jax.experimental.pallas import tpu as pltpu
from jax.sharding import PartitionSpec as P

BF = jnp.bfloat16
F32 = jnp.float32
NN = (((1,), (0,)), ((), ()))
NT = (((1,), (1,)), ((), ()))
TN = (((0,), (0,)), ((), ()))
MIB = 1024 * 1024
FLOPS_PER_US = 1153000000
VMEM = pl.BlockSpec(memory_space=pltpu.VMEM)
SMEM = pl.BlockSpec(memory_space=pltpu.SMEM)
HBM = pl.BlockSpec(memory_space=pltpu.HBM)
ANY = pl.BlockSpec(memory_space=pl.ANY)


def dot(a, b, dims=NN):
    return lax.dot_general(a, b, dims, preferred_element_type=F32)


def shaped(*shape):
    return jax.ShapeDtypeStruct(shape, BF)


def kernel_call(
    kernel, name, in_specs, out_specs, out_shape, scratch=(), limit=4, flops=0, alias=None, after=()
):
    count = len(in_specs)

    def run(*refs):
        kernel(*refs[:count], *refs[count + len(after) :])

    call = pl.pallas_call(
        run,
        in_specs=list(in_specs) + [ANY] * len(after),
        out_specs=out_specs,
        out_shape=out_shape,
        scratch_shapes=list(scratch),
        input_output_aliases=alias or {},
        cost_estimate=pl.CostEstimate(flops=flops, bytes_accessed=0, transcendentals=0),
        compiler_params=pltpu.CompilerParams(vmem_limit_bytes=limit * MIB),
        name=name,
    )
    return lambda *operands: call(*operands, *after)


def places(ids, experts):
    top, toks = ids.shape
    rows = lax.broadcasted_iota(jnp.int32, (experts, toks), 0)
    hot = [(ids[k : k + 1, :] == rows).astype(F32) for k in range(top)]
    earlier = (
        lax.broadcasted_iota(jnp.int32, (toks, toks), 0)
        < lax.broadcasted_iota(jnp.int32, (toks, toks), 1)
    ).astype(BF)
    counts = dot(sum(hot).astype(BF), earlier)
    return [jnp.sum(counts * h, axis=0, keepdims=True).astype(jnp.int32) for h in hot]


def start_all(pairs, sems):
    copies = [pltpu.make_async_copy(a, b, sems.at[i]) for i, (a, b) in enumerate(pairs)]
    for c in copies:
        c.start()
    return copies


def picks(ids, local, cap, experts, owner):
    top, toks = ids.shape
    here = places(ids, experts)
    rows = lax.broadcasted_iota(jnp.int32, (local * cap, toks), 0)
    return [
        jnp.where(
            (ids[k : k + 1, :] // local == owner)
            & ((ids[k : k + 1, :] % local) * cap + here[k] == rows),
            1.0,
            0.0,
        )
        for k in range(top)
    ]


def place_rows_kernel(experts, local, cap, expert_pos, ids_hbm, tok_hbm, out, chosen, *refs):
    ids_ref, tok_ref, sems = refs
    copies = start_all(((ids_hbm, ids_ref), (tok_hbm, tok_ref)), sems)
    copies[0].wait()
    ids = ids_ref[...]
    hits = []
    for j in range(experts // local):
        owner = jnp.bitwise_xor(expert_pos[0], j)
        hits.append(sum(picks(ids, local, cap, experts, owner)))
    chosen[...] = jnp.concatenate(hits, axis=0).astype(BF)
    copies[1].wait()
    out[...] = dot(chosen[...], tok_ref[...]).astype(BF)


def place_rows(expert_pos, ids, tokens, experts, local, cap):
    toks, width = tokens.shape
    return kernel_call(
        functools.partial(place_rows_kernel, experts, local, cap),
        "place_rows",
        [SMEM] + [HBM] * 2,
        [VMEM] * 2,
        [shaped(experts * cap, width), shaped(experts * cap, toks)],
        [pltpu.VMEM(a.shape, a.dtype) for a in (ids, tokens)] + [pltpu.SemaphoreType.DMA((2,))],
    )(expert_pos, ids, tokens)


def place_scaled_kernel(experts, local, cap, expert_pos, ids_hbm, gw_hbm, cot_hbm, *refs):
    out, high, low, ids_ref, gw_ref, cot_ref, sems = refs
    copies = start_all(((ids_hbm, ids_ref), (gw_hbm, gw_ref), (cot_hbm, cot_ref)), sems)
    copies[0].wait()
    copies[1].wait()
    ids = ids_ref[...]
    gw = gw_ref[...]
    hits, scales = [], []
    for j in range(experts // local):
        owner = jnp.bitwise_xor(expert_pos[0], j)
        hit = picks(ids, local, cap, experts, owner)
        hits.append(sum(hit))
        scales.append(sum(h * gw[k : k + 1, :] for k, h in enumerate(hit)))
    chosen = jnp.concatenate(hits, axis=0).astype(BF)
    scale = jnp.concatenate(scales, axis=0)
    high[...] = scale.astype(BF)
    low[...] = (scale - scale.astype(BF).astype(F32)).astype(BF)
    copies[2].wait()
    rows = dot(chosen, cot_ref[...])
    out[...] = (jnp.sum(scale, axis=1, keepdims=True) * rows).astype(BF)


def place_scaled(expert_pos, ids, gw, cot, experts, local, cap, after):
    toks, width = cot.shape
    return kernel_call(
        functools.partial(place_scaled_kernel, experts, local, cap),
        "place_scaled",
        [SMEM] + [HBM] * 3,
        [VMEM] * 3,
        [shaped(experts * cap, width)] + [shaped(experts * cap, toks)] * 2,
        [pltpu.VMEM(a.shape, a.dtype) for a in (ids, gw, cot)] + [pltpu.SemaphoreType.DMA((3,))],
        after=after,
    )(expert_pos, ids, gw, cot)


def blend_kernel(owners, cap, core, mine, theirs, *outs):
    size = mine.shape[0]
    part = size // owners
    row = lax.broadcasted_iota(jnp.int32, (size, size), 0)
    column = lax.broadcasted_iota(jnp.int32, (size, size), 1)
    first = core[0] * cap
    inside = row % part
    here = (inside >= first) & (inside < first + cap)
    shift = (1 - 2 * core[0]) * cap
    keep = jnp.where(here & (column == row), 1.0, 0.0).astype(BF)
    take = jnp.where((~here) & (column == row - shift), 1.0, 0.0).astype(BF)
    total = dot(keep, mine[...]) + dot(take, theirs[...])
    for j, out in enumerate(outs):
        out[...] = total[j * part : (j + 1) * part].astype(BF)


def blend(core, mine, theirs, owners, cap, after=()):
    size, width = mine.shape
    return kernel_call(
        functools.partial(blend_kernel, owners, cap),
        "blend",
        [SMEM] + [VMEM] * 2,
        [VMEM] * owners,
        [shaped(size // owners, width)] * owners,
        after=after,
    )(core, mine, theirs)


def join_kernel(*refs):
    parts, out = refs[:-1], refs[-1]
    out[...] = jnp.concatenate([p[...].astype(F32) for p in parts], axis=0).astype(BF)


def join(parts, after=(), flops=0):
    size, width = parts[0].shape
    return kernel_call(
        join_kernel,
        "join",
        [VMEM] * len(parts),
        VMEM,
        shaped(len(parts) * size, width),
        after=after,
        flops=flops,
    )(*parts)


def fetch(core, weights, held, sems):
    return start_all([(w.at[core[0]], h) for w, h in zip(weights, held)], sems)


def gather_rows(parts, out):
    first = 0
    for part in parts:
        out[first : first + part.shape[0], :] = part[...]
        first += part.shape[0]


def scatter_rows(total, parts, cols):
    first = 0
    for part in parts:
        part[:, cols] = total[first : first + part.shape[0]].astype(BF)
        first += part.shape[0]


def tile_of(hidden):
    return 256 if hidden % 256 == 0 else hidden


def chunks(total, size):
    return [slice(i, min(i + size, total)) for i in range(0, total, size)]


def forward_kernel(low, high, core, *refs):
    ps = refs[6:8]
    x, f1, f2, hid, g0, u0, d0, g1, u1, d1, gate_s, up_s, sems = refs[8:]
    own, other = refs[:3], refs[3:6]
    sources = (own[0], own[1], other[0], other[1], own[2], other[2])
    loads = fetch(core, sources, (g0, u0, g1, u1, d0, d1), sems)
    gather_rows((low, high), x)
    weights = ((g0, u0, d0), (g1, u1, d1))
    hidden = g0.shape[1]
    rows, width = x.shape
    turn = 0
    for half, (a, b, _) in enumerate(weights):
        loads[2 * half].wait()
        loads[2 * half + 1].wait()
        for cols in chunks(hidden, tile_of(hidden)):
            gate_s[turn] = dot(x[...], a[:, cols])
            up_s[turn] = dot(x[...], b[:, cols])
            for r in chunks(rows, 64):
                gate, up = gate_s[turn, r], up_s[turn, r]
                sig = 1.0 / (1.0 + jnp.exp(-gate))
                act = gate * sig
                hid[half, r, cols] = (act * up).astype(BF)
                f1[half, r, cols] = (up * sig * (1.0 + gate * (1.0 - sig))).astype(BF)
                f2[half, r, cols] = act.astype(BF)
            turn = 1 - turn
    loads[4].wait()
    loads[5].wait()
    for cols in chunks(width, tile_of(width)):
        total = dot(hid[0], d0[:, cols]) + dot(hid[1], d1[:, cols])
        scatter_rows(total, ps, cols)


def forward(core, xs, own, other):
    size, width = xs[0].shape
    hidden = own[0].shape[2]
    rows = 2 * size
    out = kernel_call(
        forward_kernel,
        "forward",
        [VMEM] * 2 + [SMEM] + [HBM] * 6,
        [VMEM] * 6,
        [shaped(size, width)] * 2 + [shaped(rows, width)] + [shaped(2, rows, hidden)] * 3,
        [pltpu.VMEM(w.shape[1:], BF) for w in own + own]
        + [pltpu.VMEM((2, rows, tile_of(hidden)), F32)] * 2
        + [pltpu.SemaphoreType.DMA((6,))],
        limit=32,
        flops=12 * rows * width * hidden,
    )(*xs, core, *own, *other)
    return out[:2], *out[2:]


def backward_kernel(low, high, core, *refs):
    f1, f2, qs = refs[6], refs[7], refs[8:10]
    dy, dg, du, g0, u0, d0, g1, u1, d1, da_s, sems = refs[10:]
    own, other = refs[:3], refs[3:6]
    sources = (own[2], other[2], own[0], own[1], other[0], other[1])
    loads = fetch(core, sources, (d0, d1, g0, u0, g1, u1), sems)
    gather_rows((low, high), dy)
    hidden = g0.shape[1]
    rows, width = dy.shape
    turn = 0
    for half, a in enumerate((d0, d1)):
        loads[half].wait()
        for cols in chunks(hidden, tile_of(hidden)):
            da_s[turn] = dot(dy[...], a[cols, :], NT)
            for r in chunks(rows, 64):
                da = da_s[turn, r]
                dg[half, r, cols] = (da * f1[half, r, cols].astype(F32)).astype(BF)
                du[half, r, cols] = (da * f2[half, r, cols].astype(F32)).astype(BF)
            turn = 1 - turn
    for c in loads[2:]:
        c.wait()
    for cols in chunks(width, tile_of(width)):
        total = dot(dg[0], g0[cols, :], NT) + dot(du[0], u0[cols, :], NT)
        total = total + dot(dg[1], g1[cols, :], NT) + dot(du[1], u1[cols, :], NT)
        scatter_rows(total, qs, cols)


def backward(core, dys, own, other, f1, f2):
    size, width = dys[0].shape
    hidden = own[0].shape[2]
    rows = 2 * size
    out = kernel_call(
        backward_kernel,
        "backward",
        [VMEM] * 2 + [SMEM] + [HBM] * 6 + [VMEM] * 2,
        [VMEM] * 5,
        [shaped(size, width)] * 2 + [shaped(rows, width)] + [shaped(2, rows, hidden)] * 2,
        [pltpu.VMEM(w.shape[1:], BF) for w in own + own]
        + [pltpu.VMEM((2, rows, tile_of(hidden)), F32)]
        + [pltpu.SemaphoreType.DMA((6,))],
        limit=32,
        flops=12 * rows * width * hidden,
    )(*dys, core, *own, *other, f1, f2)
    return out[:2], *out[2:]


def grads_kernel(half, core, x, dy, dg, du, hid, *refs):
    outs = [refs[0].at[i] for i in range(3)] if half else refs[3:6]
    hidden = dg.shape[2]
    width = x.shape[1]
    save = []

    def store(i):
        if not half:
            save.append(pltpu.make_async_copy(outs[i], refs[i].at[core[0]], refs[6].at[i]))
            save[i].start()

    for cols in chunks(hidden, tile_of(hidden)):
        outs[0][:, cols] = dot(x[...], dg[half, :, cols], TN).astype(BF)
    store(0)
    for cols in chunks(hidden, tile_of(hidden)):
        outs[1][:, cols] = dot(x[...], du[half, :, cols], TN).astype(BF)
    store(1)
    if half:
        for cols in chunks(hidden, tile_of(hidden)):
            outs[2][:, cols] = dot(dy[...], hid[half, :, cols], TN).astype(BF)
    else:
        for cols in chunks(width, tile_of(width)):
            outs[2][:, cols] = dot(hid[half], dy[:, cols], TN).astype(BF)
    store(2)
    for c in save:
        c.wait()


def grads(half, core, x, dy, dg, du, hid, local, after):
    rows, width = x.shape
    hidden = dg.shape[2]
    wide, tall = (width, hidden), (hidden, width)
    if half:
        outs, scratch = [shaped(3, *wide)], []
    else:
        outs = [shaped(local, *s) for s in (wide, wide, tall)]
        scratch = [pltpu.VMEM(s, BF) for s in (wide, wide, tall)] + [pltpu.SemaphoreType.DMA((3,))]
    return kernel_call(
        functools.partial(grads_kernel, half),
        "grads_given" if half else "grads_kept",
        [SMEM] + [VMEM] * 5,
        [VMEM if half else HBM] * len(outs),
        outs,
        scratch,
        limit=32,
        flops=6 * rows * width * hidden,
        after=after,
    )(core, x, dy, dg, du, hid)


def finish_kernel(core, got, *refs):
    outs, down, sems = refs[3:6], refs[6], refs[7]
    place = 1 - core[0]
    copies = start_all([(got.at[i], outs[i].at[place]) for i in range(2)], sems)
    down[...] = got[2].T
    copies += start_all([(down, outs[2].at[place])], sems.at[pl.ds(2, 1)])
    for c in copies:
        c.wait()


def finish(core, got, kept):
    return kernel_call(
        finish_kernel,
        "finish",
        [SMEM, VMEM] + [HBM] * 3,
        [HBM] * 3,
        [shaped(*k.shape) for k in kept],
        [pltpu.VMEM(kept[2].shape[1:], BF), pltpu.SemaphoreType.DMA((3,))],
        limit=14,
        alias={2: 0, 3: 1, 4: 2},
    )(core, got, *kept)


def add_kernel(first, second, *outs):
    total = first[...].astype(F32) + second[...].astype(F32)
    size = total.shape[0] // len(outs)
    for j, out in enumerate(outs):
        out[...] = total[j * size : (j + 1) * size].astype(BF)


def add(arrays, pieces=1, after=()):
    rows, width = arrays[0].shape
    return kernel_call(
        add_kernel,
        "add",
        [VMEM] * 2,
        [VMEM] * pieces,
        [shaped(rows // pieces, width)] * pieces,
        after=after,
    )(*arrays)


def combine_kernel(weights, *refs):
    messages, out = refs[weights:-1], refs[-1]
    values = jnp.concatenate([m[...].astype(F32) for m in messages], axis=0).astype(BF)
    out[...] = sum(dot(w[...], values, TN) for w in refs[:weights]).astype(BF)


def combine(weights, messages, after=()):
    return kernel_call(
        functools.partial(combine_kernel, len(weights)),
        "combine",
        [VMEM] * (len(weights) + len(messages)),
        VMEM,
        shaped(weights[0].shape[1], messages[0].shape[1]),
        after=after,
    )(*weights, *messages)


def body(tokens, expert_ids, gate_weights, w_gate, w_up, w_down, cotangent):
    owners = lax.axis_size("expert")
    devices = lax.axis_size("dp")
    toks, width = tokens.shape
    top = expert_ids.shape[1]
    local = w_gate.shape[0]
    experts = local * owners
    cap = max(2, 5 * toks * top // (4 * experts))
    bits = (devices // 2).bit_length() - 1
    assert local == 2 and devices == 2 << bits and owners & (owners - 1) == 0

    side = lax.axis_index("dp") % 2
    core = side.astype(jnp.int32).reshape(1)
    expert_pos = lax.axis_index("expert").astype(jnp.int32).reshape(1)
    ids, gw = expert_ids.T, gate_weights.T

    def to_pair(a):
        return lax.ppermute(a, "dp", [(i, i ^ 1) for i in range(devices)])

    def to_owner(a, j):
        return lax.ppermute(a, "expert", [(i, i ^ j) for i in range(owners)])

    def to_chip(a, s):
        def bit(i):
            return 2 << ((s + (i % 2) * (bits // 2)) % bits)

        return lax.ppermute(a, "dp", [(i, i ^ bit(i)) for i in range(devices)])

    def swap(messages):
        return [messages[0]] + [to_owner(messages[j], j) for j in range(1, owners)]

    def widen(part, after=()):
        for s in range(bits - 1):
            part = join([part, to_chip(part, s)], after)
        return part

    def reduce(low, high, after=()):
        for s in reversed(range(1, bits)):
            low, high = add([low, to_chip(high, s)], 2, after)
        return low, high

    def hand_out(rows, after=()):
        return blend(core, rows, to_pair(rows), owners, cap, after)

    own = (w_gate, w_up, w_down)
    rows, chosen = place_rows(expert_pos, ids, tokens, experts, local, cap)
    messages = hand_out(rows)
    rows, high, low = place_scaled(expert_pos, ids, gw, cotangent, experts, local, cap, [rows])
    scaled = hand_out(rows)
    joined = join(swap(messages), scaled[:1])
    joined_scaled = join(swap(scaled), [joined], 18 * FLOPS_PER_US)
    x_low = widen(joined)
    x_high = to_chip(x_low, bits - 1)
    *behind, _ = lax.optimization_barrier((*own, x_low))
    other = [to_pair(w) for w in behind]
    dy_low = widen(joined_scaled, [x_low])
    dy_high = to_chip(dy_low, bits - 1)
    ps, x, f1, f2, hid = forward(core, (x_low, x_high), own, other)
    qs, dy, dg, du = backward(core, (dy_low, dy_high), own, other, f1, f2)
    p_low, p_high = reduce(*ps, [dy])
    given = grads(1, core, x, dy, dg, du, hid, local, [p_high])
    q_low, q_high = reduce(*qs, given[:1])
    p_messages = hand_out(add([p_low, to_chip(p_high, 0)], 1, [q_high])[0])
    q_rows = add([q_low, to_chip(q_high, 0)], 1, p_messages[:1])[0]
    kept = grads(0, core, x, dy, dg, du, hid, local, [q_rows])
    p_messages = join(swap(p_messages), kept[:1], 20 * FLOPS_PER_US)
    q_messages = hand_out(q_rows, [p_messages])
    mixed = combine([high, low], [p_messages], q_messages[:1])
    behind, _ = lax.optimization_barrier((given[0], q_messages[0]))
    got = to_pair(behind)
    grad_gate, grad_up, grad_down = finish(core, got, kept)
    grad_tokens = combine([chosen], swap(q_messages), [grad_gate])
    return (mixed, grad_tokens, grad_gate, grad_up, grad_down)


def solution(mesh):
    rows = P(("dp", "expert"), None)
    wide, tall = P("expert", None, "dp"), P("expert", "dp", None)
    return jax.shard_map(
        body,
        mesh=mesh,
        in_specs=(rows, rows, rows, wide, wide, tall, rows),
        out_specs=(rows, rows, wide, wide, tall),
        check_vma=False,
    )
```

time: 249 us -> 97.1 us (0.39)
  waiting for transfers between devices: 129 us -> 32.7 us
  matrix products: 35.6 us -> 0 us
  blocking collectives: 28.6 us -> 0 us
  Pallas kernels: 0 us -> 24.4 us
  starting transfers between devices: 8.31 us -> 32.4 us
  local copies, waits for them, and re-layouts: 27.4 us -> 6.51 us
  between operations: 14.1 us -> 0.9 us
  other arithmetic: 4.97 us -> 0 us
    unnamed x4 -> x0, waiting for transfers between devices: 86.4 us -> none
    all_gather x2 -> x0, waiting for transfers between devices: 37.2 us -> none  [spread_one(): return lax.all_gather(arrived[None], 'dp', axis=0, tiled=True)]
    dot_general x11 -> x0, matrix products: 35.6 us -> none  [the longest x1 6.04 us: body(): jnp.einsum('pcjkd,jfd->pcjkf', grad_rows, w_down, preferred_element_type=...]
    ppermute x0 -> x28, waiting for transfers between devices: none -> 32.7 us  [the longest x8 18.8 us: to_chip(): return lax.ppermute(a, 'dp', [(i, i ^ bit(i)) for i in range(devices)])]
    ppermute x0 -> x28, starting transfers between devices: none -> 32.4 us  [the longest x12 19 us: to_owner(): return lax.ppermute(a, 'expert', [(i, i ^ j) for i in range(owners)])]
    all_to_all x2 -> x0, blocking collectives: 28.6 us -> none  [spread_one(): lax.all_to_all(buffer, 'expert', split_axis=0, concat_axis=0, tiled=True)]
    pallas_call x0 -> x22, Pallas kernels: none -> 24.4 us  [kernel_call(): return lambda *operands: call(*operands, *after)]
    all_to_all x2 -> x0, starting transfers between devices: 8.19 us -> none  [collect(): lax.all_to_all(summed, 'expert', split_axis=1, concat_axis=1, tiled=True)]
  transfers between devices with their start and end apart: 5 -> 28, of which waited for: 5 -> 13; matrix products, arithmetic and copies ran while one was open for 13% -> 0% of each run, Pallas kernels for 0% -> 23%
where the time goes in v3:
time: 97.1 us; the launch traced here: 96.8 us
  waiting for transfers between devices  32.7 us (34%)
  starting transfers between devices  32.4 us (33%)
  Pallas kernels  24.4 us (25%)
  local copies, waits for them, and re-layouts  6.51 us (7%)
    pallas_call x22, Pallas kernels, kernel_call(): return lambda *operands: call(*operands, *after)  24.4 us
    ppermute x12, starting transfers between devices, to_owner(): return lax.ppermute(a, 'expert', [(i, i ^ j) for i in range(owners)])  19 us
    ppermute x8, waiting for transfers between devices, to_chip(): return lax.ppermute(a, 'dp', [(i, i ^ bit(i)) for i in range(devices)])  18.8 us
    ppermute x12, waiting for transfers between devices, to_owner(): return lax.ppermute(a, 'expert', [(i, i ^ j) for i in range(owners)])  13.2 us
    ppermute x8, starting transfers between devices, to_chip(): return lax.ppermute(a, 'dp', [(i, i ^ bit(i)) for i in range(devices)])  10.8 us
    unnamed x18, local copies, waits for them, and re-layouts  6.51 us
    ppermute x8, starting transfers between devices, to_pair(): return lax.ppermute(a, 'dp', [(i, i ^ 1) for i in range(devices)])  2.57 us
  transfers between devices with their start and end apart: 28, of which 13 were waited for; matrix products, arithmetic and copies ran while one was open for 0% of the time, Pallas kernels for 23%

profile of v3, /device:TPU:0, one launch (start us, length us, event | category | flops | bytes accessed | tf_op | source)
XLA Modules:
  0.0 96.8 jit_solution(5299840120990492978)
XLA Ops:
  0.7 1.0 %copy-done.5 = bf16[64,1024]{1,0:T(8,128)(2,1)S(1)} copy-done((bf16[64,1024]{1,0:T(8,128)(2,1)S(1)}, bf16[64,1024]{1,0:T(8,128)(2,1)}, u32[]{:S(2)}) %copy-start.5) | copy-done | bytes 131096
  1.7 0.7 copy-done.7
  2.4 0.6 place_rows.1
  2.9 0.5 collective-permute-start
  3.5 0.9 copy-done.6
  4.4 0.7 copy-done.8
  5.0 0.6 place_scaled.1
  5.6 0.1 collective-permute-start.4
  5.8 0.3 blend.4
  6.1 3.1 %collective-permute-start.1 = (bf16[40,1024]{1,0:T(8,128)(2,1)S(1)}, bf16[40,1024]{1,0:T(8,128)(2,1)S(1)}, u32[]{:S(2)}, u32[]{:S(2)}) collective-permute-start(bf16[40,1024]{1,0:T(8,128)(2,1)S(1)} %get-tuple-element.55), channel_id=1, source_target_pairs={{0,1},{1,0},{2,3},{3,2},{4,5},{5,4},{6,7},{7,6},{8,9},{9,8},{10,11... | collective-permute-start | bytes 245768 | tf_op jit(solution)/shard_map/ppermute | solution.py:446
  9.2 2.6 %collective-permute-start.2 = (bf16[40,1024]{1,0:T(8,128)(2,1)S(1)}, bf16[40,1024]{1,0:T(8,128)(2,1)S(1)}, u32[]{:S(2)}, u32[]{:S(2)}) collective-permute-start(bf16[40,1024]{1,0:T(8,128)(2,1)S(1)} %get-tuple-element.56), channel_id=1, source_target_pairs={{0,2},{1,3},{2,0},{3,1},{4,6},{5,7},{6,4},{7,5},{8,10},{9,11},{10,... | collective-permute-start | bytes 245768 | tf_op jit(solution)/shard_map/ppermute | solution.py:446
  11.8 0.0 collective-permute-start.3
  11.8 0.3 blend.5
  12.1 6.5 %collective-permute-done.2.refs_2_ = bf16[40,1024]{1,0:T(8,128)(2,1)S(1)} collective-permute-done((bf16[40,1024]{1,0:T(8,128)(2,1)S(1)}, bf16[40,1024]{1,0:T(8,128)(2,1)S(1)}, u32[]{:S(2)}, u32[]{:S(2)}) %collective-permute-start.2) | collective-permute-done | bytes 81952 | tf_op jit(solution)/shard_map/ppermute | solution.py:446
  18.6 1.6 %collective-permute-start.5 = (bf16[160,1024]{1,0:T(8,128)(2,1)S(1)}, bf16[160,1024]{1,0:T(8,128)(2,1)S(1)}, u32[]{:S(2)}, u32[]{:S(2)}) collective-permute-start(bf16[160,1024]{1,0:T(8,128)(2,1)S(1)} %join.5.refs_0_.refs_4_), channel_id=1, source_target_pairs={{0,8},{4,20},{8,0},{12,28},{16,24},{20,4},{24,16},{28,12},{1,9},{5... | collective-permute-start | bytes 983048 | tf_op jit(solution)/shard_map/ppermute | solution.py:452
  20.2 1.5 %collective-permute-start.11 = (bf16[40,1024]{1,0:T(8,128)(2,1)S(1)}, bf16[40,1024]{1,0:T(8,128)(2,1)S(1)}, u32[]{:S(2)}, u32[]{:S(2)}) collective-permute-start(bf16[40,1024]{1,0:T(8,128)(2,1)S(1)} %get-tuple-element.65), channel_id=1, source_target_pairs={{0,1},{1,0},{2,3},{3,2},{4,5},{5,4},{6,7},{7,6},{8,9},{9,8},{10,11... | collective-permute-start | bytes 245768 | tf_op jit(solution)/shard_map/ppermute | solution.py:446
  21.7 1.5 %collective-permute-start.12 = (bf16[40,1024]{1,0:T(8,128)(2,1)S(1)}, bf16[40,1024]{1,0:T(8,128)(2,1)S(1)}, u32[]{:S(2)}, u32[]{:S(2)}) collective-permute-start(bf16[40,1024]{1,0:T(8,128)(2,1)S(1)} %get-tuple-element.66), channel_id=1, source_target_pairs={{0,2},{1,3},{2,0},{3,1},{4,6},{5,7},{6,4},{7,5},{8,10},{9,11},{10,... | collective-permute-start | bytes 245768 | tf_op jit(solution)/shard_map/ppermute | solution.py:446
  23.2 1.4 %collective-permute-start.13 = (bf16[40,1024]{1,0:T(8,128)(2,1)S(1)}, bf16[40,1024]{1,0:T(8,128)(2,1)S(1)}, u32[]{:S(2)}, u32[]{:S(2)}) collective-permute-start(bf16[40,1024]{1,0:T(8,128)(2,1)S(1)} %get-tuple-element.67), channel_id=1, source_target_pairs={{0,3},{1,2},{2,1},{3,0},{4,7},{5,6},{6,5},{7,4},{8,11},{9,10},{10,... | collective-permute-start | bytes 245768 | tf_op jit(solution)/shard_map/ppermute | solution.py:446
  24.6 1.4 %collective-permute-done.5.refs_1_ = bf16[160,1024]{1,0:T(8,128)(2,1)S(1)} collective-permute-done((bf16[160,1024]{1,0:T(8,128)(2,1)S(1)}, bf16[160,1024]{1,0:T(8,128)(2,1)S(1)}, u32[]{:S(2)}, u32[]{:S(2)}) %collective-permute-start.5) | collective-permute-done | bytes 327712 | tf_op jit(solution)/shard_map/ppermute | solution.py:452
  26.0 0.0 copy-start.3
  26.0 0.0 copy-start.4
  26.0 1.6 %collective-permute-start.6 = (bf16[320,1024]{1,0:T(8,128)(2,1)S(1)}, bf16[320,1024]{1,0:T(8,128)(2,1)S(1)}, u32[]{:S(2)}, u32[]{:S(2)}) collective-permute-start(bf16[320,1024]{1,0:T(8,128)(2,1)S(1)} %join.6.refs_0_.refs_2_), channel_id=1, source_target_pairs={{0,16},{4,12},{8,24},{12,4},{16,0},{20,28},{24,8},{28,20},{1,17},{... | collective-permute-start | bytes 1966088 | tf_op jit(solution)/shard_map/ppermute | solution.py:452
  27.6 0.5 collective-permute-start.8
  28.1 1.8 %collective-permute-done.12.refs_2_ = bf16[40,1024]{1,0:T(8,128)(2,1)S(1)} collective-permute-done((bf16[40,1024]{1,0:T(8,128)(2,1)S(1)}, bf16[40,1024]{1,0:T(8,128)(2,1)S(1)}, u32[]{:S(2)}, u32[]{:S(2)}) %collective-permute-start.12) | collective-permute-done | bytes 81952 | tf_op jit(solution)/shard_map/ppermute | solution.py:446
  29.9 1.2 %collective-permute-start.14 = (bf16[160,1024]{1,0:T(8,128)(2,1)S(1)}, bf16[160,1024]{1,0:T(8,128)(2,1)S(1)}, u32[]{:S(2)}, u32[]{:S(2)}) collective-permute-start(bf16[160,1024]{1,0:T(8,128)(2,1)S(1)} %join.7.refs_0_), channel_id=1, source_target_pairs={{0,8},{4,20},{8,0},{12,28},{16,24},{20,4},{24,16},{28,12},{1,9},{5... | collective-permute-start | bytes 983048 | tf_op jit(solution)/shard_map/ppermute | solution.py:452
  31.2 5.9 %collective-permute-done.14.refs_1_ = bf16[160,1024]{1,0:T(8,128)(2,1)S(1)} collective-permute-done((bf16[160,1024]{1,0:T(8,128)(2,1)S(1)}, bf16[160,1024]{1,0:T(8,128)(2,1)S(1)}, u32[]{:S(2)}, u32[]{:S(2)}) %collective-permute-start.14) | collective-permute-done | bytes 327712 | tf_op jit(solution)/shard_map/ppermute | solution.py:452
  37.1 1.2 %collective-permute-start.15 = (bf16[320,1024]{1,0:T(8,128)(2,1)S(1)}, bf16[320,1024]{1,0:T(8,128)(2,1)S(1)}, u32[]{:S(2)}, u32[]{:S(2)}) collective-permute-start(bf16[320,1024]{1,0:T(8,128)(2,1)S(1)} %join.8.refs_0_), channel_id=1, source_target_pairs={{0,16},{4,12},{8,24},{12,4},{16,0},{20,28},{24,8},{28,20},{1,17},{... | collective-permute-start | bytes 1966088 | tf_op jit(solution)/shard_map/ppermute | solution.py:452
  38.4 1.8 %collective-permute-done.6.refs_1_ = bf16[320,1024]{1,0:T(8,128)(2,1)S(1)} collective-permute-done((bf16[320,1024]{1,0:T(8,128)(2,1)S(1)}, bf16[320,1024]{1,0:T(8,128)(2,1)S(1)}, u32[]{:S(2)}, u32[]{:S(2)}) %collective-permute-start.6) | collective-permute-done | bytes 655392 | tf_op jit(solution)/shard_map/ppermute | solution.py:452
  40.2 5.9 %forward.1 = (bf16[320,1024]{1,0:T(8,128)(2,1)S(1)}, bf16[320,1024]{1,0:T(8,128)(2,1)S(1)}, bf16[640,1024]{1,0:T(8,128)(2,1)S(1)}, bf16[2,640,512]{2,1,0:T(8,128...) custom-call(bf16[320,1024]{1,0:T(8,128)(2,1)S(1)} %join.6.refs_0_.refs_2_, ...), custom_call_target="tpu_custom_call" | custom-call | flops 4026531840 | tf_op jit(solution)/shard_map/forward/pallas_call | solution.py:50
  46.1 1.6 %collective-permute-start.10 = (bf16[320,1024]{1,0:T(8,128)(2,1)S(1)}, bf16[320,1024]{1,0:T(8,128)(2,1)S(1)}, u32[]{:S(2)}, u32[]{:S(2)}) collective-permute-start(bf16[320,1024]{1,0:T(8,128)(2,1)S(1)} %get-tuple-element.64), channel_id=1, source_target_pairs={{0,16},{4,12},{8,24},{12,4},{16,0},{20,28},{24,8},{28,20},{1,17},{... | collective-permute-start | bytes 1966088 | tf_op jit(solution)/shard_map/ppermute | solution.py:452
  47.7 0.1 collective-permute-done.15.refs_1_
  47.8 5.5 %backward.1 = (bf16[320,1024]{1,0:T(8,128)(2,1)S(1)}, bf16[320,1024]{1,0:T(8,128)(2,1)S(1)}, bf16[640,1024]{1,0:T(8,128)(2,1)S(1)}, bf16[2,640,512]{2,1,0:T(8,128)(2,1)S(1)}, bf16[2,640,512]{2,1,0:T(8,128)(2,1)S(1)}) custom-call(bf16[320,1024]{1,0:T(8,128)(2,1)S(1)} %join.8.refs_0_, bf16[320,1024]{1,0:T(8,128)(2,1)S(1)} %collective-permute-done.15.refs_1_, ...), custom_call_target="tpu_custom_call" | custom-call | flops 4026531840 | tf_op jit(solution)/shard_map/backward/pallas_call | solution.py:50
  53.3 1.2 %collective-permute-start.17 = (bf16[320,1024]{1,0:T(8,128)(2,1)S(1)}, bf16[320,1024]{1,0:T(8,128)(2,1)S(1)}, u32[]{:S(2)}, u32[]{:S(2)}) collective-permute-start(bf16[320,1024]{1,0:T(8,128)(2,1)S(1)} %get-tuple-element.74), channel_id=1, source_target_pairs={{0,16},{4,12},{8,24},{12,4},{16,0},{20,28},{24,8},{28,20},{1,17},{... | collective-permute-start | bytes 1966088 | tf_op jit(solution)/shard_map/ppermute | solution.py:452
  54.5 2.2 %collective-permute-done.10.refs_1_ = bf16[320,1024]{1,0:T(8,128)(2,1)S(1)} collective-permute-done((bf16[320,1024]{1,0:T(8,128)(2,1)S(1)}, bf16[320,1024]{1,0:T(8,128)(2,1)S(1)}, u32[]{:S(2)}, u32[]{:S(2)}) %collective-permute-start.10) | collective-permute-done | bytes 655392 | tf_op jit(solution)/shard_map/ppermute | solution.py:452
  56.8 0.2 add.9
  56.9 1.5 %collective-permute-start.16 = (bf16[160,1024]{1,0:T(8,128)(2,1)S(1)}, bf16[160,1024]{1,0:T(8,128)(2,1)S(1)}, u32[]{:S(2)}, u32[]{:S(2)}) collective-permute-start(bf16[160,1024]{1,0:T(8,128)(2,1)S(1)} %get-tuple-element.72.refs_6_), channel_id=1, source_target_pairs={{0,8},{4,20},{8,0},{12,28},{16,24},{20,4},{24,16},{28,12},{1,9},{5... | collective-permute-start | bytes 983048 | tf_op jit(solution)/shard_map/ppermute | solution.py:452
  58.5 2.7 %grads_given.1.refs_2_ = bf16[3,1024,512]{2,1,0:T(8,128)(2,1)S(1)} custom-call(s32[1]{0:T(128)} %bitcast.3.refs_0_.refs_2_, bf16[640,1024]{1,0:T(8,128)(2,1)S(1)} %get-tuple-element.75.refs_1_, bf16[640,1024]{1,0:T(8,128)(2,1)S(1)} %get-tuple-element.70.refs_2_, bf16[2,640,512]{2,1,0:T(8,128)(2,1)S(1)} %get-tuple-element.76.refs_3_, ...), custom_call_target="tpu_custom_call" | custom-call | flops 2013265920 | tf_op jit(solution)/shard_map/grads_given/pallas_call | solution.py:50
  61.1 6.3 %collective-permute-done.17.refs_1_ = bf16[320,1024]{1,0:T(8,128)(2,1)S(1)} collective-permute-done((bf16[320,1024]{1,0:T(8,128)(2,1)S(1)}, bf16[320,1024]{1,0:T(8,128)(2,1)S(1)}, u32[]{:S(2)}, u32[]{:S(2)}) %collective-permute-start.17) | collective-permute-done | bytes 655392 | tf_op jit(solution)/shard_map/ppermute | solution.py:452
  67.5 0.2 add.10
  67.6 0.1 add.11.refs_1_
  67.7 1.3 %collective-permute-start.18 = (bf16[160,1024]{1,0:T(8,128)(2,1)S(1)}, bf16[160,1024]{1,0:T(8,128)(2,1)S(1)}, u32[]{:S(2)}, u32[]{:S(2)}) collective-permute-start(bf16[160,1024]{1,0:T(8,128)(2,1)S(1)} %add.11.refs_1_), channel_id=1, source_target_pairs={{0,4},{4,0},{8,12},{12,8},{16,20},{20,16},{24,28},{28,24},{1,5},{5... | collective-permute-start | bytes 983048 | tf_op jit(solution)/shard_map/ppermute | solution.py:443
  69.0 0.9 collective-permute-start.22
  69.9 0.4 collective-permute-done.18.refs_2_
  70.3 0.3 blend.6
  70.6 1.1 %collective-permute-start.19 = (bf16[40,1024]{1,0:T(8,128)(2,1)S(1)}, bf16[40,1024]{1,0:T(8,128)(2,1)S(1)}, u32[]{:S(2)}, u32[]{:S(2)}) collective-permute-start(bf16[40,1024]{1,0:T(8,128)(2,1)S(1)} %get-tuple-element.81), channel_id=1, source_target_pairs={{0,1},{1,0},{2,3},{3,2},{4,5},{5,4},{6,7},{7,6},{8,9},{9,8},{10,11... | collective-permute-start | bytes 245768 | tf_op jit(solution)/shard_map/ppermute | solution.py:446
  71.7 2.2 %collective-permute-start.20 = (bf16[40,1024]{1,0:T(8,128)(2,1)S(1)}, bf16[40,1024]{1,0:T(8,128)(2,1)S(1)}, u32[]{:S(2)}, u32[]{:S(2)}) collective-permute-start(bf16[40,1024]{1,0:T(8,128)(2,1)S(1)} %get-tuple-element.82), channel_id=1, source_target_pairs={{0,2},{1,3},{2,0},{3,1},{4,6},{5,7},{6,4},{7,5},{8,10},{9,11},{10,... | collective-permute-start | bytes 245768 | tf_op jit(solution)/shard_map/ppermute | solution.py:446
  73.8 1.2 %collective-permute-start.21 = (bf16[40,1024]{1,0:T(8,128)(2,1)S(1)}, bf16[40,1024]{1,0:T(8,128)(2,1)S(1)}, u32[]{:S(2)}, u32[]{:S(2)}) collective-permute-start(bf16[40,1024]{1,0:T(8,128)(2,1)S(1)} %get-tuple-element.83), channel_id=1, source_target_pairs={{0,3},{1,2},{2,1},{3,0},{4,7},{5,6},{6,5},{7,4},{8,11},{9,10},{10,... | collective-permute-start | bytes 245768 | tf_op jit(solution)/shard_map/ppermute | solution.py:446
  75.1 1.0 %collective-permute-done.22.refs_1_ = bf16[160,1024]{1,0:T(8,128)(2,1)S(1)} collective-permute-done((bf16[160,1024]{1,0:T(8,128)(2,1)S(1)}, bf16[160,1024]{1,0:T(8,128)(2,1)S(1)}, u32[]{:S(2)}, u32[]{:S(2)}) %collective-permute-start.22) | collective-permute-done | bytes 327712 | tf_op jit(solution)/shard_map/ppermute | solution.py:452
  76.1 0.1 add.12.refs_6_.refs_1_
  76.2 3.7 %grads_kept.1 = (bf16[2,1024,512]{2,1,0:T(8,128)(2,1)}, bf16[2,1024,512]{2,1,0:T(8,128)(2,1)}, bf16[2,512,1024]{2,1,0:T(8,128)(2,1)}) custom-call(s32[1]{0:T(128)} %bitcast.3.refs_0_.refs_2_, bf16[640,1024]{1,0:T(8,128)(2,1)S(1)} %get-tuple-element.75.refs_1_, bf16[640,1024]{1,0:T(8,128)(2,1)S(1)} %get-tuple-element.70.refs_2_, ...), custom_call_target="tpu_custom_call" | custom-call | flops 2013265920 | tf_op jit(solution)/shard_map/grads_kept/pallas_call | solution.py:50
  79.8 0.1 collective-permute-start.23
  79.9 1.2 %collective-permute-done.20.refs_2_ = bf16[40,1024]{1,0:T(8,128)(2,1)S(1)} collective-permute-done((bf16[40,1024]{1,0:T(8,128)(2,1)S(1)}, bf16[40,1024]{1,0:T(8,128)(2,1)S(1)}, u32[]{:S(2)}, u32[]{:S(2)}) %collective-permute-start.20) | collective-permute-done | bytes 81952 | tf_op jit(solution)/shard_map/ppermute | solution.py:446
  81.2 1.6 %copy-done = bf16[2,1024,512]{2,1,0:T(8,128)(2,1)S(1)} copy-done((bf16[2,1024,512]{2,1,0:T(8,128)(2,1)S(1)}, bf16[2,1024,512]{2,1,0:T(8,128)(2,1)}, u32[]{:S(2)}) %copy-start) | copy-done | bytes 2097176
  82.8 0.3 blend.7
  83.2 0.1 collective-permute-start.27
  83.2 1.5 %collective-permute-start.24 = (bf16[40,1024]{1,0:T(8,128)(2,1)S(1)}, bf16[40,1024]{1,0:T(8,128)(2,1)S(1)}, u32[]{:S(2)}, u32[]{:S(2)}) collective-permute-start(bf16[40,1024]{1,0:T(8,128)(2,1)S(1)} %get-tuple-element.88), channel_id=1, source_target_pairs={{0,1},{1,0},{2,3},{3,2},{4,5},{5,4},{6,7},{7,6},{8,9},{9,8},{10,11... | collective-permute-start | bytes 245768 | tf_op jit(solution)/shard_map/ppermute | solution.py:446
  84.7 1.1 %collective-permute-start.25 = (bf16[40,1024]{1,0:T(8,128)(2,1)S(1)}, bf16[40,1024]{1,0:T(8,128)(2,1)S(1)}, u32[]{:S(2)}, u32[]{:S(2)}) collective-permute-start(bf16[40,1024]{1,0:T(8,128)(2,1)S(1)} %get-tuple-element.89), channel_id=1, source_target_pairs={{0,2},{1,3},{2,0},{3,1},{4,6},{5,7},{6,4},{7,5},{8,10},{9,11},{10,... | collective-permute-start | bytes 245768 | tf_op jit(solution)/shard_map/ppermute | solution.py:446
  85.8 1.9 %collective-permute-start.26 = (bf16[40,1024]{1,0:T(8,128)(2,1)S(1)}, bf16[40,1024]{1,0:T(8,128)(2,1)S(1)}, u32[]{:S(2)}, u32[]{:S(2)}) collective-permute-start(bf16[40,1024]{1,0:T(8,128)(2,1)S(1)} %get-tuple-element.90), channel_id=1, source_target_pairs={{0,3},{1,2},{2,1},{3,0},{4,7},{5,6},{6,5},{7,4},{8,11},{9,10},{10,... | collective-permute-start | bytes 245768 | tf_op jit(solution)/shard_map/ppermute | solution.py:446
  87.7 0.9 combine.2
  88.6 0.3 collective-permute-done.27.refs_1_
  88.9 1.7 %finish.1 = (bf16[2,1024,512]{2,1,0:T(8,128)(2,1)}, bf16[2,1024,512]{2,1,0:T(8,128)(2,1)}, bf16[2,512,1024]{2,1,0:T(8,128)(2,1)}) custom-call(s32[1]{0:T(128)} %bitcast.3.refs_0_.refs_2_, bf16[3,1024,512]{2,1,0:T(8,128)(2,1)S(1)} %collective-permute-done.27.refs_1_, ...), custom_call_target="tpu_custom_call", output_to_operand_aliasing={{0}: (2, {}), {1}: (3, {}), {2}: (4, {})} | custom-call | tf_op jit(solution)/shard_map/finish/pallas_call | solution.py:50
  90.6 3.7 %collective-permute-done.25.refs_3_ = bf16[40,1024]{1,0:T(8,128)(2,1)S(1)} collective-permute-done((bf16[40,1024]{1,0:T(8,128)(2,1)S(1)}, bf16[40,1024]{1,0:T(8,128)(2,1)S(1)}, u32[]{:S(2)}, u32[]{:S(2)}) %collective-permute-start.25) | collective-permute-done | bytes 81952 | tf_op jit(solution)/shard_map/ppermute | solution.py:446
  94.3 1.6 %copy-done.1 = bf16[2,1024,512]{2,1,0:T(8,128)(2,1)S(1)} copy-done((bf16[2,1024,512]{2,1,0:T(8,128)(2,1)S(1)}, bf16[2,1024,512]{2,1,0:T(8,128)(2,1)}, u32[]{:S(2)}) %copy-start.1) | copy-done | bytes 2097176
  95.9 0.9 combine.3
  (32 shorter events, 0.2 us)
Async XLA Ops:
  0.6 27.0 %copy-start.2 = (bf16[2,1024,512]{2,1,0:T(8,128)(2,1)S(1)}, bf16[2,1024,512]{2,1,0:T(8,128)(2,1)}, u32[]{:S(2)}) copy-start(bf16[2,1024,512]{2,1,0:T(8,128)(2,1)} %refs_3_.5) | copy-start | bytes 6291460
  0.6 1.1 %copy-start.5 = (bf16[64,1024]{1,0:T(8,128)(2,1)S(1)}, bf16[64,1024]{1,0:T(8,128)(2,1)}, u32[]{:S(2)}) copy-start(bf16[64,1024]{1,0:T(8,128)(2,1)} %refs_2_.1) | copy-start | bytes 393220
  1.7 0.7 copy-start.7
  2.9 2.8 %collective-permute-start = (bf16[160,1024]{1,0:T(8,128)(2,1)S(1)}, bf16[160,1024]{1,0:T(8,128)(2,1)S(1)}, u32[]{:S(2)}, u32[]{:S(2)}) collective-permute-start(bf16[160,1024]{1,0:T(8,128)(2,1)S(1)} %get-tuple-element.51.refs_4_.refs_1_), channel_id=1, source_target_pairs={{0,4},{4,0},{8,12},{12,8},{16,20},{20,16},{24,28},{28,24},{1,5},{5... | collective-permute-start | bytes 983048 | tf_op jit(solution)/shard_map/ppermute | solution.py:443
  3.5 0.9 copy-start.6
  4.4 0.7 copy-start.8
  5.6 6.2 %collective-permute-start.4 = (bf16[160,1024]{1,0:T(8,128)(2,1)S(1)}, bf16[160,1024]{1,0:T(8,128)(2,1)S(1)}, u32[]{:S(2)}, u32[]{:S(2)}) collective-permute-start(bf16[160,1024]{1,0:T(8,128)(2,1)S(1)} %get-tuple-element.58.refs_1_), channel_id=1, source_target_pairs={{0,4},{4,0},{8,12},{12,8},{16,20},{20,16},{24,28},{28,24},{1,5},{5... | collective-permute-start | bytes 983048 | tf_op jit(solution)/shard_map/ppermute | solution.py:443
  6.1 6.0 %collective-permute-start.1 = (bf16[40,1024]{1,0:T(8,128)(2,1)S(1)}, bf16[40,1024]{1,0:T(8,128)(2,1)S(1)}, u32[]{:S(2)}, u32[]{:S(2)}) collective-permute-start(bf16[40,1024]{1,0:T(8,128)(2,1)S(1)} %get-tuple-element.55), channel_id=1, source_target_pairs={{0,1},{1,0},{2,3},{3,2},{4,5},{5,4},{6,7},{7,6},{8,9},{9,8},{10,11... | collective-permute-start | bytes 245768 | tf_op jit(solution)/shard_map/ppermute | solution.py:446
  9.2 9.4 %collective-permute-start.2 = (bf16[40,1024]{1,0:T(8,128)(2,1)S(1)}, bf16[40,1024]{1,0:T(8,128)(2,1)S(1)}, u32[]{:S(2)}, u32[]{:S(2)}) collective-permute-start(bf16[40,1024]{1,0:T(8,128)(2,1)S(1)} %get-tuple-element.56), channel_id=1, source_target_pairs={{0,2},{1,3},{2,0},{3,1},{4,6},{5,7},{6,4},{7,5},{8,10},{9,11},{10,... | collective-permute-start | bytes 245768 | tf_op jit(solution)/shard_map/ppermute | solution.py:446
  11.8 6.8 %collective-permute-start.3 = (bf16[40,1024]{1,0:T(8,128)(2,1)S(1)}, bf16[40,1024]{1,0:T(8,128)(2,1)S(1)}, u32[]{:S(2)}, u32[]{:S(2)}) collective-permute-start(bf16[40,1024]{1,0:T(8,128)(2,1)S(1)} %get-tuple-element.57), channel_id=1, source_target_pairs={{0,3},{1,2},{2,1},{3,0},{4,7},{5,6},{6,5},{7,4},{8,11},{9,10},{10,... | collective-permute-start | bytes 245768 | tf_op jit(solution)/shard_map/ppermute | solution.py:446
  18.6 7.3 %collective-permute-start.5 = (bf16[160,1024]{1,0:T(8,128)(2,1)S(1)}, bf16[160,1024]{1,0:T(8,128)(2,1)S(1)}, u32[]{:S(2)}, u32[]{:S(2)}) collective-permute-start(bf16[160,1024]{1,0:T(8,128)(2,1)S(1)} %join.5.refs_0_.refs_4_), channel_id=1, source_target_pairs={{0,8},{4,20},{8,0},{12,28},{16,24},{20,4},{24,16},{28,12},{1,9},{5... | collective-permute-start | bytes 983048 | tf_op jit(solution)/shard_map/ppermute | solution.py:452
  20.2 7.4 %collective-permute-start.11 = (bf16[40,1024]{1,0:T(8,128)(2,1)S(1)}, bf16[40,1024]{1,0:T(8,128)(2,1)S(1)}, u32[]{:S(2)}, u32[]{:S(2)}) collective-permute-start(bf16[40,1024]{1,0:T(8,128)(2,1)S(1)} %get-tuple-element.65), channel_id=1, source_target_pairs={{0,1},{1,0},{2,3},{3,2},{4,5},{5,4},{6,7},{7,6},{8,9},{9,8},{10,11... | collective-permute-start | bytes 245768 | tf_op jit(solution)/shard_map/ppermute | solution.py:446
  21.7 8.2 %collective-permute-start.12 = (bf16[40,1024]{1,0:T(8,128)(2,1)S(1)}, bf16[40,1024]{1,0:T(8,128)(2,1)S(1)}, u32[]{:S(2)}, u32[]{:S(2)}) collective-permute-start(bf16[40,1024]{1,0:T(8,128)(2,1)S(1)} %get-tuple-element.66), channel_id=1, source_target_pairs={{0,2},{1,3},{2,0},{3,1},{4,6},{5,7},{6,4},{7,5},{8,10},{9,11},{10,... | collective-permute-start | bytes 245768 | tf_op jit(solution)/shard_map/ppermute | solution.py:446
  23.2 6.7 %collective-permute-start.13 = (bf16[40,1024]{1,0:T(8,128)(2,1)S(1)}, bf16[40,1024]{1,0:T(8,128)(2,1)S(1)}, u32[]{:S(2)}, u32[]{:S(2)}) collective-permute-start(bf16[40,1024]{1,0:T(8,128)(2,1)S(1)} %get-tuple-element.67), channel_id=1, source_target_pairs={{0,3},{1,2},{2,1},{3,0},{4,7},{5,6},{6,5},{7,4},{8,11},{9,10},{10,... | collective-permute-start | bytes 245768 | tf_op jit(solution)/shard_map/ppermute | solution.py:446
  26.0 14.2 %copy-start.3 = (bf16[2,1024,512]{2,1,0:T(8,128)(2,1)S(1)}, bf16[2,1024,512]{2,1,0:T(8,128)(2,1)}, u32[]{:S(2)}) copy-start(bf16[2,1024,512]{2,1,0:T(8,128)(2,1)} %refs_4_.3) | copy-start | bytes 6291460
  26.0 14.2 %copy-start.4 = (bf16[2,512,1024]{2,1,0:T(8,128)(2,1)S(1)}, bf16[2,512,1024]{2,1,0:T(8,128)(2,1)}, u32[]{:S(2)}) copy-start(bf16[2,512,1024]{2,1,0:T(8,128)(2,1)} %refs_5_.3) | copy-start | bytes 6291460
  26.0 14.2 %collective-permute-start.6 = (bf16[320,1024]{1,0:T(8,128)(2,1)S(1)}, bf16[320,1024]{1,0:T(8,128)(2,1)S(1)}, u32[]{:S(2)}, u32[]{:S(2)}) collective-permute-start(bf16[320,1024]{1,0:T(8,128)(2,1)S(1)} %join.6.refs_0_.refs_2_), channel_id=1, source_target_pairs={{0,16},{4,12},{8,24},{12,4},{16,0},{20,28},{24,8},{28,20},{1,17},{... | collective-permute-start | bytes 1966088 | tf_op jit(solution)/shard_map/ppermute | solution.py:452
  27.6 12.6 %collective-permute-start.7 = (bf16[2,1024,512]{2,1,0:T(8,128)(2,1)S(1)}, bf16[2,1024,512]{2,1,0:T(8,128)(2,1)S(1)}, u32[]{:S(2)}, u32[]{:S(2)}) collective-permute-start(bf16[2,1024,512]{2,1,0:T(8,128)(2,1)S(1)} %copy-done.2), channel_id=1, source_target_pairs={{0,4},{4,0},{8,12},{12,8},{16,20},{20,16},{24,28},{28,24},{1,5},{5... | collective-permute-start | bytes 6291464 | tf_op jit(solution)/shard_map/ppermute | solution.py:443
  27.6 12.6 %collective-permute-start.8 = (bf16[2,1024,512]{2,1,0:T(8,128)(2,1)}, bf16[2,1024,512]{2,1,0:T(8,128)(2,1)S(1)}, u32[]{:S(2)}, u32[]{:S(2)}) collective-permute-start(bf16[2,1024,512]{2,1,0:T(8,128)(2,1)} %refs_4_.3), channel_id=1, source_target_pairs={{0,4},{4,0},{8,12},{12,8},{16,20},{20,16},{24,28},{28,24},{1,5},{5... | collective-permute-start | bytes 6291464 | tf_op jit(solution)/shard_map/ppermute | solution.py:443
  29.9 10.3 %collective-permute-start.9 = (bf16[2,512,1024]{2,1,0:T(8,128)(2,1)}, bf16[2,512,1024]{2,1,0:T(8,128)(2,1)S(1)}, u32[]{:S(2)}, u32[]{:S(2)}) collective-permute-start(bf16[2,512,1024]{2,1,0:T(8,128)(2,1)} %refs_5_.3), channel_id=1, source_target_pairs={{0,4},{4,0},{8,12},{12,8},{16,20},{20,16},{24,28},{28,24},{1,5},{5... | collective-permute-start | bytes 6291464 | tf_op jit(solution)/shard_map/ppermute | solution.py:443
  29.9 7.1 %collective-permute-start.14 = (bf16[160,1024]{1,0:T(8,128)(2,1)S(1)}, bf16[160,1024]{1,0:T(8,128)(2,1)S(1)}, u32[]{:S(2)}, u32[]{:S(2)}) collective-permute-start(bf16[160,1024]{1,0:T(8,128)(2,1)S(1)} %join.7.refs_0_), channel_id=1, source_target_pairs={{0,8},{4,20},{8,0},{12,28},{16,24},{20,4},{24,16},{28,12},{1,9},{5... | collective-permute-start | bytes 983048 | tf_op jit(solution)/shard_map/ppermute | solution.py:452
  37.1 10.7 %collective-permute-start.15 = (bf16[320,1024]{1,0:T(8,128)(2,1)S(1)}, bf16[320,1024]{1,0:T(8,128)(2,1)S(1)}, u32[]{:S(2)}, u32[]{:S(2)}) collective-permute-start(bf16[320,1024]{1,0:T(8,128)(2,1)S(1)} %join.8.refs_0_), channel_id=1, source_target_pairs={{0,16},{4,12},{8,24},{12,4},{16,0},{20,28},{24,8},{28,20},{1,17},{... | collective-permute-start | bytes 1966088 | tf_op jit(solution)/shard_map/ppermute | solution.py:452
  46.1 10.7 %collective-permute-start.10 = (bf16[320,1024]{1,0:T(8,128)(2,1)S(1)}, bf16[320,1024]{1,0:T(8,128)(2,1)S(1)}, u32[]{:S(2)}, u32[]{:S(2)}) collective-permute-start(bf16[320,1024]{1,0:T(8,128)(2,1)S(1)} %get-tuple-element.64), channel_id=1, source_target_pairs={{0,16},{4,12},{8,24},{12,4},{16,0},{20,28},{24,8},{28,20},{1,17},{... | collective-permute-start | bytes 1966088 | tf_op jit(solution)/shard_map/ppermute | solution.py:452
  53.3 14.2 %collective-permute-start.17 = (bf16[320,1024]{1,0:T(8,128)(2,1)S(1)}, bf16[320,1024]{1,0:T(8,128)(2,1)S(1)}, u32[]{:S(2)}, u32[]{:S(2)}) collective-permute-start(bf16[320,1024]{1,0:T(8,128)(2,1)S(1)} %get-tuple-element.74), channel_id=1, source_target_pairs={{0,16},{4,12},{8,24},{12,4},{16,0},{20,28},{24,8},{28,20},{1,17},{... | collective-permute-start | bytes 1966088 | tf_op jit(solution)/shard_map/ppermute | solution.py:452
  56.9 10.7 %collective-permute-start.16 = (bf16[160,1024]{1,0:T(8,128)(2,1)S(1)}, bf16[160,1024]{1,0:T(8,128)(2,1)S(1)}, u32[]{:S(2)}, u32[]{:S(2)}) collective-permute-start(bf16[160,1024]{1,0:T(8,128)(2,1)S(1)} %get-tuple-element.72.refs_6_), channel_id=1, source_target_pairs={{0,8},{4,20},{8,0},{12,28},{16,24},{20,4},{24,16},{28,12},{1,9},{5... | collective-permute-start | bytes 983048 | tf_op jit(solution)/shard_map/ppermute | solution.py:452
  67.7 2.5 %collective-permute-start.18 = (bf16[160,1024]{1,0:T(8,128)(2,1)S(1)}, bf16[160,1024]{1,0:T(8,128)(2,1)S(1)}, u32[]{:S(2)}, u32[]{:S(2)}) collective-permute-start(bf16[160,1024]{1,0:T(8,128)(2,1)S(1)} %add.11.refs_1_), channel_id=1, source_target_pairs={{0,4},{4,0},{8,12},{12,8},{16,20},{20,16},{24,28},{28,24},{1,5},{5... | collective-permute-start | bytes 983048 | tf_op jit(solution)/shard_map/ppermute | solution.py:443
  69.0 7.1 %collective-permute-start.22 = (bf16[160,1024]{1,0:T(8,128)(2,1)S(1)}, bf16[160,1024]{1,0:T(8,128)(2,1)S(1)}, u32[]{:S(2)}, u32[]{:S(2)}) collective-permute-start(bf16[160,1024]{1,0:T(8,128)(2,1)S(1)} %get-tuple-element.79.refs_2_), channel_id=1, source_target_pairs={{0,8},{4,20},{8,0},{12,28},{16,24},{20,4},{24,16},{28,12},{1,9},{5... | collective-permute-start | bytes 983048 | tf_op jit(solution)/shard_map/ppermute | solution.py:452
  70.6 9.3 %collective-permute-start.19 = (bf16[40,1024]{1,0:T(8,128)(2,1)S(1)}, bf16[40,1024]{1,0:T(8,128)(2,1)S(1)}, u32[]{:S(2)}, u32[]{:S(2)}) collective-permute-start(bf16[40,1024]{1,0:T(8,128)(2,1)S(1)} %get-tuple-element.81), channel_id=1, source_target_pairs={{0,1},{1,0},{2,3},{3,2},{4,5},{5,4},{6,7},{7,6},{8,9},{9,8},{10,11... | collective-permute-start | bytes 245768 | tf_op jit(solution)/shard_map/ppermute | solution.py:446
  71.7 9.5 %collective-permute-start.20 = (bf16[40,1024]{1,0:T(8,128)(2,1)S(1)}, bf16[40,1024]{1,0:T(8,128)(2,1)S(1)}, u32[]{:S(2)}, u32[]{:S(2)}) collective-permute-start(bf16[40,1024]{1,0:T(8,128)(2,1)S(1)} %get-tuple-element.82), channel_id=1, source_target_pairs={{0,2},{1,3},{2,0},{3,1},{4,6},{5,7},{6,4},{7,5},{8,10},{9,11},{10,... | collective-permute-start | bytes 245768 | tf_op jit(solution)/shard_map/ppermute | solution.py:446
  73.8 7.3 %collective-permute-start.21 = (bf16[40,1024]{1,0:T(8,128)(2,1)S(1)}, bf16[40,1024]{1,0:T(8,128)(2,1)S(1)}, u32[]{:S(2)}, u32[]{:S(2)}) collective-permute-start(bf16[40,1024]{1,0:T(8,128)(2,1)S(1)} %get-tuple-element.83), channel_id=1, source_target_pairs={{0,3},{1,2},{2,1},{3,0},{4,7},{5,6},{6,5},{7,4},{8,11},{9,10},{10,... | collective-permute-start | bytes 245768 | tf_op jit(solution)/shard_map/ppermute | solution.py:446
  79.8 2.9 %collective-permute-start.23 = (bf16[160,1024]{1,0:T(8,128)(2,1)S(1)}, bf16[160,1024]{1,0:T(8,128)(2,1)S(1)}, u32[]{:S(2)}, u32[]{:S(2)}) collective-permute-start(bf16[160,1024]{1,0:T(8,128)(2,1)S(1)} %add.12.refs_6_.refs_1_), channel_id=1, source_target_pairs={{0,4},{4,0},{8,12},{12,8},{16,20},{20,16},{24,28},{28,24},{1,5},{5... | collective-permute-start | bytes 983048 | tf_op jit(solution)/shard_map/ppermute | solution.py:443
  81.2 1.6 %copy-start = (bf16[2,1024,512]{2,1,0:T(8,128)(2,1)S(1)}, bf16[2,1024,512]{2,1,0:T(8,128)(2,1)}, u32[]{:S(2)}) copy-start(bf16[2,1024,512]{2,1,0:T(8,128)(2,1)} %get-tuple-element.85.refs_4_.refs_2_) | copy-start | bytes 6291460
  83.2 5.7 %collective-permute-start.27 = (bf16[3,1024,512]{2,1,0:T(8,128)(2,1)S(1)}, bf16[3,1024,512]{2,1,0:T(8,128)(2,1)S(1)}, u32[]{:S(2)}, u32[]{:S(2)}) collective-permute-start(bf16[3,1024,512]{2,1,0:T(8,128)(2,1)S(1)} %grads_given.1.refs_2_), channel_id=1, source_target_pairs={{0,4},{4,0},{8,12},{12,8},{16,20},{20,16},{24,28},{28,24},{1,5},{5... | collective-permute-start | bytes 9437192 | tf_op jit(solution)/shard_map/ppermute | solution.py:443
  83.2 7.4 %collective-permute-start.24 = (bf16[40,1024]{1,0:T(8,128)(2,1)S(1)}, bf16[40,1024]{1,0:T(8,128)(2,1)S(1)}, u32[]{:S(2)}, u32[]{:S(2)}) collective-permute-start(bf16[40,1024]{1,0:T(8,128)(2,1)S(1)} %get-tuple-element.88), channel_id=1, source_target_pairs={{0,1},{1,0},{2,3},{3,2},{4,5},{5,4},{6,7},{7,6},{8,9},{9,8},{10,11... | collective-permute-start | bytes 245768 | tf_op jit(solution)/shard_map/ppermute | solution.py:446
  84.7 9.6 %collective-permute-start.25 = (bf16[40,1024]{1,0:T(8,128)(2,1)S(1)}, bf16[40,1024]{1,0:T(8,128)(2,1)S(1)}, u32[]{:S(2)}, u32[]{:S(2)}) collective-permute-start(bf16[40,1024]{1,0:T(8,128)(2,1)S(1)} %get-tuple-element.89), channel_id=1, source_target_pairs={{0,2},{1,3},{2,0},{3,1},{4,6},{5,7},{6,4},{7,5},{8,10},{9,11},{10,... | collective-permute-start | bytes 245768 | tf_op jit(solution)/shard_map/ppermute | solution.py:446
  85.8 8.5 %collective-permute-start.26 = (bf16[40,1024]{1,0:T(8,128)(2,1)S(1)}, bf16[40,1024]{1,0:T(8,128)(2,1)S(1)}, u32[]{:S(2)}, u32[]{:S(2)}) collective-permute-start(bf16[40,1024]{1,0:T(8,128)(2,1)S(1)} %get-tuple-element.90), channel_id=1, source_target_pairs={{0,3},{1,2},{2,1},{3,0},{4,7},{5,6},{6,5},{7,4},{8,11},{9,10},{10,... | collective-permute-start | bytes 245768 | tf_op jit(solution)/shard_map/ppermute | solution.py:446
  94.3 1.6 %copy-start.1 = (bf16[2,1024,512]{2,1,0:T(8,128)(2,1)S(1)}, bf16[2,1024,512]{2,1,0:T(8,128)(2,1)}, u32[]{:S(2)}) copy-start(bf16[2,1024,512]{2,1,0:T(8,128)(2,1)} %get-tuple-element.48.refs_5_) | copy-start | bytes 6291460

commit v4 on v3

--- a/solution.py
+++ b/solution.py
@@ -26,6 +26,9 @@
 
 def shaped(*shape):
     return jax.ShapeDtypeStruct(shape, BF)
+
+
+TOKEN = shaped(16, 128)
 
 
 def kernel_call(
@@ -191,10 +194,6 @@
     )(*parts)
 
 
-def fetch(core, weights, held, sems):
-    return start_all([(w.at[core[0]], h) for w, h in zip(weights, held)], sems)
-
-
 def gather_rows(parts, out):
     first = 0
     for part in parts:
@@ -219,18 +218,14 @@
 
 def forward_kernel(low, high, core, *refs):
     ps = refs[6:8]
-    x, f1, f2, hid, g0, u0, d0, g1, u1, d1, gate_s, up_s, sems = refs[8:]
-    own, other = refs[:3], refs[3:6]
-    sources = (own[0], own[1], other[0], other[1], own[2], other[2])
-    loads = fetch(core, sources, (g0, u0, g1, u1, d0, d1), sems)
+    x, f1, f2, hid, gate_s, up_s = refs[8:]
+    g0, u0, d0, g1, u1, d1 = (w.at[core[0]] for w in refs[:6])
     gather_rows((low, high), x)
     weights = ((g0, u0, d0), (g1, u1, d1))
     hidden = g0.shape[1]
     rows, width = x.shape
     turn = 0
     for half, (a, b, _) in enumerate(weights):
-        loads[2 * half].wait()
-        loads[2 * half + 1].wait()
         for cols in chunks(hidden, tile_of(hidden)):
             gate_s[turn] = dot(x[...], a[:, cols])
             up_s[turn] = dot(x[...], b[:, cols])
@@ -242,8 +237,6 @@
                 f1[half, r, cols] = (up * sig * (1.0 + gate * (1.0 - sig))).astype(BF)
                 f2[half, r, cols] = act.astype(BF)
             turn = 1 - turn
-    loads[4].wait()
-    loads[5].wait()
     for cols in chunks(width, tile_of(width)):
         total = dot(hid[0], d0[:, cols]) + dot(hid[1], d1[:, cols])
         scatter_rows(total, ps, cols)
@@ -256,12 +249,10 @@
     out = kernel_call(
         forward_kernel,
         "forward",
-        [VMEM] * 2 + [SMEM] + [HBM] * 6,
+        [VMEM] * 2 + [SMEM] + [VMEM] * 6,
         [VMEM] * 6,
         [shaped(size, width)] * 2 + [shaped(rows, width)] + [shaped(2, rows, hidden)] * 3,
-        [pltpu.VMEM(w.shape[1:], BF) for w in own + own]
-        + [pltpu.VMEM((2, rows, tile_of(hidden)), F32)] * 2
-        + [pltpu.SemaphoreType.DMA((6,))],
+        [pltpu.VMEM((2, rows, tile_of(hidden)), F32)] * 2,
         limit=32,
         flops=12 * rows * width * hidden,
     )(*xs, core, *own, *other)
@@ -270,16 +261,13 @@
 
 def backward_kernel(low, high, core, *refs):
     f1, f2, qs = refs[6], refs[7], refs[8:10]
-    dy, dg, du, g0, u0, d0, g1, u1, d1, da_s, sems = refs[10:]
-    own, other = refs[:3], refs[3:6]
-    sources = (own[2], other[2], own[0], own[1], other[0], other[1])
-    loads = fetch(core, sources, (d0, d1, g0, u0, g1, u1), sems)
+    dy, dg, du, da_s = refs[10:]
+    g0, u0, d0, g1, u1, d1 = (w.at[core[0]] for w in refs[:6])
     gather_rows((low, high), dy)
     hidden = g0.shape[1]
     rows, width = dy.shape
     turn = 0
     for half, a in enumerate((d0, d1)):
-        loads[half].wait()
         for cols in chunks(hidden, tile_of(hidden)):
             da_s[turn] = dot(dy[...], a[cols, :], NT)
             for r in chunks(rows, 64):
@@ -287,8 +275,6 @@
                 dg[half, r, cols] = (da * f1[half, r, cols].astype(F32)).astype(BF)
                 du[half, r, cols] = (da * f2[half, r, cols].astype(F32)).astype(BF)
             turn = 1 - turn
-    for c in loads[2:]:
-        c.wait()
     for cols in chunks(width, tile_of(width)):
         total = dot(dg[0], g0[cols, :], NT) + dot(du[0], u0[cols, :], NT)
         total = total + dot(dg[1], g1[cols, :], NT) + dot(du[1], u1[cols, :], NT)
@@ -302,12 +288,10 @@
     out = kernel_call(
         backward_kernel,
         "backward",
-        [VMEM] * 2 + [SMEM] + [HBM] * 6 + [VMEM] * 2,
+        [VMEM] * 2 + [SMEM] + [VMEM] * 8,
         [VMEM] * 5,
         [shaped(size, width)] * 2 + [shaped(rows, width)] + [shaped(2, rows, hidden)] * 2,
-        [pltpu.VMEM(w.shape[1:], BF) for w in own + own]
-        + [pltpu.VMEM((2, rows, tile_of(hidden)), F32)]
-        + [pltpu.SemaphoreType.DMA((6,))],
+        [pltpu.VMEM((2, rows, tile_of(hidden)), F32)],
         limit=32,
         flops=12 * rows * width * hidden,
     )(*dys, core, *own, *other, f1, f2)
@@ -315,6 +299,8 @@
 
 
 def grads_kernel(half, core, x, dy, dg, du, hid, *refs):
+    *refs, token = refs if half else (*refs[:3], *refs[4:], refs[3])
+    token[...] = jnp.zeros(token.shape, BF)
     outs = [refs[0].at[i] for i in range(3)] if half else refs[3:6]
     hidden = dg.shape[2]
     width = x.shape[1]
@@ -355,8 +341,8 @@
         functools.partial(grads_kernel, half),
         "grads_given" if half else "grads_kept",
         [SMEM] + [VMEM] * 5,
-        [VMEM if half else HBM] * len(outs),
-        outs,
+        [VMEM if half else HBM] * len(outs) + [VMEM],
+        outs + [TOKEN],
         scratch,
         limit=32,
         flops=6 * rows * width * hidden,
@@ -365,7 +351,8 @@
 
 
 def finish_kernel(core, got, *refs):
-    outs, down, sems = refs[3:6], refs[6], refs[7]
+    outs, token, down, sems = refs[3:6], refs[6], refs[7], refs[8]
+    token[...] = jnp.zeros(token.shape, BF)
     place = 1 - core[0]
     copies = start_all([(got.at[i], outs[i].at[place]) for i in range(2)], sems)
     down[...] = got[2].T
@@ -374,16 +361,17 @@
         c.wait()
 
 
-def finish(core, got, kept):
+def finish(core, got, kept, after):
     return kernel_call(
         finish_kernel,
         "finish",
         [SMEM, VMEM] + [HBM] * 3,
-        [HBM] * 3,
-        [shaped(*k.shape) for k in kept],
+        [HBM] * 3 + [VMEM],
+        [shaped(*k.shape) for k in kept] + [TOKEN],
         [pltpu.VMEM(kept[2].shape[1:], BF), pltpu.SemaphoreType.DMA((3,))],
         limit=14,
         alias={2: 0, 3: 1, 4: 2},
+        after=after,
     )(core, got, *kept)
 
 
@@ -483,18 +471,18 @@
     ps, x, f1, f2, hid = forward(core, (x_low, x_high), own, other)
     qs, dy, dg, du = backward(core, (dy_low, dy_high), own, other, f1, f2)
     p_low, p_high = reduce(*ps, [dy])
-    given = grads(1, core, x, dy, dg, du, hid, local, [p_high])
-    q_low, q_high = reduce(*qs, given[:1])
+    given, token = grads(1, core, x, dy, dg, du, hid, local, [p_high])
+    *kept, token = grads(0, core, x, dy, dg, du, hid, local, [token])
+    q_low, q_high = reduce(*qs, [token])
     p_messages = hand_out(add([p_low, to_chip(p_high, 0)], 1, [q_high])[0])
     q_rows = add([q_low, to_chip(q_high, 0)], 1, p_messages[:1])[0]
-    kept = grads(0, core, x, dy, dg, du, hid, local, [q_rows])
-    p_messages = join(swap(p_messages), kept[:1], 20 * FLOPS_PER_US)
+    p_messages = join(swap(p_messages), [q_rows], 20 * FLOPS_PER_US)
     q_messages = hand_out(q_rows, [p_messages])
     mixed = combine([high, low], [p_messages], q_messages[:1])
-    behind, _ = lax.optimization_barrier((given[0], q_messages[0]))
+    behind, _ = lax.optimization_barrier((given, q_messages[0]))
     got = to_pair(behind)
-    grad_gate, grad_up, grad_down = finish(core, got, kept)
-    grad_tokens = combine([chosen], swap(q_messages), [grad_gate])
+    grad_gate, grad_up, grad_down, token = finish(core, got, kept, [mixed])
+    grad_tokens = combine([chosen], swap(q_messages), [token])
     return (mixed, grad_tokens, grad_gate, grad_up, grad_down)
 
 

time: 97.1 us -> 92.7 us (0.955)
  local copies, waits for them, and re-layouts: 6.51 us -> 4.23 us
  Pallas kernels: 24.4 us -> 22.4 us
    ppermute x12, waiting for transfers between devices: 13.2 us -> 16 us  [to_owner(): return lax.ppermute(a, 'expert', [(i, i ^ j) for i in range(owners)])]
    ppermute x8, waiting for transfers between devices: 18.8 us -> 16 us  [to_chip(): return lax.ppermute(a, 'dp', [(i, i ^ bit(i)) for i in range(devices)])]
    unnamed x18 -> x16, local copies, waits for them, and re-layouts: 6.51 us -> 4.23 us
    pallas_call x22, Pallas kernels: 24.4 us -> 22.4 us  [kernel_call(): return lambda *operands: call(*operands, *after)]
  transfers between devices with their start and end apart: 28 -> 28, of which waited for: 13 -> 15; matrix products, arithmetic and copies ran while one was open for 0% -> 0% of each run, Pallas kernels for 23% -> 22%
where the time goes in v4:
time: 92.7 us; the launch traced here: 92.5 us
  starting transfers between devices  32.6 us (35%)
  waiting for transfers between devices  32.4 us (35%)
  Pallas kernels  22.4 us (24%)
  local copies, waits for them, and re-layouts  4.23 us (5%)
    pallas_call x22, Pallas kernels, kernel_call(): return lambda *operands: call(*operands, *after)  22.4 us
    ppermute x12, starting transfers between devices, to_owner(): return lax.ppermute(a, 'expert', [(i, i ^ j) for i in range(owners)])  19 us
    ppermute x12, waiting for transfers between devices, to_owner(): return lax.ppermute(a, 'expert', [(i, i ^ j) for i in range(owners)])  16 us
    ppermute x8, waiting for transfers between devices, to_chip(): return lax.ppermute(a, 'dp', [(i, i ^ bit(i)) for i in range(devices)])  16 us
    ppermute x8, starting transfers between devices, to_chip(): return lax.ppermute(a, 'dp', [(i, i ^ bit(i)) for i in range(devices)])  11.2 us
    unnamed x16, local copies, waits for them, and re-layouts  4.23 us
    ppermute x8, starting transfers between devices, to_pair(): return lax.ppermute(a, 'dp', [(i, i ^ 1) for i in range(devices)])  2.47 us
  transfers between devices with their start and end apart: 28, of which 15 were waited for; matrix products, arithmetic and copies ran while one was open for 0% of the time, Pallas kernels for 22%

profile of v4, /device:TPU:0, one launch (start us, length us, event | category | flops | bytes accessed | tf_op | source)
XLA Modules:
  0.0 92.5 jit_solution(11525179129100077913)
XLA Ops:
  0.7 1.0 %copy-done.4 = bf16[64,1024]{1,0:T(8,128)(2,1)S(1)} copy-done((bf16[64,1024]{1,0:T(8,128)(2,1)S(1)}, bf16[64,1024]{1,0:T(8,128)(2,1)}, u32[]{:S(2)}) %copy-start.4) | copy-done | bytes 131096
  1.7 0.7 copy-done.6
  2.4 0.6 place_rows.1
  2.9 0.5 collective-permute-start
  3.5 0.9 copy-done.5
  4.4 0.7 copy-done.7
  5.0 0.6 place_scaled.1
  5.6 0.1 collective-permute-start.4
  5.8 0.3 blend.4
  6.1 3.1 %collective-permute-start.1 = (bf16[40,1024]{1,0:T(8,128)(2,1)S(1)}, bf16[40,1024]{1,0:T(8,128)(2,1)S(1)}, u32[]{:S(2)}, u32[]{:S(2)}) collective-permute-start(bf16[40,1024]{1,0:T(8,128)(2,1)S(1)} %get-tuple-element.59), channel_id=1, source_target_pairs={{0,1},{1,0},{2,3},{3,2},{4,5},{5,4},{6,7},{7,6},{8,9},{9,8},{10,11... | collective-permute-start | bytes 245768 | tf_op jit(solution)/shard_map/ppermute | solution.py:434
  9.2 2.6 %collective-permute-start.2 = (bf16[40,1024]{1,0:T(8,128)(2,1)S(1)}, bf16[40,1024]{1,0:T(8,128)(2,1)S(1)}, u32[]{:S(2)}, u32[]{:S(2)}) collective-permute-start(bf16[40,1024]{1,0:T(8,128)(2,1)S(1)} %get-tuple-element.60), channel_id=1, source_target_pairs={{0,2},{1,3},{2,0},{3,1},{4,6},{5,7},{6,4},{7,5},{8,10},{9,11},{10,... | collective-permute-start | bytes 245768 | tf_op jit(solution)/shard_map/ppermute | solution.py:434
  11.8 0.3 blend.5
  12.1 6.5 %collective-permute-done.2.refs_2_ = bf16[40,1024]{1,0:T(8,128)(2,1)S(1)} collective-permute-done((bf16[40,1024]{1,0:T(8,128)(2,1)S(1)}, bf16[40,1024]{1,0:T(8,128)(2,1)S(1)}, u32[]{:S(2)}, u32[]{:S(2)}) %collective-permute-start.2) | collective-permute-done | bytes 81952 | tf_op jit(solution)/shard_map/ppermute | solution.py:434
  18.6 1.6 %collective-permute-start.5 = (bf16[160,1024]{1,0:T(8,128)(2,1)S(1)}, bf16[160,1024]{1,0:T(8,128)(2,1)S(1)}, u32[]{:S(2)}, u32[]{:S(2)}) collective-permute-start(bf16[160,1024]{1,0:T(8,128)(2,1)S(1)} %join.5.refs_0_.refs_4_), channel_id=1, source_target_pairs={{0,8},{4,20},{8,0},{12,28},{16,24},{20,4},{24,16},{28,12},{1,9},{5... | collective-permute-start | bytes 983048 | tf_op jit(solution)/shard_map/ppermute | solution.py:440
  20.2 1.5 %collective-permute-start.11 = (bf16[40,1024]{1,0:T(8,128)(2,1)S(1)}, bf16[40,1024]{1,0:T(8,128)(2,1)S(1)}, u32[]{:S(2)}, u32[]{:S(2)}) collective-permute-start(bf16[40,1024]{1,0:T(8,128)(2,1)S(1)} %get-tuple-element.69), channel_id=1, source_target_pairs={{0,1},{1,0},{2,3},{3,2},{4,5},{5,4},{6,7},{7,6},{8,9},{9,8},{10,11... | collective-permute-start | bytes 245768 | tf_op jit(solution)/shard_map/ppermute | solution.py:434
  21.7 1.5 %collective-permute-start.12 = (bf16[40,1024]{1,0:T(8,128)(2,1)S(1)}, bf16[40,1024]{1,0:T(8,128)(2,1)S(1)}, u32[]{:S(2)}, u32[]{:S(2)}) collective-permute-start(bf16[40,1024]{1,0:T(8,128)(2,1)S(1)} %get-tuple-element.70), channel_id=1, source_target_pairs={{0,2},{1,3},{2,0},{3,1},{4,6},{5,7},{6,4},{7,5},{8,10},{9,11},{10,... | collective-permute-start | bytes 245768 | tf_op jit(solution)/shard_map/ppermute | solution.py:434
  23.2 1.4 %collective-permute-start.13 = (bf16[40,1024]{1,0:T(8,128)(2,1)S(1)}, bf16[40,1024]{1,0:T(8,128)(2,1)S(1)}, u32[]{:S(2)}, u32[]{:S(2)}) collective-permute-start(bf16[40,1024]{1,0:T(8,128)(2,1)S(1)} %get-tuple-element.71), channel_id=1, source_target_pairs={{0,3},{1,2},{2,1},{3,0},{4,7},{5,6},{6,5},{7,4},{8,11},{9,10},{10,... | collective-permute-start | bytes 245768 | tf_op jit(solution)/shard_map/ppermute | solution.py:434
  24.6 1.4 %collective-permute-done.5.refs_1_ = bf16[160,1024]{1,0:T(8,128)(2,1)S(1)} collective-permute-done((bf16[160,1024]{1,0:T(8,128)(2,1)S(1)}, bf16[160,1024]{1,0:T(8,128)(2,1)S(1)}, u32[]{:S(2)}, u32[]{:S(2)}) %collective-permute-start.5) | collective-permute-done | bytes 327712 | tf_op jit(solution)/shard_map/ppermute | solution.py:440
  26.0 0.0 copy-start.1
  26.0 0.0 copy-start.2
  26.0 1.6 %collective-permute-start.6 = (bf16[320,1024]{1,0:T(8,128)(2,1)S(1)}, bf16[320,1024]{1,0:T(8,128)(2,1)S(1)}, u32[]{:S(2)}, u32[]{:S(2)}) collective-permute-start(bf16[320,1024]{1,0:T(8,128)(2,1)S(1)} %join.6.refs_0_.refs_2_), channel_id=1, source_target_pairs={{0,16},{4,12},{8,24},{12,4},{16,0},{20,28},{24,8},{28,20},{1,17},{... | collective-permute-start | bytes 1966088 | tf_op jit(solution)/shard_map/ppermute | solution.py:440
  27.6 0.5 collective-permute-start.8
  28.1 1.8 %collective-permute-done.12.refs_2_ = bf16[40,1024]{1,0:T(8,128)(2,1)S(1)} collective-permute-done((bf16[40,1024]{1,0:T(8,128)(2,1)S(1)}, bf16[40,1024]{1,0:T(8,128)(2,1)S(1)}, u32[]{:S(2)}, u32[]{:S(2)}) %collective-permute-start.12) | collective-permute-done | bytes 81952 | tf_op jit(solution)/shard_map/ppermute | solution.py:434
  29.9 1.2 %collective-permute-start.14 = (bf16[160,1024]{1,0:T(8,128)(2,1)S(1)}, bf16[160,1024]{1,0:T(8,128)(2,1)S(1)}, u32[]{:S(2)}, u32[]{:S(2)}) collective-permute-start(bf16[160,1024]{1,0:T(8,128)(2,1)S(1)} %join.7.refs_0_), channel_id=1, source_target_pairs={{0,8},{4,20},{8,0},{12,28},{16,24},{20,4},{24,16},{28,12},{1,9},{5... | collective-permute-start | bytes 983048 | tf_op jit(solution)/shard_map/ppermute | solution.py:440
  31.2 5.9 %collective-permute-done.14.refs_1_ = bf16[160,1024]{1,0:T(8,128)(2,1)S(1)} collective-permute-done((bf16[160,1024]{1,0:T(8,128)(2,1)S(1)}, bf16[160,1024]{1,0:T(8,128)(2,1)S(1)}, u32[]{:S(2)}, u32[]{:S(2)}) %collective-permute-start.14) | collective-permute-done | bytes 327712 | tf_op jit(solution)/shard_map/ppermute | solution.py:440
  37.1 1.2 %collective-permute-start.15 = (bf16[320,1024]{1,0:T(8,128)(2,1)S(1)}, bf16[320,1024]{1,0:T(8,128)(2,1)S(1)}, u32[]{:S(2)}, u32[]{:S(2)}) collective-permute-start(bf16[320,1024]{1,0:T(8,128)(2,1)S(1)} %join.8.refs_0_), channel_id=1, source_target_pairs={{0,16},{4,12},{8,24},{12,4},{16,0},{20,28},{24,8},{28,20},{1,17},{... | collective-permute-start | bytes 1966088 | tf_op jit(solution)/shard_map/ppermute | solution.py:440
  38.4 1.8 %collective-permute-done.6.refs_1_ = bf16[320,1024]{1,0:T(8,128)(2,1)S(1)} collective-permute-done((bf16[320,1024]{1,0:T(8,128)(2,1)S(1)}, bf16[320,1024]{1,0:T(8,128)(2,1)S(1)}, u32[]{:S(2)}, u32[]{:S(2)}) %collective-permute-start.6) | collective-permute-done | bytes 655392 | tf_op jit(solution)/shard_map/ppermute | solution.py:440
  40.2 4.9 %forward.1 = (bf16[320,1024]{1,0:T(8,128)(2,1)S(1)}, bf16[320,1024]{1,0:T(8,128)(2,1)S(1)}, bf16[640,1024]{1,0:T(8,128)(2,1)S(1)}, bf16[2,640,512]{2,1,0:T(8,128...) custom-call(bf16[320,1024]{1,0:T(8,128)(2,1)S(1)} %join.6.refs_0_.refs_2_, ...), custom_call_target="tpu_custom_call" | custom-call | flops 4026531840 | tf_op jit(solution)/shard_map/forward/pallas_call | solution.py:53
  45.1 1.6 %collective-permute-start.10 = (bf16[320,1024]{1,0:T(8,128)(2,1)S(1)}, bf16[320,1024]{1,0:T(8,128)(2,1)S(1)}, u32[]{:S(2)}, u32[]{:S(2)}) collective-permute-start(bf16[320,1024]{1,0:T(8,128)(2,1)S(1)} %get-tuple-element.68), channel_id=1, source_target_pairs={{0,16},{4,12},{8,24},{12,4},{16,0},{20,28},{24,8},{28,20},{1,17},{... | collective-permute-start | bytes 1966088 | tf_op jit(solution)/shard_map/ppermute | solution.py:440
  46.7 1.1 %collective-permute-done.15.refs_1_ = bf16[320,1024]{1,0:T(8,128)(2,1)S(1)} collective-permute-done((bf16[320,1024]{1,0:T(8,128)(2,1)S(1)}, bf16[320,1024]{1,0:T(8,128)(2,1)S(1)}, u32[]{:S(2)}, u32[]{:S(2)}) %collective-permute-start.15) | collective-permute-done | bytes 655392 | tf_op jit(solution)/shard_map/ppermute | solution.py:440
  47.8 4.4 %backward.1 = (bf16[320,1024]{1,0:T(8,128)(2,1)S(1)}, bf16[320,1024]{1,0:T(8,128)(2,1)S(1)}, bf16[640,1024]{1,0:T(8,128)(2,1)S(1)}, bf16[2,640,512]{2,1,0:T(8,128)(2,1)S(1)}, bf16[2,640,512]{2,1,0:T(8,128)(2,1)S(1)}) custom-call(bf16[320,1024]{1,0:T(8,128)(2,1)S(1)} %join.8.refs_0_, bf16[320,1024]{1,0:T(8,128)(2,1)S(1)} %collective-permute-done.15.refs_1_, ...), custom_call_target="tpu_custom_call" | custom-call | flops 4026531840 | tf_op jit(solution)/shard_map/backward/pallas_call | solution.py:53
  52.2 1.2 %collective-permute-start.17 = (bf16[320,1024]{1,0:T(8,128)(2,1)S(1)}, bf16[320,1024]{1,0:T(8,128)(2,1)S(1)}, u32[]{:S(2)}, u32[]{:S(2)}) collective-permute-start(bf16[320,1024]{1,0:T(8,128)(2,1)S(1)} %get-tuple-element.78), channel_id=1, source_target_pairs={{0,16},{4,12},{8,24},{12,4},{16,0},{20,28},{24,8},{28,20},{1,17},{... | collective-permute-start | bytes 1966088 | tf_op jit(solution)/shard_map/ppermute | solution.py:440
  53.4 2.3 %collective-permute-done.10.refs_1_ = bf16[320,1024]{1,0:T(8,128)(2,1)S(1)} collective-permute-done((bf16[320,1024]{1,0:T(8,128)(2,1)S(1)}, bf16[320,1024]{1,0:T(8,128)(2,1)S(1)}, u32[]{:S(2)}, u32[]{:S(2)}) %collective-permute-start.10) | collective-permute-done | bytes 655392 | tf_op jit(solution)/shard_map/ppermute | solution.py:440
  55.7 0.2 add.9
  55.9 1.6 %collective-permute-start.16 = (bf16[160,1024]{1,0:T(8,128)(2,1)S(1)}, bf16[160,1024]{1,0:T(8,128)(2,1)S(1)}, u32[]{:S(2)}, u32[]{:S(2)}) collective-permute-start(bf16[160,1024]{1,0:T(8,128)(2,1)S(1)} %get-tuple-element.76.refs_6_), channel_id=1, source_target_pairs={{0,8},{4,20},{8,0},{12,28},{16,24},{20,4},{24,16},{28,12},{1,9},{5... | collective-permute-start | bytes 983048 | tf_op jit(solution)/shard_map/ppermute | solution.py:440
  57.5 2.7 %grads_given.1 = (bf16[3,1024,512]{2,1,0:T(8,128)(2,1)S(1)}, bf16[16,128]{1,0:T(8,128)(2,1)S(1)}) custom-call(s32[1]{0:T(128)} %bitcast.3.refs_0_.refs_2_, bf16[640,1024]{1,0:T(8,128)(2,1)S(1)} %get-tuple-element.79.refs_1_, bf16[640,1024]{1,0:T(8,128)(2,1)S(1)} %get-tuple-element.74.refs_2_, bf16[2,640,512]{2,1,0:T(8,128)(2,1)S(1)} %get-tuple-element.80.refs_3_, ...), custom_call_target="tpu_custom_call" | custom-call | flops 2013265920 | tf_op jit(solution)/shard_map/grads_given/pallas_call | solution.py:53
  60.1 3.9 %grads_kept.1 = (bf16[2,1024,512]{2,1,0:T(8,128)(2,1)}, bf16[2,1024,512]{2,1,0:T(8,128)(2,1)}, bf16[2,512,1024]{2,1,0:T(8,128)(2,1)}, bf16[16,128]{1,0:T(8,128)(2,1)S(1)}) custom-call(s32[1]{0:T(128)} %bitcast.3.refs_0_.refs_2_, bf16[640,1024]{1,0:T(8,128)(2,1)S(1)} %get-tuple-element.79.refs_1_, bf16[640,1024]{1,0:T(8,128)(2,1)S(1)} %get-tuple-element.74.refs_2_, ...), custom_call_target="tpu_custom_call" | custom-call | flops 2013265920 | tf_op jit(solution)/shard_map/grads_kept/pallas_call | solution.py:53
  64.0 1.6 %collective-permute-done.17.refs_1_ = bf16[320,1024]{1,0:T(8,128)(2,1)S(1)} collective-permute-done((bf16[320,1024]{1,0:T(8,128)(2,1)S(1)}, bf16[320,1024]{1,0:T(8,128)(2,1)S(1)}, u32[]{:S(2)}, u32[]{:S(2)}) %collective-permute-start.17) | collective-permute-done | bytes 655392 | tf_op jit(solution)/shard_map/ppermute | solution.py:440
  65.6 0.2 add.10
  65.8 0.9 collective-permute-done.16.refs_1_
  66.6 0.1 add.11.refs_1_
  66.7 1.2 %collective-permute-start.18 = (bf16[160,1024]{1,0:T(8,128)(2,1)S(1)}, bf16[160,1024]{1,0:T(8,128)(2,1)S(1)}, u32[]{:S(2)}, u32[]{:S(2)}) collective-permute-start(bf16[160,1024]{1,0:T(8,128)(2,1)S(1)} %add.11.refs_1_), channel_id=1, source_target_pairs={{0,4},{4,0},{8,12},{12,8},{16,20},{20,16},{24,28},{28,24},{1,5},{5... | collective-permute-start | bytes 983048 | tf_op jit(solution)/shard_map/ppermute | solution.py:431
  67.9 1.2 %collective-permute-start.22 = (bf16[160,1024]{1,0:T(8,128)(2,1)S(1)}, bf16[160,1024]{1,0:T(8,128)(2,1)S(1)}, u32[]{:S(2)}, u32[]{:S(2)}) collective-permute-start(bf16[160,1024]{1,0:T(8,128)(2,1)S(1)} %get-tuple-element.85.refs_2_), channel_id=1, source_target_pairs={{0,8},{4,20},{8,0},{12,28},{16,24},{20,4},{24,16},{28,12},{1,9},{5... | collective-permute-start | bytes 983048 | tf_op jit(solution)/shard_map/ppermute | solution.py:440
  69.1 0.1 collective-permute-done.18.refs_2_
  69.1 0.3 blend.6
  69.5 1.1 %collective-permute-start.19 = (bf16[40,1024]{1,0:T(8,128)(2,1)S(1)}, bf16[40,1024]{1,0:T(8,128)(2,1)S(1)}, u32[]{:S(2)}, u32[]{:S(2)}) collective-permute-start(bf16[40,1024]{1,0:T(8,128)(2,1)S(1)} %get-tuple-element.87), channel_id=1, source_target_pairs={{0,1},{1,0},{2,3},{3,2},{4,5},{5,4},{6,7},{7,6},{8,9},{9,8},{10,11... | collective-permute-start | bytes 245768 | tf_op jit(solution)/shard_map/ppermute | solution.py:434
  70.6 2.0 %collective-permute-start.20 = (bf16[40,1024]{1,0:T(8,128)(2,1)S(1)}, bf16[40,1024]{1,0:T(8,128)(2,1)S(1)}, u32[]{:S(2)}, u32[]{:S(2)}) collective-permute-start(bf16[40,1024]{1,0:T(8,128)(2,1)S(1)} %get-tuple-element.88), channel_id=1, source_target_pairs={{0,2},{1,3},{2,0},{3,1},{4,6},{5,7},{6,4},{7,5},{8,10},{9,11},{10,... | collective-permute-start | bytes 245768 | tf_op jit(solution)/shard_map/ppermute | solution.py:434
  72.6 1.4 %collective-permute-start.21 = (bf16[40,1024]{1,0:T(8,128)(2,1)S(1)}, bf16[40,1024]{1,0:T(8,128)(2,1)S(1)}, u32[]{:S(2)}, u32[]{:S(2)}) collective-permute-start(bf16[40,1024]{1,0:T(8,128)(2,1)S(1)} %get-tuple-element.89), channel_id=1, source_target_pairs={{0,3},{1,2},{2,1},{3,0},{4,7},{5,6},{6,5},{7,4},{8,11},{9,10},{10,... | collective-permute-start | bytes 245768 | tf_op jit(solution)/shard_map/ppermute | solution.py:434
  74.0 1.0 %collective-permute-done.22.refs_1_ = bf16[160,1024]{1,0:T(8,128)(2,1)S(1)} collective-permute-done((bf16[160,1024]{1,0:T(8,128)(2,1)S(1)}, bf16[160,1024]{1,0:T(8,128)(2,1)S(1)}, u32[]{:S(2)}, u32[]{:S(2)}) %collective-permute-start.22) | collective-permute-done | bytes 327712 | tf_op jit(solution)/shard_map/ppermute | solution.py:440
  75.0 0.1 add.12.refs_4_.refs_1_
  75.0 0.1 collective-permute-start.23
  75.1 0.1 collective-permute-done.19.refs_1_
  75.2 4.9 %collective-permute-done.20.refs_2_ = bf16[40,1024]{1,0:T(8,128)(2,1)S(1)} collective-permute-done((bf16[40,1024]{1,0:T(8,128)(2,1)S(1)}, bf16[40,1024]{1,0:T(8,128)(2,1)S(1)}, u32[]{:S(2)}, u32[]{:S(2)}) %collective-permute-start.20) | collective-permute-done | bytes 81952 | tf_op jit(solution)/shard_map/ppermute | solution.py:434
  80.1 0.3 blend.7
  80.4 0.1 collective-permute-start.27
  80.5 1.5 %collective-permute-start.24 = (bf16[40,1024]{1,0:T(8,128)(2,1)S(1)}, bf16[40,1024]{1,0:T(8,128)(2,1)S(1)}, u32[]{:S(2)}, u32[]{:S(2)}) collective-permute-start(bf16[40,1024]{1,0:T(8,128)(2,1)S(1)} %get-tuple-element.93), channel_id=1, source_target_pairs={{0,1},{1,0},{2,3},{3,2},{4,5},{5,4},{6,7},{7,6},{8,9},{9,8},{10,11... | collective-permute-start | bytes 245768 | tf_op jit(solution)/shard_map/ppermute | solution.py:434
  82.0 1.1 %collective-permute-start.25 = (bf16[40,1024]{1,0:T(8,128)(2,1)S(1)}, bf16[40,1024]{1,0:T(8,128)(2,1)S(1)}, u32[]{:S(2)}, u32[]{:S(2)}) collective-permute-start(bf16[40,1024]{1,0:T(8,128)(2,1)S(1)} %get-tuple-element.94), channel_id=1, source_target_pairs={{0,2},{1,3},{2,0},{3,1},{4,6},{5,7},{6,4},{7,5},{8,10},{9,11},{10,... | collective-permute-start | bytes 245768 | tf_op jit(solution)/shard_map/ppermute | solution.py:434
  83.1 1.9 %collective-permute-start.26 = (bf16[40,1024]{1,0:T(8,128)(2,1)S(1)}, bf16[40,1024]{1,0:T(8,128)(2,1)S(1)}, u32[]{:S(2)}, u32[]{:S(2)}) collective-permute-start(bf16[40,1024]{1,0:T(8,128)(2,1)S(1)} %get-tuple-element.95), channel_id=1, source_target_pairs={{0,3},{1,2},{2,1},{3,0},{4,7},{5,6},{6,5},{7,4},{8,11},{9,10},{10,... | collective-permute-start | bytes 245768 | tf_op jit(solution)/shard_map/ppermute | solution.py:434
  85.0 0.9 %combine.2.refs_5_ = bf16[64,1024]{1,0:T(8,128)(2,1)} custom-call(bf16[160,64]{1,0:T(8,128)(2,1)S(1)} %get-tuple-element.56.refs_0_, bf16[160,64]{1,0:T(8,128)(2,1)S(1)} %get-tuple-element.57.refs_1_, bf16[160,1024]{1,0:T(8,128)(2,1)S(1)} %join.9.refs_3_.refs_2_, bf16[40,1024]{1,0:T(8,128)(2,1)S(1)} %get-tuple-element.91.refs_3_.refs_1_), custom_call_target="tpu_custom_call" | custom-call | tf_op jit(solution)/shard_map/combine/pallas_call | solution.py:53
  85.9 0.3 collective-permute-done.27.refs_1_
  86.2 0.9 copy-done.3
  87.1 1.7 %finish.1 = (bf16[2,1024,512]{2,1,0:T(8,128)(2,1)}, bf16[2,1024,512]{2,1,0:T(8,128)(2,1)}, bf16[2,512,1024]{2,1,0:T(8,128)(2,1)}, bf16[16,128]{1,0:T(8,128)(2,1)S(1)}) custom-call(s32[1]{0:T(128)} %bitcast.3.refs_0_.refs_2_, bf16[3,1024,512]{2,1,0:T(8,128)(2,1)S(1)} %collective-permute-done.27.refs_1_, ...), custom_call_target="tpu_custom_call", output_to_operand_aliasing={{0}: (2, {}), {1}: (3, {}), {2}: (4, {})} | custom-call | tf_op jit(solution)/shard_map/finish/pallas_call | solution.py:53
  88.8 2.8 %collective-permute-done.25.refs_3_ = bf16[40,1024]{1,0:T(8,128)(2,1)S(1)} collective-permute-done((bf16[40,1024]{1,0:T(8,128)(2,1)S(1)}, bf16[40,1024]{1,0:T(8,128)(2,1)S(1)}, u32[]{:S(2)}, u32[]{:S(2)}) %collective-permute-start.25) | collective-permute-done | bytes 81952 | tf_op jit(solution)/shard_map/ppermute | solution.py:434
  91.6 0.9 combine.3
  (30 shorter events, 0.2 us)
Async XLA Ops:
  0.6 27.0 %copy-start = (bf16[2,1024,512]{2,1,0:T(8,128)(2,1)S(1)}, bf16[2,1024,512]{2,1,0:T(8,128)(2,1)}, u32[]{:S(2)}) copy-start(bf16[2,1024,512]{2,1,0:T(8,128)(2,1)} %refs_3_.5) | copy-start | bytes 6291460
  0.6 1.1 %copy-start.4 = (bf16[64,1024]{1,0:T(8,128)(2,1)S(1)}, bf16[64,1024]{1,0:T(8,128)(2,1)}, u32[]{:S(2)}) copy-start(bf16[64,1024]{1,0:T(8,128)(2,1)} %refs_2_.1) | copy-start | bytes 393220
  1.7 0.7 copy-start.6
  2.9 2.8 %collective-permute-start = (bf16[160,1024]{1,0:T(8,128)(2,1)S(1)}, bf16[160,1024]{1,0:T(8,128)(2,1)S(1)}, u32[]{:S(2)}, u32[]{:S(2)}) collective-permute-start(bf16[160,1024]{1,0:T(8,128)(2,1)S(1)} %get-tuple-element.55.refs_4_.refs_1_), channel_id=1, source_target_pairs={{0,4},{4,0},{8,12},{12,8},{16,20},{20,16},{24,28},{28,24},{1,5},{5... | collective-permute-start | bytes 983048 | tf_op jit(solution)/shard_map/ppermute | solution.py:431
  3.5 0.9 copy-start.5
  4.4 0.7 copy-start.7
  5.6 6.2 %collective-permute-start.4 = (bf16[160,1024]{1,0:T(8,128)(2,1)S(1)}, bf16[160,1024]{1,0:T(8,128)(2,1)S(1)}, u32[]{:S(2)}, u32[]{:S(2)}) collective-permute-start(bf16[160,1024]{1,0:T(8,128)(2,1)S(1)} %get-tuple-element.62.refs_1_), channel_id=1, source_target_pairs={{0,4},{4,0},{8,12},{12,8},{16,20},{20,16},{24,28},{28,24},{1,5},{5... | collective-permute-start | bytes 983048 | tf_op jit(solution)/shard_map/ppermute | solution.py:431
  6.1 6.0 %collective-permute-start.1 = (bf16[40,1024]{1,0:T(8,128)(2,1)S(1)}, bf16[40,1024]{1,0:T(8,128)(2,1)S(1)}, u32[]{:S(2)}, u32[]{:S(2)}) collective-permute-start(bf16[40,1024]{1,0:T(8,128)(2,1)S(1)} %get-tuple-element.59), channel_id=1, source_target_pairs={{0,1},{1,0},{2,3},{3,2},{4,5},{5,4},{6,7},{7,6},{8,9},{9,8},{10,11... | collective-permute-start | bytes 245768 | tf_op jit(solution)/shard_map/ppermute | solution.py:434
  9.2 9.4 %collective-permute-start.2 = (bf16[40,1024]{1,0:T(8,128)(2,1)S(1)}, bf16[40,1024]{1,0:T(8,128)(2,1)S(1)}, u32[]{:S(2)}, u32[]{:S(2)}) collective-permute-start(bf16[40,1024]{1,0:T(8,128)(2,1)S(1)} %get-tuple-element.60), channel_id=1, source_target_pairs={{0,2},{1,3},{2,0},{3,1},{4,6},{5,7},{6,4},{7,5},{8,10},{9,11},{10,... | collective-permute-start | bytes 245768 | tf_op jit(solution)/shard_map/ppermute | solution.py:434
  11.8 6.8 %collective-permute-start.3 = (bf16[40,1024]{1,0:T(8,128)(2,1)S(1)}, bf16[40,1024]{1,0:T(8,128)(2,1)S(1)}, u32[]{:S(2)}, u32[]{:S(2)}) collective-permute-start(bf16[40,1024]{1,0:T(8,128)(2,1)S(1)} %get-tuple-element.61), channel_id=1, source_target_pairs={{0,3},{1,2},{2,1},{3,0},{4,7},{5,6},{6,5},{7,4},{8,11},{9,10},{10,... | collective-permute-start | bytes 245768 | tf_op jit(solution)/shard_map/ppermute | solution.py:434
  18.6 7.3 %collective-permute-start.5 = (bf16[160,1024]{1,0:T(8,128)(2,1)S(1)}, bf16[160,1024]{1,0:T(8,128)(2,1)S(1)}, u32[]{:S(2)}, u32[]{:S(2)}) collective-permute-start(bf16[160,1024]{1,0:T(8,128)(2,1)S(1)} %join.5.refs_0_.refs_4_), channel_id=1, source_target_pairs={{0,8},{4,20},{8,0},{12,28},{16,24},{20,4},{24,16},{28,12},{1,9},{5... | collective-permute-start | bytes 983048 | tf_op jit(solution)/shard_map/ppermute | solution.py:440
  20.2 7.4 %collective-permute-start.11 = (bf16[40,1024]{1,0:T(8,128)(2,1)S(1)}, bf16[40,1024]{1,0:T(8,128)(2,1)S(1)}, u32[]{:S(2)}, u32[]{:S(2)}) collective-permute-start(bf16[40,1024]{1,0:T(8,128)(2,1)S(1)} %get-tuple-element.69), channel_id=1, source_target_pairs={{0,1},{1,0},{2,3},{3,2},{4,5},{5,4},{6,7},{7,6},{8,9},{9,8},{10,11... | collective-permute-start | bytes 245768 | tf_op jit(solution)/shard_map/ppermute | solution.py:434
  21.7 8.2 %collective-permute-start.12 = (bf16[40,1024]{1,0:T(8,128)(2,1)S(1)}, bf16[40,1024]{1,0:T(8,128)(2,1)S(1)}, u32[]{:S(2)}, u32[]{:S(2)}) collective-permute-start(bf16[40,1024]{1,0:T(8,128)(2,1)S(1)} %get-tuple-element.70), channel_id=1, source_target_pairs={{0,2},{1,3},{2,0},{3,1},{4,6},{5,7},{6,4},{7,5},{8,10},{9,11},{10,... | collective-permute-start | bytes 245768 | tf_op jit(solution)/shard_map/ppermute | solution.py:434
  23.2 6.7 %collective-permute-start.13 = (bf16[40,1024]{1,0:T(8,128)(2,1)S(1)}, bf16[40,1024]{1,0:T(8,128)(2,1)S(1)}, u32[]{:S(2)}, u32[]{:S(2)}) collective-permute-start(bf16[40,1024]{1,0:T(8,128)(2,1)S(1)} %get-tuple-element.71), channel_id=1, source_target_pairs={{0,3},{1,2},{2,1},{3,0},{4,7},{5,6},{6,5},{7,4},{8,11},{9,10},{10,... | collective-permute-start | bytes 245768 | tf_op jit(solution)/shard_map/ppermute | solution.py:434
  26.0 14.2 %copy-start.1 = (bf16[2,1024,512]{2,1,0:T(8,128)(2,1)S(1)}, bf16[2,1024,512]{2,1,0:T(8,128)(2,1)}, u32[]{:S(2)}) copy-start(bf16[2,1024,512]{2,1,0:T(8,128)(2,1)} %refs_4_.3) | copy-start | bytes 6291460
  26.0 14.2 %copy-start.2 = (bf16[2,512,1024]{2,1,0:T(8,128)(2,1)S(1)}, bf16[2,512,1024]{2,1,0:T(8,128)(2,1)}, u32[]{:S(2)}) copy-start(bf16[2,512,1024]{2,1,0:T(8,128)(2,1)} %refs_5_.3) | copy-start | bytes 6291460
  26.0 14.2 %collective-permute-start.6 = (bf16[320,1024]{1,0:T(8,128)(2,1)S(1)}, bf16[320,1024]{1,0:T(8,128)(2,1)S(1)}, u32[]{:S(2)}, u32[]{:S(2)}) collective-permute-start(bf16[320,1024]{1,0:T(8,128)(2,1)S(1)} %join.6.refs_0_.refs_2_), channel_id=1, source_target_pairs={{0,16},{4,12},{8,24},{12,4},{16,0},{20,28},{24,8},{28,20},{1,17},{... | collective-permute-start | bytes 1966088 | tf_op jit(solution)/shard_map/ppermute | solution.py:440
  27.6 12.6 %collective-permute-start.7 = (bf16[2,1024,512]{2,1,0:T(8,128)(2,1)S(1)}, bf16[2,1024,512]{2,1,0:T(8,128)(2,1)S(1)}, u32[]{:S(2)}, u32[]{:S(2)}) collective-permute-start(bf16[2,1024,512]{2,1,0:T(8,128)(2,1)S(1)} %copy-done), channel_id=1, source_target_pairs={{0,4},{4,0},{8,12},{12,8},{16,20},{20,16},{24,28},{28,24},{1,5},{5... | collective-permute-start | bytes 6291464 | tf_op jit(solution)/shard_map/ppermute | solution.py:431
  27.6 12.6 %collective-permute-start.8 = (bf16[2,1024,512]{2,1,0:T(8,128)(2,1)}, bf16[2,1024,512]{2,1,0:T(8,128)(2,1)S(1)}, u32[]{:S(2)}, u32[]{:S(2)}) collective-permute-start(bf16[2,1024,512]{2,1,0:T(8,128)(2,1)} %refs_4_.3), channel_id=1, source_target_pairs={{0,4},{4,0},{8,12},{12,8},{16,20},{20,16},{24,28},{28,24},{1,5},{5... | collective-permute-start | bytes 6291464 | tf_op jit(solution)/shard_map/ppermute | solution.py:431
  29.9 10.3 %collective-permute-start.9 = (bf16[2,512,1024]{2,1,0:T(8,128)(2,1)}, bf16[2,512,1024]{2,1,0:T(8,128)(2,1)S(1)}, u32[]{:S(2)}, u32[]{:S(2)}) collective-permute-start(bf16[2,512,1024]{2,1,0:T(8,128)(2,1)} %refs_5_.3), channel_id=1, source_target_pairs={{0,4},{4,0},{8,12},{12,8},{16,20},{20,16},{24,28},{28,24},{1,5},{5... | collective-permute-start | bytes 6291464 | tf_op jit(solution)/shard_map/ppermute | solution.py:431
  29.9 7.1 %collective-permute-start.14 = (bf16[160,1024]{1,0:T(8,128)(2,1)S(1)}, bf16[160,1024]{1,0:T(8,128)(2,1)S(1)}, u32[]{:S(2)}, u32[]{:S(2)}) collective-permute-start(bf16[160,1024]{1,0:T(8,128)(2,1)S(1)} %join.7.refs_0_), channel_id=1, source_target_pairs={{0,8},{4,20},{8,0},{12,28},{16,24},{20,4},{24,16},{28,12},{1,9},{5... | collective-permute-start | bytes 983048 | tf_op jit(solution)/shard_map/ppermute | solution.py:440
  37.1 10.7 %collective-permute-start.15 = (bf16[320,1024]{1,0:T(8,128)(2,1)S(1)}, bf16[320,1024]{1,0:T(8,128)(2,1)S(1)}, u32[]{:S(2)}, u32[]{:S(2)}) collective-permute-start(bf16[320,1024]{1,0:T(8,128)(2,1)S(1)} %join.8.refs_0_), channel_id=1, source_target_pairs={{0,16},{4,12},{8,24},{12,4},{16,0},{20,28},{24,8},{28,20},{1,17},{... | collective-permute-start | bytes 1966088 | tf_op jit(solution)/shard_map/ppermute | solution.py:440
  45.1 10.7 %collective-permute-start.10 = (bf16[320,1024]{1,0:T(8,128)(2,1)S(1)}, bf16[320,1024]{1,0:T(8,128)(2,1)S(1)}, u32[]{:S(2)}, u32[]{:S(2)}) collective-permute-start(bf16[320,1024]{1,0:T(8,128)(2,1)S(1)} %get-tuple-element.68), channel_id=1, source_target_pairs={{0,16},{4,12},{8,24},{12,4},{16,0},{20,28},{24,8},{28,20},{1,17},{... | collective-permute-start | bytes 1966088 | tf_op jit(solution)/shard_map/ppermute | solution.py:440
  52.2 13.4 %collective-permute-start.17 = (bf16[320,1024]{1,0:T(8,128)(2,1)S(1)}, bf16[320,1024]{1,0:T(8,128)(2,1)S(1)}, u32[]{:S(2)}, u32[]{:S(2)}) collective-permute-start(bf16[320,1024]{1,0:T(8,128)(2,1)S(1)} %get-tuple-element.78), channel_id=1, source_target_pairs={{0,16},{4,12},{8,24},{12,4},{16,0},{20,28},{24,8},{28,20},{1,17},{... | collective-permute-start | bytes 1966088 | tf_op jit(solution)/shard_map/ppermute | solution.py:440
  55.9 10.7 %collective-permute-start.16 = (bf16[160,1024]{1,0:T(8,128)(2,1)S(1)}, bf16[160,1024]{1,0:T(8,128)(2,1)S(1)}, u32[]{:S(2)}, u32[]{:S(2)}) collective-permute-start(bf16[160,1024]{1,0:T(8,128)(2,1)S(1)} %get-tuple-element.76.refs_6_), channel_id=1, source_target_pairs={{0,8},{4,20},{8,0},{12,28},{16,24},{20,4},{24,16},{28,12},{1,9},{5... | collective-permute-start | bytes 983048 | tf_op jit(solution)/shard_map/ppermute | solution.py:440
  66.7 2.4 %collective-permute-start.18 = (bf16[160,1024]{1,0:T(8,128)(2,1)S(1)}, bf16[160,1024]{1,0:T(8,128)(2,1)S(1)}, u32[]{:S(2)}, u32[]{:S(2)}) collective-permute-start(bf16[160,1024]{1,0:T(8,128)(2,1)S(1)} %add.11.refs_1_), channel_id=1, source_target_pairs={{0,4},{4,0},{8,12},{12,8},{16,20},{20,16},{24,28},{28,24},{1,5},{5... | collective-permute-start | bytes 983048 | tf_op jit(solution)/shard_map/ppermute | solution.py:431
  67.9 7.1 %collective-permute-start.22 = (bf16[160,1024]{1,0:T(8,128)(2,1)S(1)}, bf16[160,1024]{1,0:T(8,128)(2,1)S(1)}, u32[]{:S(2)}, u32[]{:S(2)}) collective-permute-start(bf16[160,1024]{1,0:T(8,128)(2,1)S(1)} %get-tuple-element.85.refs_2_), channel_id=1, source_target_pairs={{0,8},{4,20},{8,0},{12,28},{16,24},{20,4},{24,16},{28,12},{1,9},{5... | collective-permute-start | bytes 983048 | tf_op jit(solution)/shard_map/ppermute | solution.py:440
  69.5 5.7 %collective-permute-start.19 = (bf16[40,1024]{1,0:T(8,128)(2,1)S(1)}, bf16[40,1024]{1,0:T(8,128)(2,1)S(1)}, u32[]{:S(2)}, u32[]{:S(2)}) collective-permute-start(bf16[40,1024]{1,0:T(8,128)(2,1)S(1)} %get-tuple-element.87), channel_id=1, source_target_pairs={{0,1},{1,0},{2,3},{3,2},{4,5},{5,4},{6,7},{7,6},{8,9},{9,8},{10,11... | collective-permute-start | bytes 245768 | tf_op jit(solution)/shard_map/ppermute | solution.py:434
  70.6 9.5 %collective-permute-start.20 = (bf16[40,1024]{1,0:T(8,128)(2,1)S(1)}, bf16[40,1024]{1,0:T(8,128)(2,1)S(1)}, u32[]{:S(2)}, u32[]{:S(2)}) collective-permute-start(bf16[40,1024]{1,0:T(8,128)(2,1)S(1)} %get-tuple-element.88), channel_id=1, source_target_pairs={{0,2},{1,3},{2,0},{3,1},{4,6},{5,7},{6,4},{7,5},{8,10},{9,11},{10,... | collective-permute-start | bytes 245768 | tf_op jit(solution)/shard_map/ppermute | solution.py:434
  72.6 7.5 %collective-permute-start.21 = (bf16[40,1024]{1,0:T(8,128)(2,1)S(1)}, bf16[40,1024]{1,0:T(8,128)(2,1)S(1)}, u32[]{:S(2)}, u32[]{:S(2)}) collective-permute-start(bf16[40,1024]{1,0:T(8,128)(2,1)S(1)} %get-tuple-element.89), channel_id=1, source_target_pairs={{0,3},{1,2},{2,1},{3,0},{4,7},{5,6},{6,5},{7,4},{8,11},{9,10},{10,... | collective-permute-start | bytes 245768 | tf_op jit(solution)/shard_map/ppermute | solution.py:434
  75.0 5.0 %collective-permute-start.23 = (bf16[160,1024]{1,0:T(8,128)(2,1)S(1)}, bf16[160,1024]{1,0:T(8,128)(2,1)S(1)}, u32[]{:S(2)}, u32[]{:S(2)}) collective-permute-start(bf16[160,1024]{1,0:T(8,128)(2,1)S(1)} %add.12.refs_4_.refs_1_), channel_id=1, source_target_pairs={{0,4},{4,0},{8,12},{12,8},{16,20},{20,16},{24,28},{28,24},{1,5},{5... | collective-permute-start | bytes 983048 | tf_op jit(solution)/shard_map/ppermute | solution.py:431
  80.4 5.7 %collective-permute-start.27 = (bf16[3,1024,512]{2,1,0:T(8,128)(2,1)S(1)}, bf16[3,1024,512]{2,1,0:T(8,128)(2,1)S(1)}, u32[]{:S(2)}, u32[]{:S(2)}) collective-permute-start(bf16[3,1024,512]{2,1,0:T(8,128)(2,1)S(1)} %get-tuple-element.97), channel_id=1, source_target_pairs={{0,4},{4,0},{8,12},{12,8},{16,20},{20,16},{24,28},{28,24},{1,5},{5... | collective-permute-start | bytes 9437192 | tf_op jit(solution)/shard_map/ppermute | solution.py:431
  80.5 8.3 %collective-permute-start.24 = (bf16[40,1024]{1,0:T(8,128)(2,1)S(1)}, bf16[40,1024]{1,0:T(8,128)(2,1)S(1)}, u32[]{:S(2)}, u32[]{:S(2)}) collective-permute-start(bf16[40,1024]{1,0:T(8,128)(2,1)S(1)} %get-tuple-element.93), channel_id=1, source_target_pairs={{0,1},{1,0},{2,3},{3,2},{4,5},{5,4},{6,7},{7,6},{8,9},{9,8},{10,11... | collective-permute-start | bytes 245768 | tf_op jit(solution)/shard_map/ppermute | solution.py:434
  82.0 9.6 %collective-permute-start.25 = (bf16[40,1024]{1,0:T(8,128)(2,1)S(1)}, bf16[40,1024]{1,0:T(8,128)(2,1)S(1)}, u32[]{:S(2)}, u32[]{:S(2)}) collective-permute-start(bf16[40,1024]{1,0:T(8,128)(2,1)S(1)} %get-tuple-element.94), channel_id=1, source_target_pairs={{0,2},{1,3},{2,0},{3,1},{4,6},{5,7},{6,4},{7,5},{8,10},{9,11},{10,... | collective-permute-start | bytes 245768 | tf_op jit(solution)/shard_map/ppermute | solution.py:434
  83.1 8.5 %collective-permute-start.26 = (bf16[40,1024]{1,0:T(8,128)(2,1)S(1)}, bf16[40,1024]{1,0:T(8,128)(2,1)S(1)}, u32[]{:S(2)}, u32[]{:S(2)}) collective-permute-start(bf16[40,1024]{1,0:T(8,128)(2,1)S(1)} %get-tuple-element.95), channel_id=1, source_target_pairs={{0,3},{1,2},{2,1},{3,0},{4,7},{5,6},{6,5},{7,4},{8,11},{9,10},{10,... | collective-permute-start | bytes 245768 | tf_op jit(solution)/shard_map/ppermute | solution.py:434
  86.2 0.9 copy-start.3

commit v5 on v4

--- a/solution.py
+++ b/solution.py
@@ -442,9 +442,9 @@
     def swap(messages):
         return [messages[0]] + [to_owner(messages[j], j) for j in range(1, owners)]
 
-    def widen(part, after=()):
+    def widen(part, after=(), flops=0):
         for s in range(bits - 1):
-            part = join([part, to_chip(part, s)], after)
+            part = join([part, to_chip(part, s)], after, flops)
         return part
 
     def reduce(low, high, after=()):
@@ -476,8 +476,10 @@
     q_low, q_high = reduce(*qs, [token])
     p_messages = hand_out(add([p_low, to_chip(p_high, 0)], 1, [q_high])[0])
     q_rows = add([q_low, to_chip(q_high, 0)], 1, p_messages[:1])[0]
-    p_messages = join(swap(p_messages), [q_rows], 20 * FLOPS_PER_US)
-    q_messages = hand_out(q_rows, [p_messages])
+    p_messages = swap(p_messages)
+    early = join(p_messages[:-1], [q_rows], 20 * FLOPS_PER_US)
+    q_messages = hand_out(q_rows, [early])
+    p_messages = join(p_messages, q_messages[:1])
     mixed = combine([high, low], [p_messages], q_messages[:1])
     behind, _ = lax.optimization_barrier((given, q_messages[0]))
     got = to_pair(behind)

time: 92.7 us -> 91.1 us (0.983)
  waiting for transfers between devices: 32.4 us -> 30.1 us
    ppermute x12, waiting for transfers between devices: 16 us -> 12.6 us  [to_owner(): return lax.ppermute(a, 'expert', [(i, i ^ j) for i in range(owners)])]
    ppermute x8, waiting for transfers between devices: 16 us -> 17.4 us  [to_chip(): return lax.ppermute(a, 'dp', [(i, i ^ bit(i)) for i in range(devices)])]
    pallas_call x22 -> x23, Pallas kernels: 22.4 us -> 22.4 us  [kernel_call(): return lambda *operands: call(*operands, *after)]
  transfers between devices with their start and end apart: 28 -> 28, of which waited for: 15 -> 15; matrix products, arithmetic and copies ran while one was open for 0% -> 0% of each run, Pallas kernels for 22% -> 23%
where the time goes in v5:
time: 91.1 us; the launch traced here: 90.9 us
  starting transfers between devices  33.3 us (37%)
  waiting for transfers between devices  30.1 us (33%)
  Pallas kernels  22.4 us (25%)
  local copies, waits for them, and re-layouts  4.23 us (5%)
    pallas_call x23, Pallas kernels, kernel_call(): return lambda *operands: call(*operands, *after)  22.4 us
    ppermute x12, starting transfers between devices, to_owner(): return lax.ppermute(a, 'expert', [(i, i ^ j) for i in range(owners)])  19.6 us
    ppermute x8, waiting for transfers between devices, to_chip(): return lax.ppermute(a, 'dp', [(i, i ^ bit(i)) for i in range(devices)])  17.4 us
    ppermute x12, waiting for transfers between devices, to_owner(): return lax.ppermute(a, 'expert', [(i, i ^ j) for i in range(owners)])  12.6 us
    ppermute x8, starting transfers between devices, to_chip(): return lax.ppermute(a, 'dp', [(i, i ^ bit(i)) for i in range(devices)])  11.2 us
    unnamed x16, local copies, waits for them, and re-layouts  4.23 us
    ppermute x8, starting transfers between devices, to_pair(): return lax.ppermute(a, 'dp', [(i, i ^ 1) for i in range(devices)])  2.47 us
  transfers between devices with their start and end apart: 28, of which 15 were waited for; matrix products, arithmetic and copies ran while one was open for 0% of the time, Pallas kernels for 23%

profile of v5, /device:TPU:0, one launch (start us, length us, event | category | flops | bytes accessed | tf_op | source)
XLA Modules:
  0.0 90.9 jit_solution(5304488972681625212)
XLA Ops:
  0.7 1.0 %copy-done.4 = bf16[64,1024]{1,0:T(8,128)(2,1)S(1)} copy-done((bf16[64,1024]{1,0:T(8,128)(2,1)S(1)}, bf16[64,1024]{1,0:T(8,128)(2,1)}, u32[]{:S(2)}) %copy-start.4) | copy-done | bytes 131096
  1.7 0.7 copy-done.6
  2.4 0.6 place_rows.1
  2.9 0.5 collective-permute-start
  3.5 0.9 copy-done.5
  4.4 0.7 copy-done.7
  5.0 0.6 place_scaled.1
  5.6 0.1 collective-permute-start.4
  5.8 0.3 blend.4
  6.1 3.1 %collective-permute-start.1 = (bf16[40,1024]{1,0:T(8,128)(2,1)S(1)}, bf16[40,1024]{1,0:T(8,128)(2,1)S(1)}, u32[]{:S(2)}, u32[]{:S(2)}) collective-permute-start(bf16[40,1024]{1,0:T(8,128)(2,1)S(1)} %get-tuple-element.59), channel_id=1, source_target_pairs={{0,1},{1,0},{2,3},{3,2},{4,5},{5,4},{6,7},{7,6},{8,9},{9,8},{10,11... | collective-permute-start | bytes 245768 | tf_op jit(solution)/shard_map/ppermute | solution.py:434
  9.2 2.6 %collective-permute-start.2 = (bf16[40,1024]{1,0:T(8,128)(2,1)S(1)}, bf16[40,1024]{1,0:T(8,128)(2,1)S(1)}, u32[]{:S(2)}, u32[]{:S(2)}) collective-permute-start(bf16[40,1024]{1,0:T(8,128)(2,1)S(1)} %get-tuple-element.60), channel_id=1, source_target_pairs={{0,2},{1,3},{2,0},{3,1},{4,6},{5,7},{6,4},{7,5},{8,10},{9,11},{10,... | collective-permute-start | bytes 245768 | tf_op jit(solution)/shard_map/ppermute | solution.py:434
  11.8 0.0 collective-permute-start.3
  11.8 0.3 blend.5
  12.1 6.5 %collective-permute-done.2.refs_2_ = bf16[40,1024]{1,0:T(8,128)(2,1)S(1)} collective-permute-done((bf16[40,1024]{1,0:T(8,128)(2,1)S(1)}, bf16[40,1024]{1,0:T(8,128)(2,1)S(1)}, u32[]{:S(2)}, u32[]{:S(2)}) %collective-permute-start.2) | collective-permute-done | bytes 81952 | tf_op jit(solution)/shard_map/ppermute | solution.py:434
  18.6 1.6 %collective-permute-start.5 = (bf16[160,1024]{1,0:T(8,128)(2,1)S(1)}, bf16[160,1024]{1,0:T(8,128)(2,1)S(1)}, u32[]{:S(2)}, u32[]{:S(2)}) collective-permute-start(bf16[160,1024]{1,0:T(8,128)(2,1)S(1)} %join.6.refs_0_.refs_4_), channel_id=1, source_target_pairs={{0,8},{4,20},{8,0},{12,28},{16,24},{20,4},{24,16},{28,12},{1,9},{5... | collective-permute-start | bytes 983048 | tf_op jit(solution)/shard_map/ppermute | solution.py:440
  20.2 1.5 %collective-permute-start.11 = (bf16[40,1024]{1,0:T(8,128)(2,1)S(1)}, bf16[40,1024]{1,0:T(8,128)(2,1)S(1)}, u32[]{:S(2)}, u32[]{:S(2)}) collective-permute-start(bf16[40,1024]{1,0:T(8,128)(2,1)S(1)} %get-tuple-element.69), channel_id=1, source_target_pairs={{0,1},{1,0},{2,3},{3,2},{4,5},{5,4},{6,7},{7,6},{8,9},{9,8},{10,11... | collective-permute-start | bytes 245768 | tf_op jit(solution)/shard_map/ppermute | solution.py:434
  21.7 1.5 %collective-permute-start.12 = (bf16[40,1024]{1,0:T(8,128)(2,1)S(1)}, bf16[40,1024]{1,0:T(8,128)(2,1)S(1)}, u32[]{:S(2)}, u32[]{:S(2)}) collective-permute-start(bf16[40,1024]{1,0:T(8,128)(2,1)S(1)} %get-tuple-element.70), channel_id=1, source_target_pairs={{0,2},{1,3},{2,0},{3,1},{4,6},{5,7},{6,4},{7,5},{8,10},{9,11},{10,... | collective-permute-start | bytes 245768 | tf_op jit(solution)/shard_map/ppermute | solution.py:434
  23.2 1.4 %collective-permute-start.13 = (bf16[40,1024]{1,0:T(8,128)(2,1)S(1)}, bf16[40,1024]{1,0:T(8,128)(2,1)S(1)}, u32[]{:S(2)}, u32[]{:S(2)}) collective-permute-start(bf16[40,1024]{1,0:T(8,128)(2,1)S(1)} %get-tuple-element.71), channel_id=1, source_target_pairs={{0,3},{1,2},{2,1},{3,0},{4,7},{5,6},{6,5},{7,4},{8,11},{9,10},{10,... | collective-permute-start | bytes 245768 | tf_op jit(solution)/shard_map/ppermute | solution.py:434
  24.6 1.4 %collective-permute-done.5.refs_1_ = bf16[160,1024]{1,0:T(8,128)(2,1)S(1)} collective-permute-done((bf16[160,1024]{1,0:T(8,128)(2,1)S(1)}, bf16[160,1024]{1,0:T(8,128)(2,1)S(1)}, u32[]{:S(2)}, u32[]{:S(2)}) %collective-permute-start.5) | collective-permute-done | bytes 327712 | tf_op jit(solution)/shard_map/ppermute | solution.py:440
  26.0 0.0 copy-start.1
  26.0 0.0 copy-start.2
  26.0 1.6 %collective-permute-start.6 = (bf16[320,1024]{1,0:T(8,128)(2,1)S(1)}, bf16[320,1024]{1,0:T(8,128)(2,1)S(1)}, u32[]{:S(2)}, u32[]{:S(2)}) collective-permute-start(bf16[320,1024]{1,0:T(8,128)(2,1)S(1)} %join.7.refs_0_.refs_2_), channel_id=1, source_target_pairs={{0,16},{4,12},{8,24},{12,4},{16,0},{20,28},{24,8},{28,20},{1,17},{... | collective-permute-start | bytes 1966088 | tf_op jit(solution)/shard_map/ppermute | solution.py:440
  27.6 0.5 collective-permute-start.8
  28.1 1.8 %collective-permute-done.12.refs_2_ = bf16[40,1024]{1,0:T(8,128)(2,1)S(1)} collective-permute-done((bf16[40,1024]{1,0:T(8,128)(2,1)S(1)}, bf16[40,1024]{1,0:T(8,128)(2,1)S(1)}, u32[]{:S(2)}, u32[]{:S(2)}) %collective-permute-start.12) | collective-permute-done | bytes 81952 | tf_op jit(solution)/shard_map/ppermute | solution.py:434
  29.9 1.2 %collective-permute-start.14 = (bf16[160,1024]{1,0:T(8,128)(2,1)S(1)}, bf16[160,1024]{1,0:T(8,128)(2,1)S(1)}, u32[]{:S(2)}, u32[]{:S(2)}) collective-permute-start(bf16[160,1024]{1,0:T(8,128)(2,1)S(1)} %join.8.refs_0_), channel_id=1, source_target_pairs={{0,8},{4,20},{8,0},{12,28},{16,24},{20,4},{24,16},{28,12},{1,9},{5... | collective-permute-start | bytes 983048 | tf_op jit(solution)/shard_map/ppermute | solution.py:440
  31.2 5.9 %collective-permute-done.14.refs_1_ = bf16[160,1024]{1,0:T(8,128)(2,1)S(1)} collective-permute-done((bf16[160,1024]{1,0:T(8,128)(2,1)S(1)}, bf16[160,1024]{1,0:T(8,128)(2,1)S(1)}, u32[]{:S(2)}, u32[]{:S(2)}) %collective-permute-start.14) | collective-permute-done | bytes 327712 | tf_op jit(solution)/shard_map/ppermute | solution.py:440
  37.1 1.2 %collective-permute-start.15 = (bf16[320,1024]{1,0:T(8,128)(2,1)S(1)}, bf16[320,1024]{1,0:T(8,128)(2,1)S(1)}, u32[]{:S(2)}, u32[]{:S(2)}) collective-permute-start(bf16[320,1024]{1,0:T(8,128)(2,1)S(1)} %join.9.refs_0_), channel_id=1, source_target_pairs={{0,16},{4,12},{8,24},{12,4},{16,0},{20,28},{24,8},{28,20},{1,17},{... | collective-permute-start | bytes 1966088 | tf_op jit(solution)/shard_map/ppermute | solution.py:440
  38.4 1.8 %collective-permute-done.6.refs_1_ = bf16[320,1024]{1,0:T(8,128)(2,1)S(1)} collective-permute-done((bf16[320,1024]{1,0:T(8,128)(2,1)S(1)}, bf16[320,1024]{1,0:T(8,128)(2,1)S(1)}, u32[]{:S(2)}, u32[]{:S(2)}) %collective-permute-start.6) | collective-permute-done | bytes 655392 | tf_op jit(solution)/shard_map/ppermute | solution.py:440
  40.2 4.9 %forward.1 = (bf16[320,1024]{1,0:T(8,128)(2,1)S(1)}, bf16[320,1024]{1,0:T(8,128)(2,1)S(1)}, bf16[640,1024]{1,0:T(8,128)(2,1)S(1)}, bf16[2,640,512]{2,1,0:T(8,128...) custom-call(bf16[320,1024]{1,0:T(8,128)(2,1)S(1)} %join.7.refs_0_.refs_2_, ...), custom_call_target="tpu_custom_call" | custom-call | flops 4026531840 | tf_op jit(solution)/shard_map/forward/pallas_call | solution.py:53
  45.1 1.6 %collective-permute-start.10 = (bf16[320,1024]{1,0:T(8,128)(2,1)S(1)}, bf16[320,1024]{1,0:T(8,128)(2,1)S(1)}, u32[]{:S(2)}, u32[]{:S(2)}) collective-permute-start(bf16[320,1024]{1,0:T(8,128)(2,1)S(1)} %get-tuple-element.68), channel_id=1, source_target_pairs={{0,16},{4,12},{8,24},{12,4},{16,0},{20,28},{24,8},{28,20},{1,17},{... | collective-permute-start | bytes 1966088 | tf_op jit(solution)/shard_map/ppermute | solution.py:440
  46.7 1.1 %collective-permute-done.15.refs_1_ = bf16[320,1024]{1,0:T(8,128)(2,1)S(1)} collective-permute-done((bf16[320,1024]{1,0:T(8,128)(2,1)S(1)}, bf16[320,1024]{1,0:T(8,128)(2,1)S(1)}, u32[]{:S(2)}, u32[]{:S(2)}) %collective-permute-start.15) | collective-permute-done | bytes 655392 | tf_op jit(solution)/shard_map/ppermute | solution.py:440
  47.8 4.4 %backward.1 = (bf16[320,1024]{1,0:T(8,128)(2,1)S(1)}, bf16[320,1024]{1,0:T(8,128)(2,1)S(1)}, bf16[640,1024]{1,0:T(8,128)(2,1)S(1)}, bf16[2,640,512]{2,1,0:T(8,128)(2,1)S(1)}, bf16[2,640,512]{2,1,0:T(8,128)(2,1)S(1)}) custom-call(bf16[320,1024]{1,0:T(8,128)(2,1)S(1)} %join.9.refs_0_, bf16[320,1024]{1,0:T(8,128)(2,1)S(1)} %collective-permute-done.15.refs_1_, ...), custom_call_target="tpu_custom_call" | custom-call | flops 4026531840 | tf_op jit(solution)/shard_map/backward/pallas_call | solution.py:53
  52.2 1.2 %collective-permute-start.17 = (bf16[320,1024]{1,0:T(8,128)(2,1)S(1)}, bf16[320,1024]{1,0:T(8,128)(2,1)S(1)}, u32[]{:S(2)}, u32[]{:S(2)}) collective-permute-start(bf16[320,1024]{1,0:T(8,128)(2,1)S(1)} %get-tuple-element.78), channel_id=1, source_target_pairs={{0,16},{4,12},{8,24},{12,4},{16,0},{20,28},{24,8},{28,20},{1,17},{... | collective-permute-start | bytes 1966088 | tf_op jit(solution)/shard_map/ppermute | solution.py:440
  53.4 2.3 %collective-permute-done.10.refs_1_ = bf16[320,1024]{1,0:T(8,128)(2,1)S(1)} collective-permute-done((bf16[320,1024]{1,0:T(8,128)(2,1)S(1)}, bf16[320,1024]{1,0:T(8,128)(2,1)S(1)}, u32[]{:S(2)}, u32[]{:S(2)}) %collective-permute-start.10) | collective-permute-done | bytes 655392 | tf_op jit(solution)/shard_map/ppermute | solution.py:440
  55.7 0.2 add.9
  55.9 1.6 %collective-permute-start.16 = (bf16[160,1024]{1,0:T(8,128)(2,1)S(1)}, bf16[160,1024]{1,0:T(8,128)(2,1)S(1)}, u32[]{:S(2)}, u32[]{:S(2)}) collective-permute-start(bf16[160,1024]{1,0:T(8,128)(2,1)S(1)} %get-tuple-element.76.refs_6_), channel_id=1, source_target_pairs={{0,8},{4,20},{8,0},{12,28},{16,24},{20,4},{24,16},{28,12},{1,9},{5... | collective-permute-start | bytes 983048 | tf_op jit(solution)/shard_map/ppermute | solution.py:440
  57.5 2.7 %grads_given.1 = (bf16[3,1024,512]{2,1,0:T(8,128)(2,1)S(1)}, bf16[16,128]{1,0:T(8,128)(2,1)S(1)}) custom-call(s32[1]{0:T(128)} %bitcast.3.refs_0_.refs_2_, bf16[640,1024]{1,0:T(8,128)(2,1)S(1)} %get-tuple-element.79.refs_1_, bf16[640,1024]{1,0:T(8,128)(2,1)S(1)} %get-tuple-element.74.refs_2_, bf16[2,640,512]{2,1,0:T(8,128)(2,1)S(1)} %get-tuple-element.80.refs_3_, ...), custom_call_target="tpu_custom_call" | custom-call | flops 2013265920 | tf_op jit(solution)/shard_map/grads_given/pallas_call | solution.py:53
  60.1 3.9 %grads_kept.1 = (bf16[2,1024,512]{2,1,0:T(8,128)(2,1)}, bf16[2,1024,512]{2,1,0:T(8,128)(2,1)}, bf16[2,512,1024]{2,1,0:T(8,128)(2,1)}, bf16[16,128]{1,0:T(8,128)(2,1)S(1)}) custom-call(s32[1]{0:T(128)} %bitcast.3.refs_0_.refs_2_, bf16[640,1024]{1,0:T(8,128)(2,1)S(1)} %get-tuple-element.79.refs_1_, bf16[640,1024]{1,0:T(8,128)(2,1)S(1)} %get-tuple-element.74.refs_2_, ...), custom_call_target="tpu_custom_call" | custom-call | flops 2013265920 | tf_op jit(solution)/shard_map/grads_kept/pallas_call | solution.py:53
  64.0 1.6 %collective-permute-done.17.refs_1_ = bf16[320,1024]{1,0:T(8,128)(2,1)S(1)} collective-permute-done((bf16[320,1024]{1,0:T(8,128)(2,1)S(1)}, bf16[320,1024]{1,0:T(8,128)(2,1)S(1)}, u32[]{:S(2)}, u32[]{:S(2)}) %collective-permute-start.17) | collective-permute-done | bytes 655392 | tf_op jit(solution)/shard_map/ppermute | solution.py:440
  65.6 0.2 add.10
  65.8 0.9 collective-permute-done.16.refs_1_
  66.6 0.1 add.11.refs_1_
  66.7 1.2 %collective-permute-start.18 = (bf16[160,1024]{1,0:T(8,128)(2,1)S(1)}, bf16[160,1024]{1,0:T(8,128)(2,1)S(1)}, u32[]{:S(2)}, u32[]{:S(2)}) collective-permute-start(bf16[160,1024]{1,0:T(8,128)(2,1)S(1)} %add.11.refs_1_), channel_id=1, source_target_pairs={{0,4},{4,0},{8,12},{12,8},{16,20},{20,16},{24,28},{28,24},{1,5},{5... | collective-permute-start | bytes 983048 | tf_op jit(solution)/shard_map/ppermute | solution.py:431
  67.9 1.2 %collective-permute-start.22 = (bf16[160,1024]{1,0:T(8,128)(2,1)S(1)}, bf16[160,1024]{1,0:T(8,128)(2,1)S(1)}, u32[]{:S(2)}, u32[]{:S(2)}) collective-permute-start(bf16[160,1024]{1,0:T(8,128)(2,1)S(1)} %get-tuple-element.85.refs_2_), channel_id=1, source_target_pairs={{0,8},{4,20},{8,0},{12,28},{16,24},{20,4},{24,16},{28,12},{1,9},{5... | collective-permute-start | bytes 983048 | tf_op jit(solution)/shard_map/ppermute | solution.py:440
  69.1 0.1 collective-permute-done.18.refs_2_
  69.1 0.3 blend.6
  69.5 1.1 %collective-permute-start.19 = (bf16[40,1024]{1,0:T(8,128)(2,1)S(1)}, bf16[40,1024]{1,0:T(8,128)(2,1)S(1)}, u32[]{:S(2)}, u32[]{:S(2)}) collective-permute-start(bf16[40,1024]{1,0:T(8,128)(2,1)S(1)} %get-tuple-element.87), channel_id=1, source_target_pairs={{0,1},{1,0},{2,3},{3,2},{4,5},{5,4},{6,7},{7,6},{8,9},{9,8},{10,11... | collective-permute-start | bytes 245768 | tf_op jit(solution)/shard_map/ppermute | solution.py:434
  70.6 2.0 %collective-permute-start.20 = (bf16[40,1024]{1,0:T(8,128)(2,1)S(1)}, bf16[40,1024]{1,0:T(8,128)(2,1)S(1)}, u32[]{:S(2)}, u32[]{:S(2)}) collective-permute-start(bf16[40,1024]{1,0:T(8,128)(2,1)S(1)} %get-tuple-element.88), channel_id=1, source_target_pairs={{0,2},{1,3},{2,0},{3,1},{4,6},{5,7},{6,4},{7,5},{8,10},{9,11},{10,... | collective-permute-start | bytes 245768 | tf_op jit(solution)/shard_map/ppermute | solution.py:434
  72.6 2.4 %collective-permute-done.22.refs_1_ = bf16[160,1024]{1,0:T(8,128)(2,1)S(1)} collective-permute-done((bf16[160,1024]{1,0:T(8,128)(2,1)S(1)}, bf16[160,1024]{1,0:T(8,128)(2,1)S(1)}, u32[]{:S(2)}, u32[]{:S(2)}) %collective-permute-start.22) | collective-permute-done | bytes 327712 | tf_op jit(solution)/shard_map/ppermute | solution.py:440
  75.0 0.1 add.12.refs_3_.refs_1_
  75.0 0.1 collective-permute-start.23
  75.1 0.2 collective-permute-done.19.refs_1_
  75.3 2.2 %collective-permute-done.20.refs_2_ = bf16[40,1024]{1,0:T(8,128)(2,1)S(1)} collective-permute-done((bf16[40,1024]{1,0:T(8,128)(2,1)S(1)}, bf16[40,1024]{1,0:T(8,128)(2,1)S(1)}, u32[]{:S(2)}, u32[]{:S(2)}) %collective-permute-start.20) | collective-permute-done | bytes 81952 | tf_op jit(solution)/shard_map/ppermute | solution.py:434
  77.5 0.3 blend.7
  77.8 0.1 collective-permute-start.27
  77.9 2.1 %collective-permute-start.21 = (bf16[40,1024]{1,0:T(8,128)(2,1)S(1)}, bf16[40,1024]{1,0:T(8,128)(2,1)S(1)}, u32[]{:S(2)}, u32[]{:S(2)}) collective-permute-start(bf16[40,1024]{1,0:T(8,128)(2,1)S(1)} %get-tuple-element.89), channel_id=1, source_target_pairs={{0,3},{1,2},{2,1},{3,0},{4,7},{5,6},{6,5},{7,4},{8,11},{9,10},{10,... | collective-permute-start | bytes 245768 | tf_op jit(solution)/shard_map/ppermute | solution.py:434
  80.0 2.3 %collective-permute-start.25 = (bf16[40,1024]{1,0:T(8,128)(2,1)S(1)}, bf16[40,1024]{1,0:T(8,128)(2,1)S(1)}, u32[]{:S(2)}, u32[]{:S(2)}) collective-permute-start(bf16[40,1024]{1,0:T(8,128)(2,1)S(1)} %get-tuple-element.94), channel_id=1, source_target_pairs={{0,2},{1,3},{2,0},{3,1},{4,6},{5,7},{6,4},{7,5},{8,10},{9,11},{10,... | collective-permute-start | bytes 245768 | tf_op jit(solution)/shard_map/ppermute | solution.py:434
  82.3 2.0 %collective-permute-start.26 = (bf16[40,1024]{1,0:T(8,128)(2,1)S(1)}, bf16[40,1024]{1,0:T(8,128)(2,1)S(1)}, u32[]{:S(2)}, u32[]{:S(2)}) collective-permute-start(bf16[40,1024]{1,0:T(8,128)(2,1)S(1)} %get-tuple-element.95), channel_id=1, source_target_pairs={{0,3},{1,2},{2,1},{3,0},{4,7},{5,6},{6,5},{7,4},{8,11},{9,10},{10,... | collective-permute-start | bytes 245768 | tf_op jit(solution)/shard_map/ppermute | solution.py:434
  84.4 0.7 collective-permute-done.21.refs_3_
  85.1 0.9 %combine.2.refs_5_ = bf16[64,1024]{1,0:T(8,128)(2,1)} custom-call(bf16[160,64]{1,0:T(8,128)(2,1)S(1)} %get-tuple-element.56.refs_0_, bf16[160,64]{1,0:T(8,128)(2,1)S(1)} %get-tuple-element.57.refs_1_, bf16[160,1024]{1,0:T(8,128)(2,1)S(1)} %join.11.refs_2_, bf16[40,1024]{1,0:T(8,128)(2,1)S(1)} %get-tuple-element.91.refs_4_.refs_3_.refs_1_), custom_call_target="tpu_custom_call" | custom-call | tf_op jit(solution)/shard_map/combine/pallas_call | solution.py:53
  86.0 0.9 copy-done.3
  86.9 1.7 %finish.1 = (bf16[2,1024,512]{2,1,0:T(8,128)(2,1)}, bf16[2,1024,512]{2,1,0:T(8,128)(2,1)}, bf16[2,512,1024]{2,1,0:T(8,128)(2,1)}, bf16[16,128]{1,0:T(8,128)(2,1)S(1)}) custom-call(s32[1]{0:T(128)} %bitcast.3.refs_0_.refs_2_, bf16[3,1024,512]{2,1,0:T(8,128)(2,1)S(1)} %collective-permute-done.27.refs_1_, ...), custom_call_target="tpu_custom_call", output_to_operand_aliasing={{0}: (2, {}), {1}: (3, {}), {2}: (4, {})} | custom-call | tf_op jit(solution)/shard_map/finish/pallas_call | solution.py:53
  88.6 1.4 %collective-permute-done.25.refs_3_ = bf16[40,1024]{1,0:T(8,128)(2,1)S(1)} collective-permute-done((bf16[40,1024]{1,0:T(8,128)(2,1)S(1)}, bf16[40,1024]{1,0:T(8,128)(2,1)S(1)}, u32[]{:S(2)}, u32[]{:S(2)}) %collective-permute-start.25) | collective-permute-done | bytes 81952 | tf_op jit(solution)/shard_map/ppermute | solution.py:434
  90.0 0.9 combine.3
  (31 shorter events, 0.2 us)
Async XLA Ops:
  0.6 27.0 %copy-start = (bf16[2,1024,512]{2,1,0:T(8,128)(2,1)S(1)}, bf16[2,1024,512]{2,1,0:T(8,128)(2,1)}, u32[]{:S(2)}) copy-start(bf16[2,1024,512]{2,1,0:T(8,128)(2,1)} %refs_3_.5) | copy-start | bytes 6291460
  0.6 1.1 %copy-start.4 = (bf16[64,1024]{1,0:T(8,128)(2,1)S(1)}, bf16[64,1024]{1,0:T(8,128)(2,1)}, u32[]{:S(2)}) copy-start(bf16[64,1024]{1,0:T(8,128)(2,1)} %refs_2_.1) | copy-start | bytes 393220
  1.7 0.7 copy-start.6
  2.9 2.8 %collective-permute-start = (bf16[160,1024]{1,0:T(8,128)(2,1)S(1)}, bf16[160,1024]{1,0:T(8,128)(2,1)S(1)}, u32[]{:S(2)}, u32[]{:S(2)}) collective-permute-start(bf16[160,1024]{1,0:T(8,128)(2,1)S(1)} %get-tuple-element.55.refs_4_.refs_1_), channel_id=1, source_target_pairs={{0,4},{4,0},{8,12},{12,8},{16,20},{20,16},{24,28},{28,24},{1,5},{5... | collective-permute-start | bytes 983048 | tf_op jit(solution)/shard_map/ppermute | solution.py:431
  3.5 0.9 copy-start.5
  4.4 0.7 copy-start.7
  5.6 6.2 %collective-permute-start.4 = (bf16[160,1024]{1,0:T(8,128)(2,1)S(1)}, bf16[160,1024]{1,0:T(8,128)(2,1)S(1)}, u32[]{:S(2)}, u32[]{:S(2)}) collective-permute-start(bf16[160,1024]{1,0:T(8,128)(2,1)S(1)} %get-tuple-element.62.refs_1_), channel_id=1, source_target_pairs={{0,4},{4,0},{8,12},{12,8},{16,20},{20,16},{24,28},{28,24},{1,5},{5... | collective-permute-start | bytes 983048 | tf_op jit(solution)/shard_map/ppermute | solution.py:431
  6.1 6.0 %collective-permute-start.1 = (bf16[40,1024]{1,0:T(8,128)(2,1)S(1)}, bf16[40,1024]{1,0:T(8,128)(2,1)S(1)}, u32[]{:S(2)}, u32[]{:S(2)}) collective-permute-start(bf16[40,1024]{1,0:T(8,128)(2,1)S(1)} %get-tuple-element.59), channel_id=1, source_target_pairs={{0,1},{1,0},{2,3},{3,2},{4,5},{5,4},{6,7},{7,6},{8,9},{9,8},{10,11... | collective-permute-start | bytes 245768 | tf_op jit(solution)/shard_map/ppermute | solution.py:434
  9.2 9.4 %collective-permute-start.2 = (bf16[40,1024]{1,0:T(8,128)(2,1)S(1)}, bf16[40,1024]{1,0:T(8,128)(2,1)S(1)}, u32[]{:S(2)}, u32[]{:S(2)}) collective-permute-start(bf16[40,1024]{1,0:T(8,128)(2,1)S(1)} %get-tuple-element.60), channel_id=1, source_target_pairs={{0,2},{1,3},{2,0},{3,1},{4,6},{5,7},{6,4},{7,5},{8,10},{9,11},{10,... | collective-permute-start | bytes 245768 | tf_op jit(solution)/shard_map/ppermute | solution.py:434
  11.8 6.8 %collective-permute-start.3 = (bf16[40,1024]{1,0:T(8,128)(2,1)S(1)}, bf16[40,1024]{1,0:T(8,128)(2,1)S(1)}, u32[]{:S(2)}, u32[]{:S(2)}) collective-permute-start(bf16[40,1024]{1,0:T(8,128)(2,1)S(1)} %get-tuple-element.61), channel_id=1, source_target_pairs={{0,3},{1,2},{2,1},{3,0},{4,7},{5,6},{6,5},{7,4},{8,11},{9,10},{10,... | collective-permute-start | bytes 245768 | tf_op jit(solution)/shard_map/ppermute | solution.py:434
  18.6 7.3 %collective-permute-start.5 = (bf16[160,1024]{1,0:T(8,128)(2,1)S(1)}, bf16[160,1024]{1,0:T(8,128)(2,1)S(1)}, u32[]{:S(2)}, u32[]{:S(2)}) collective-permute-start(bf16[160,1024]{1,0:T(8,128)(2,1)S(1)} %join.6.refs_0_.refs_4_), channel_id=1, source_target_pairs={{0,8},{4,20},{8,0},{12,28},{16,24},{20,4},{24,16},{28,12},{1,9},{5... | collective-permute-start | bytes 983048 | tf_op jit(solution)/shard_map/ppermute | solution.py:440
  20.2 7.4 %collective-permute-start.11 = (bf16[40,1024]{1,0:T(8,128)(2,1)S(1)}, bf16[40,1024]{1,0:T(8,128)(2,1)S(1)}, u32[]{:S(2)}, u32[]{:S(2)}) collective-permute-start(bf16[40,1024]{1,0:T(8,128)(2,1)S(1)} %get-tuple-element.69), channel_id=1, source_target_pairs={{0,1},{1,0},{2,3},{3,2},{4,5},{5,4},{6,7},{7,6},{8,9},{9,8},{10,11... | collective-permute-start | bytes 245768 | tf_op jit(solution)/shard_map/ppermute | solution.py:434
  21.7 8.2 %collective-permute-start.12 = (bf16[40,1024]{1,0:T(8,128)(2,1)S(1)}, bf16[40,1024]{1,0:T(8,128)(2,1)S(1)}, u32[]{:S(2)}, u32[]{:S(2)}) collective-permute-start(bf16[40,1024]{1,0:T(8,128)(2,1)S(1)} %get-tuple-element.70), channel_id=1, source_target_pairs={{0,2},{1,3},{2,0},{3,1},{4,6},{5,7},{6,4},{7,5},{8,10},{9,11},{10,... | collective-permute-start | bytes 245768 | tf_op jit(solution)/shard_map/ppermute | solution.py:434
  23.2 6.7 %collective-permute-start.13 = (bf16[40,1024]{1,0:T(8,128)(2,1)S(1)}, bf16[40,1024]{1,0:T(8,128)(2,1)S(1)}, u32[]{:S(2)}, u32[]{:S(2)}) collective-permute-start(bf16[40,1024]{1,0:T(8,128)(2,1)S(1)} %get-tuple-element.71), channel_id=1, source_target_pairs={{0,3},{1,2},{2,1},{3,0},{4,7},{5,6},{6,5},{7,4},{8,11},{9,10},{10,... | collective-permute-start | bytes 245768 | tf_op jit(solution)/shard_map/ppermute | solution.py:434
  26.0 14.2 %copy-start.1 = (bf16[2,1024,512]{2,1,0:T(8,128)(2,1)S(1)}, bf16[2,1024,512]{2,1,0:T(8,128)(2,1)}, u32[]{:S(2)}) copy-start(bf16[2,1024,512]{2,1,0:T(8,128)(2,1)} %refs_4_.3) | copy-start | bytes 6291460
  26.0 14.2 %copy-start.2 = (bf16[2,512,1024]{2,1,0:T(8,128)(2,1)S(1)}, bf16[2,512,1024]{2,1,0:T(8,128)(2,1)}, u32[]{:S(2)}) copy-start(bf16[2,512,1024]{2,1,0:T(8,128)(2,1)} %refs_5_.3) | copy-start | bytes 6291460
  26.0 14.2 %collective-permute-start.6 = (bf16[320,1024]{1,0:T(8,128)(2,1)S(1)}, bf16[320,1024]{1,0:T(8,128)(2,1)S(1)}, u32[]{:S(2)}, u32[]{:S(2)}) collective-permute-start(bf16[320,1024]{1,0:T(8,128)(2,1)S(1)} %join.7.refs_0_.refs_2_), channel_id=1, source_target_pairs={{0,16},{4,12},{8,24},{12,4},{16,0},{20,28},{24,8},{28,20},{1,17},{... | collective-permute-start | bytes 1966088 | tf_op jit(solution)/shard_map/ppermute | solution.py:440
  27.6 12.6 %collective-permute-start.7 = (bf16[2,1024,512]{2,1,0:T(8,128)(2,1)S(1)}, bf16[2,1024,512]{2,1,0:T(8,128)(2,1)S(1)}, u32[]{:S(2)}, u32[]{:S(2)}) collective-permute-start(bf16[2,1024,512]{2,1,0:T(8,128)(2,1)S(1)} %copy-done), channel_id=1, source_target_pairs={{0,4},{4,0},{8,12},{12,8},{16,20},{20,16},{24,28},{28,24},{1,5},{5... | collective-permute-start | bytes 6291464 | tf_op jit(solution)/shard_map/ppermute | solution.py:431
  27.6 12.6 %collective-permute-start.8 = (bf16[2,1024,512]{2,1,0:T(8,128)(2,1)}, bf16[2,1024,512]{2,1,0:T(8,128)(2,1)S(1)}, u32[]{:S(2)}, u32[]{:S(2)}) collective-permute-start(bf16[2,1024,512]{2,1,0:T(8,128)(2,1)} %refs_4_.3), channel_id=1, source_target_pairs={{0,4},{4,0},{8,12},{12,8},{16,20},{20,16},{24,28},{28,24},{1,5},{5... | collective-permute-start | bytes 6291464 | tf_op jit(solution)/shard_map/ppermute | solution.py:431
  29.9 10.3 %collective-permute-start.9 = (bf16[2,512,1024]{2,1,0:T(8,128)(2,1)}, bf16[2,512,1024]{2,1,0:T(8,128)(2,1)S(1)}, u32[]{:S(2)}, u32[]{:S(2)}) collective-permute-start(bf16[2,512,1024]{2,1,0:T(8,128)(2,1)} %refs_5_.3), channel_id=1, source_target_pairs={{0,4},{4,0},{8,12},{12,8},{16,20},{20,16},{24,28},{28,24},{1,5},{5... | collective-permute-start | bytes 6291464 | tf_op jit(solution)/shard_map/ppermute | solution.py:431
  29.9 7.1 %collective-permute-start.14 = (bf16[160,1024]{1,0:T(8,128)(2,1)S(1)}, bf16[160,1024]{1,0:T(8,128)(2,1)S(1)}, u32[]{:S(2)}, u32[]{:S(2)}) collective-permute-start(bf16[160,1024]{1,0:T(8,128)(2,1)S(1)} %join.8.refs_0_), channel_id=1, source_target_pairs={{0,8},{4,20},{8,0},{12,28},{16,24},{20,4},{24,16},{28,12},{1,9},{5... | collective-permute-start | bytes 983048 | tf_op jit(solution)/shard_map/ppermute | solution.py:440
  37.1 10.7 %collective-permute-start.15 = (bf16[320,1024]{1,0:T(8,128)(2,1)S(1)}, bf16[320,1024]{1,0:T(8,128)(2,1)S(1)}, u32[]{:S(2)}, u32[]{:S(2)}) collective-permute-start(bf16[320,1024]{1,0:T(8,128)(2,1)S(1)} %join.9.refs_0_), channel_id=1, source_target_pairs={{0,16},{4,12},{8,24},{12,4},{16,0},{20,28},{24,8},{28,20},{1,17},{... | collective-permute-start | bytes 1966088 | tf_op jit(solution)/shard_map/ppermute | solution.py:440
  45.1 10.7 %collective-permute-start.10 = (bf16[320,1024]{1,0:T(8,128)(2,1)S(1)}, bf16[320,1024]{1,0:T(8,128)(2,1)S(1)}, u32[]{:S(2)}, u32[]{:S(2)}) collective-permute-start(bf16[320,1024]{1,0:T(8,128)(2,1)S(1)} %get-tuple-element.68), channel_id=1, source_target_pairs={{0,16},{4,12},{8,24},{12,4},{16,0},{20,28},{24,8},{28,20},{1,17},{... | collective-permute-start | bytes 1966088 | tf_op jit(solution)/shard_map/ppermute | solution.py:440
  52.2 13.4 %collective-permute-start.17 = (bf16[320,1024]{1,0:T(8,128)(2,1)S(1)}, bf16[320,1024]{1,0:T(8,128)(2,1)S(1)}, u32[]{:S(2)}, u32[]{:S(2)}) collective-permute-start(bf16[320,1024]{1,0:T(8,128)(2,1)S(1)} %get-tuple-element.78), channel_id=1, source_target_pairs={{0,16},{4,12},{8,24},{12,4},{16,0},{20,28},{24,8},{28,20},{1,17},{... | collective-permute-start | bytes 1966088 | tf_op jit(solution)/shard_map/ppermute | solution.py:440
  55.9 10.7 %collective-permute-start.16 = (bf16[160,1024]{1,0:T(8,128)(2,1)S(1)}, bf16[160,1024]{1,0:T(8,128)(2,1)S(1)}, u32[]{:S(2)}, u32[]{:S(2)}) collective-permute-start(bf16[160,1024]{1,0:T(8,128)(2,1)S(1)} %get-tuple-element.76.refs_6_), channel_id=1, source_target_pairs={{0,8},{4,20},{8,0},{12,28},{16,24},{20,4},{24,16},{28,12},{1,9},{5... | collective-permute-start | bytes 983048 | tf_op jit(solution)/shard_map/ppermute | solution.py:440
  66.7 2.4 %collective-permute-start.18 = (bf16[160,1024]{1,0:T(8,128)(2,1)S(1)}, bf16[160,1024]{1,0:T(8,128)(2,1)S(1)}, u32[]{:S(2)}, u32[]{:S(2)}) collective-permute-start(bf16[160,1024]{1,0:T(8,128)(2,1)S(1)} %add.11.refs_1_), channel_id=1, source_target_pairs={{0,4},{4,0},{8,12},{12,8},{16,20},{20,16},{24,28},{28,24},{1,5},{5... | collective-permute-start | bytes 983048 | tf_op jit(solution)/shard_map/ppermute | solution.py:431
  67.9 7.1 %collective-permute-start.22 = (bf16[160,1024]{1,0:T(8,128)(2,1)S(1)}, bf16[160,1024]{1,0:T(8,128)(2,1)S(1)}, u32[]{:S(2)}, u32[]{:S(2)}) collective-permute-start(bf16[160,1024]{1,0:T(8,128)(2,1)S(1)} %get-tuple-element.85.refs_2_), channel_id=1, source_target_pairs={{0,8},{4,20},{8,0},{12,28},{16,24},{20,4},{24,16},{28,12},{1,9},{5... | collective-permute-start | bytes 983048 | tf_op jit(solution)/shard_map/ppermute | solution.py:440
  69.5 5.8 %collective-permute-start.19 = (bf16[40,1024]{1,0:T(8,128)(2,1)S(1)}, bf16[40,1024]{1,0:T(8,128)(2,1)S(1)}, u32[]{:S(2)}, u32[]{:S(2)}) collective-permute-start(bf16[40,1024]{1,0:T(8,128)(2,1)S(1)} %get-tuple-element.87), channel_id=1, source_target_pairs={{0,1},{1,0},{2,3},{3,2},{4,5},{5,4},{6,7},{7,6},{8,9},{9,8},{10,11... | collective-permute-start | bytes 245768 | tf_op jit(solution)/shard_map/ppermute | solution.py:434
  70.6 6.9 %collective-permute-start.20 = (bf16[40,1024]{1,0:T(8,128)(2,1)S(1)}, bf16[40,1024]{1,0:T(8,128)(2,1)S(1)}, u32[]{:S(2)}, u32[]{:S(2)}) collective-permute-start(bf16[40,1024]{1,0:T(8,128)(2,1)S(1)} %get-tuple-element.88), channel_id=1, source_target_pairs={{0,2},{1,3},{2,0},{3,1},{4,6},{5,7},{6,4},{7,5},{8,10},{9,11},{10,... | collective-permute-start | bytes 245768 | tf_op jit(solution)/shard_map/ppermute | solution.py:434
  75.0 2.4 %collective-permute-start.23 = (bf16[160,1024]{1,0:T(8,128)(2,1)S(1)}, bf16[160,1024]{1,0:T(8,128)(2,1)S(1)}, u32[]{:S(2)}, u32[]{:S(2)}) collective-permute-start(bf16[160,1024]{1,0:T(8,128)(2,1)S(1)} %add.12.refs_3_.refs_1_), channel_id=1, source_target_pairs={{0,4},{4,0},{8,12},{12,8},{16,20},{20,16},{24,28},{28,24},{1,5},{5... | collective-permute-start | bytes 983048 | tf_op jit(solution)/shard_map/ppermute | solution.py:431
  77.8 8.2 %collective-permute-start.27 = (bf16[3,1024,512]{2,1,0:T(8,128)(2,1)S(1)}, bf16[3,1024,512]{2,1,0:T(8,128)(2,1)S(1)}, u32[]{:S(2)}, u32[]{:S(2)}) collective-permute-start(bf16[3,1024,512]{2,1,0:T(8,128)(2,1)S(1)} %get-tuple-element.97), channel_id=1, source_target_pairs={{0,4},{4,0},{8,12},{12,8},{16,20},{20,16},{24,28},{28,24},{1,5},{5... | collective-permute-start | bytes 9437192 | tf_op jit(solution)/shard_map/ppermute | solution.py:431
  77.9 7.2 %collective-permute-start.21 = (bf16[40,1024]{1,0:T(8,128)(2,1)S(1)}, bf16[40,1024]{1,0:T(8,128)(2,1)S(1)}, u32[]{:S(2)}, u32[]{:S(2)}) collective-permute-start(bf16[40,1024]{1,0:T(8,128)(2,1)S(1)} %get-tuple-element.89), channel_id=1, source_target_pairs={{0,3},{1,2},{2,1},{3,0},{4,7},{5,6},{6,5},{7,4},{8,11},{9,10},{10,... | collective-permute-start | bytes 245768 | tf_op jit(solution)/shard_map/ppermute | solution.py:434
  80.0 8.6 %collective-permute-start.24 = (bf16[40,1024]{1,0:T(8,128)(2,1)S(1)}, bf16[40,1024]{1,0:T(8,128)(2,1)S(1)}, u32[]{:S(2)}, u32[]{:S(2)}) collective-permute-start(bf16[40,1024]{1,0:T(8,128)(2,1)S(1)} %get-tuple-element.93), channel_id=1, source_target_pairs={{0,1},{1,0},{2,3},{3,2},{4,5},{5,4},{6,7},{7,6},{8,9},{9,8},{10,11... | collective-permute-start | bytes 245768 | tf_op jit(solution)/shard_map/ppermute | solution.py:434
  80.0 10.0 %collective-permute-start.25 = (bf16[40,1024]{1,0:T(8,128)(2,1)S(1)}, bf16[40,1024]{1,0:T(8,128)(2,1)S(1)}, u32[]{:S(2)}, u32[]{:S(2)}) collective-permute-start(bf16[40,1024]{1,0:T(8,128)(2,1)S(1)} %get-tuple-element.94), channel_id=1, source_target_pairs={{0,2},{1,3},{2,0},{3,1},{4,6},{5,7},{6,4},{7,5},{8,10},{9,11},{10,... | collective-permute-start | bytes 245768 | tf_op jit(solution)/shard_map/ppermute | solution.py:434
  82.3 7.7 %collective-permute-start.26 = (bf16[40,1024]{1,0:T(8,128)(2,1)S(1)}, bf16[40,1024]{1,0:T(8,128)(2,1)S(1)}, u32[]{:S(2)}, u32[]{:S(2)}) collective-permute-start(bf16[40,1024]{1,0:T(8,128)(2,1)S(1)} %get-tuple-element.95), channel_id=1, source_target_pairs={{0,3},{1,2},{2,1},{3,0},{4,7},{5,6},{6,5},{7,4},{8,11},{9,10},{10,... | collective-permute-start | bytes 245768 | tf_op jit(solution)/shard_map/ppermute | solution.py:434
  86.0 0.9 copy-start.3

commit v6 on v5

--- a/solution.py
+++ b/solution.py
@@ -411,6 +411,28 @@
     )(*weights, *messages)
 
 
+def combine_both_kernel(high, low, chosen, *refs):
+    count = (len(refs) - 2) // 2
+    first, second = [
+        jnp.concatenate([m[...].astype(F32) for m in part], axis=0).astype(BF)
+        for part in (refs[:count], refs[count : 2 * count])
+    ]
+    refs[-2][...] = (dot(high[...], first, TN) + dot(low[...], first, TN)).astype(BF)
+    refs[-1][...] = dot(chosen[...], second, TN).astype(BF)
+
+
+def combine_both(weights, first, second, after):
+    out = shaped(weights[0].shape[1], first[0].shape[1])
+    return kernel_call(
+        combine_both_kernel,
+        "combine_both",
+        [VMEM] * (3 + len(first) + len(second)),
+        [VMEM] * 2,
+        [out] * 2,
+        after=after,
+    )(*weights, *first, *second)
+
+
 def body(tokens, expert_ids, gate_weights, w_gate, w_up, w_down, cotangent):
     owners = lax.axis_size("expert")
     devices = lax.axis_size("dp")
@@ -479,12 +501,10 @@
     p_messages = swap(p_messages)
     early = join(p_messages[:-1], [q_rows], 20 * FLOPS_PER_US)
     q_messages = hand_out(q_rows, [early])
-    p_messages = join(p_messages, q_messages[:1])
-    mixed = combine([high, low], [p_messages], q_messages[:1])
     behind, _ = lax.optimization_barrier((given, q_messages[0]))
     got = to_pair(behind)
-    grad_gate, grad_up, grad_down, token = finish(core, got, kept, [mixed])
-    grad_tokens = combine([chosen], swap(q_messages), [token])
+    grad_gate, grad_up, grad_down, token = finish(core, got, kept, q_messages[:1])
+    mixed, grad_tokens = combine_both([high, low, chosen], p_messages, swap(q_messages), [token])
     return (mixed, grad_tokens, grad_gate, grad_up, grad_down)
 
 

time: 91.1 us -> 91.2 us (level)
  waiting for transfers between devices: 30.1 us -> 31.8 us
    ppermute x12, waiting for transfers between devices: 12.6 us -> 14.4 us  [to_owner(): return lax.ppermute(a, 'expert', [(i, i ^ j) for i in range(owners)])]
    unnamed x16 -> x14, local copies, waits for them, and re-layouts: 4.23 us -> 3.32 us
    pallas_call x23 -> x21, Pallas kernels: 22.4 us -> 21.7 us  [kernel_call(): return lambda *operands: call(*operands, *after)]
  transfers between devices with their start and end apart: 28 -> 28, of which waited for: 15 -> 15; matrix products, arithmetic and copies ran while one was open for 0% -> 0% of each run, Pallas kernels for 23% -> 22%
where the time goes in v6:
time: 91.2 us; the launch traced here: 91 us
  starting transfers between devices  33.3 us (37%)
  waiting for transfers between devices  31.8 us (35%)
  Pallas kernels  21.7 us (24%)
  local copies, waits for them, and re-layouts  3.32 us (4%)
    pallas_call x21, Pallas kernels, kernel_call(): return lambda *operands: call(*operands, *after)  21.7 us
    ppermute x12, starting transfers between devices, to_owner(): return lax.ppermute(a, 'expert', [(i, i ^ j) for i in range(owners)])  19.7 us
    ppermute x8, waiting for transfers between devices, to_chip(): return lax.ppermute(a, 'dp', [(i, i ^ bit(i)) for i in range(devices)])  17.3 us
    ppermute x12, waiting for transfers between devices, to_owner(): return lax.ppermute(a, 'expert', [(i, i ^ j) for i in range(owners)])  14.4 us
    ppermute x8, starting transfers between devices, to_chip(): return lax.ppermute(a, 'dp', [(i, i ^ bit(i)) for i in range(devices)])  11.1 us
    unnamed x14, local copies, waits for them, and re-layouts  3.32 us
    ppermute x8, starting transfers between devices, to_pair(): return lax.ppermute(a, 'dp', [(i, i ^ 1) for i in range(devices)])  2.44 us
  transfers between devices with their start and end apart: 28, of which 15 were waited for; matrix products, arithmetic and copies ran while one was open for 0% of the time, Pallas kernels for 22%

profile of v6, /device:TPU:0, one launch (start us, length us, event | category | flops | bytes accessed | tf_op | source)
XLA Modules:
  0.0 91.0 jit_solution(5788140468753494842)
XLA Ops:
  0.7 1.0 %copy-done.3 = bf16[64,1024]{1,0:T(8,128)(2,1)S(1)} copy-done((bf16[64,1024]{1,0:T(8,128)(2,1)S(1)}, bf16[64,1024]{1,0:T(8,128)(2,1)}, u32[]{:S(2)}) %copy-start.3) | copy-done | bytes 131096
  1.7 0.7 copy-done.5
  2.4 0.6 place_rows.1
  2.9 0.5 collective-permute-start
  3.5 0.9 copy-done.4
  4.4 0.7 copy-done.6
  5.0 0.6 place_scaled.1
  5.6 0.1 collective-permute-start.4
  5.8 0.0 collective-permute-done.refs_2_
  5.8 0.3 blend.4
  6.1 3.1 %collective-permute-start.1 = (bf16[40,1024]{1,0:T(8,128)(2,1)S(1)}, bf16[40,1024]{1,0:T(8,128)(2,1)S(1)}, u32[]{:S(2)}, u32[]{:S(2)}) collective-permute-start(bf16[40,1024]{1,0:T(8,128)(2,1)S(1)} %get-tuple-element.62), channel_id=1, source_target_pairs={{0,1},{1,0},{2,3},{3,2},{4,5},{5,4},{6,7},{7,6},{8,9},{9,8},{10,11... | collective-permute-start | bytes 245768 | tf_op jit(solution)/shard_map/ppermute | solution.py:456
  9.2 2.6 %collective-permute-start.2 = (bf16[40,1024]{1,0:T(8,128)(2,1)S(1)}, bf16[40,1024]{1,0:T(8,128)(2,1)S(1)}, u32[]{:S(2)}, u32[]{:S(2)}) collective-permute-start(bf16[40,1024]{1,0:T(8,128)(2,1)S(1)} %get-tuple-element.63), channel_id=1, source_target_pairs={{0,2},{1,3},{2,0},{3,1},{4,6},{5,7},{6,4},{7,5},{8,10},{9,11},{10,... | collective-permute-start | bytes 245768 | tf_op jit(solution)/shard_map/ppermute | solution.py:456
  11.8 0.0 collective-permute-start.3
  11.8 0.0 collective-permute-done.4.refs_2_
  11.8 0.3 blend.5
  12.1 6.5 %collective-permute-done.2.refs_2_ = bf16[40,1024]{1,0:T(8,128)(2,1)S(1)} collective-permute-done((bf16[40,1024]{1,0:T(8,128)(2,1)S(1)}, bf16[40,1024]{1,0:T(8,128)(2,1)S(1)}, u32[]{:S(2)}, u32[]{:S(2)}) %collective-permute-start.2) | collective-permute-done | bytes 81952 | tf_op jit(solution)/shard_map/ppermute | solution.py:456
  18.6 1.6 %collective-permute-start.5 = (bf16[160,1024]{1,0:T(8,128)(2,1)S(1)}, bf16[160,1024]{1,0:T(8,128)(2,1)S(1)}, u32[]{:S(2)}, u32[]{:S(2)}) collective-permute-start(bf16[160,1024]{1,0:T(8,128)(2,1)S(1)} %join.5.refs_0_.refs_4_), channel_id=1, source_target_pairs={{0,8},{4,20},{8,0},{12,28},{16,24},{20,4},{24,16},{28,12},{1,9},{5... | collective-permute-start | bytes 983048 | tf_op jit(solution)/shard_map/ppermute | solution.py:462
  20.2 1.5 %collective-permute-start.11 = (bf16[40,1024]{1,0:T(8,128)(2,1)S(1)}, bf16[40,1024]{1,0:T(8,128)(2,1)S(1)}, u32[]{:S(2)}, u32[]{:S(2)}) collective-permute-start(bf16[40,1024]{1,0:T(8,128)(2,1)S(1)} %get-tuple-element.72), channel_id=1, source_target_pairs={{0,1},{1,0},{2,3},{3,2},{4,5},{5,4},{6,7},{7,6},{8,9},{9,8},{10,11... | collective-permute-start | bytes 245768 | tf_op jit(solution)/shard_map/ppermute | solution.py:456
  21.7 1.5 %collective-permute-start.12 = (bf16[40,1024]{1,0:T(8,128)(2,1)S(1)}, bf16[40,1024]{1,0:T(8,128)(2,1)S(1)}, u32[]{:S(2)}, u32[]{:S(2)}) collective-permute-start(bf16[40,1024]{1,0:T(8,128)(2,1)S(1)} %get-tuple-element.73), channel_id=1, source_target_pairs={{0,2},{1,3},{2,0},{3,1},{4,6},{5,7},{6,4},{7,5},{8,10},{9,11},{10,... | collective-permute-start | bytes 245768 | tf_op jit(solution)/shard_map/ppermute | solution.py:456
  23.2 1.4 %collective-permute-start.13 = (bf16[40,1024]{1,0:T(8,128)(2,1)S(1)}, bf16[40,1024]{1,0:T(8,128)(2,1)S(1)}, u32[]{:S(2)}, u32[]{:S(2)}) collective-permute-start(bf16[40,1024]{1,0:T(8,128)(2,1)S(1)} %get-tuple-element.74), channel_id=1, source_target_pairs={{0,3},{1,2},{2,1},{3,0},{4,7},{5,6},{6,5},{7,4},{8,11},{9,10},{10,... | collective-permute-start | bytes 245768 | tf_op jit(solution)/shard_map/ppermute | solution.py:456
  24.6 1.4 %collective-permute-done.5.refs_1_ = bf16[160,1024]{1,0:T(8,128)(2,1)S(1)} collective-permute-done((bf16[160,1024]{1,0:T(8,128)(2,1)S(1)}, bf16[160,1024]{1,0:T(8,128)(2,1)S(1)}, u32[]{:S(2)}, u32[]{:S(2)}) %collective-permute-start.5) | collective-permute-done | bytes 327712 | tf_op jit(solution)/shard_map/ppermute | solution.py:462
  26.0 0.0 copy-start.1
  26.0 0.0 copy-start.2
  26.0 1.6 %collective-permute-start.6 = (bf16[320,1024]{1,0:T(8,128)(2,1)S(1)}, bf16[320,1024]{1,0:T(8,128)(2,1)S(1)}, u32[]{:S(2)}, u32[]{:S(2)}) collective-permute-start(bf16[320,1024]{1,0:T(8,128)(2,1)S(1)} %join.6.refs_0_.refs_2_), channel_id=1, source_target_pairs={{0,16},{4,12},{8,24},{12,4},{16,0},{20,28},{24,8},{28,20},{1,17},{... | collective-permute-start | bytes 1966088 | tf_op jit(solution)/shard_map/ppermute | solution.py:462
  27.6 0.5 collective-permute-start.8
  28.1 1.8 %collective-permute-done.12.refs_2_ = bf16[40,1024]{1,0:T(8,128)(2,1)S(1)} collective-permute-done((bf16[40,1024]{1,0:T(8,128)(2,1)S(1)}, bf16[40,1024]{1,0:T(8,128)(2,1)S(1)}, u32[]{:S(2)}, u32[]{:S(2)}) %collective-permute-start.12) | collective-permute-done | bytes 81952 | tf_op jit(solution)/shard_map/ppermute | solution.py:456
  29.9 1.2 %collective-permute-start.14 = (bf16[160,1024]{1,0:T(8,128)(2,1)S(1)}, bf16[160,1024]{1,0:T(8,128)(2,1)S(1)}, u32[]{:S(2)}, u32[]{:S(2)}) collective-permute-start(bf16[160,1024]{1,0:T(8,128)(2,1)S(1)} %join.7.refs_0_), channel_id=1, source_target_pairs={{0,8},{4,20},{8,0},{12,28},{16,24},{20,4},{24,16},{28,12},{1,9},{5... | collective-permute-start | bytes 983048 | tf_op jit(solution)/shard_map/ppermute | solution.py:462
  31.2 5.9 %collective-permute-done.14.refs_1_ = bf16[160,1024]{1,0:T(8,128)(2,1)S(1)} collective-permute-done((bf16[160,1024]{1,0:T(8,128)(2,1)S(1)}, bf16[160,1024]{1,0:T(8,128)(2,1)S(1)}, u32[]{:S(2)}, u32[]{:S(2)}) %collective-permute-start.14) | collective-permute-done | bytes 327712 | tf_op jit(solution)/shard_map/ppermute | solution.py:462
  37.1 1.2 %collective-permute-start.15 = (bf16[320,1024]{1,0:T(8,128)(2,1)S(1)}, bf16[320,1024]{1,0:T(8,128)(2,1)S(1)}, u32[]{:S(2)}, u32[]{:S(2)}) collective-permute-start(bf16[320,1024]{1,0:T(8,128)(2,1)S(1)} %join.8.refs_0_), channel_id=1, source_target_pairs={{0,16},{4,12},{8,24},{12,4},{16,0},{20,28},{24,8},{28,20},{1,17},{... | collective-permute-start | bytes 1966088 | tf_op jit(solution)/shard_map/ppermute | solution.py:462
  38.4 1.8 %collective-permute-done.6.refs_1_ = bf16[320,1024]{1,0:T(8,128)(2,1)S(1)} collective-permute-done((bf16[320,1024]{1,0:T(8,128)(2,1)S(1)}, bf16[320,1024]{1,0:T(8,128)(2,1)S(1)}, u32[]{:S(2)}, u32[]{:S(2)}) %collective-permute-start.6) | collective-permute-done | bytes 655392 | tf_op jit(solution)/shard_map/ppermute | solution.py:462
  40.2 4.9 %forward.1 = (bf16[320,1024]{1,0:T(8,128)(2,1)S(1)}, bf16[320,1024]{1,0:T(8,128)(2,1)S(1)}, bf16[640,1024]{1,0:T(8,128)(2,1)S(1)}, bf16[2,640,512]{2,1,0:T(8,128...) custom-call(bf16[320,1024]{1,0:T(8,128)(2,1)S(1)} %join.6.refs_0_.refs_2_, ...), custom_call_target="tpu_custom_call" | custom-call | flops 4026531840 | tf_op jit(solution)/shard_map/forward/pallas_call | solution.py:53
  45.1 1.6 %collective-permute-start.10 = (bf16[320,1024]{1,0:T(8,128)(2,1)S(1)}, bf16[320,1024]{1,0:T(8,128)(2,1)S(1)}, u32[]{:S(2)}, u32[]{:S(2)}) collective-permute-start(bf16[320,1024]{1,0:T(8,128)(2,1)S(1)} %get-tuple-element.71), channel_id=1, source_target_pairs={{0,16},{4,12},{8,24},{12,4},{16,0},{20,28},{24,8},{28,20},{1,17},{... | collective-permute-start | bytes 1966088 | tf_op jit(solution)/shard_map/ppermute | solution.py:462
  46.7 1.1 %collective-permute-done.15.refs_1_ = bf16[320,1024]{1,0:T(8,128)(2,1)S(1)} collective-permute-done((bf16[320,1024]{1,0:T(8,128)(2,1)S(1)}, bf16[320,1024]{1,0:T(8,128)(2,1)S(1)}, u32[]{:S(2)}, u32[]{:S(2)}) %collective-permute-start.15) | collective-permute-done | bytes 655392 | tf_op jit(solution)/shard_map/ppermute | solution.py:462
  47.8 4.4 %backward.1 = (bf16[320,1024]{1,0:T(8,128)(2,1)S(1)}, bf16[320,1024]{1,0:T(8,128)(2,1)S(1)}, bf16[640,1024]{1,0:T(8,128)(2,1)S(1)}, bf16[2,640,512]{2,1,0:T(8,128)(2,1)S(1)}, bf16[2,640,512]{2,1,0:T(8,128)(2,1)S(1)}) custom-call(bf16[320,1024]{1,0:T(8,128)(2,1)S(1)} %join.8.refs_0_, bf16[320,1024]{1,0:T(8,128)(2,1)S(1)} %collective-permute-done.15.refs_1_, ...), custom_call_target="tpu_custom_call" | custom-call | flops 4026531840 | tf_op jit(solution)/shard_map/backward/pallas_call | solution.py:53
  52.2 1.2 %collective-permute-start.17 = (bf16[320,1024]{1,0:T(8,128)(2,1)S(1)}, bf16[320,1024]{1,0:T(8,128)(2,1)S(1)}, u32[]{:S(2)}, u32[]{:S(2)}) collective-permute-start(bf16[320,1024]{1,0:T(8,128)(2,1)S(1)} %get-tuple-element.81), channel_id=1, source_target_pairs={{0,16},{4,12},{8,24},{12,4},{16,0},{20,28},{24,8},{28,20},{1,17},{... | collective-permute-start | bytes 1966088 | tf_op jit(solution)/shard_map/ppermute | solution.py:462
  53.4 2.4 %collective-permute-done.10.refs_1_ = bf16[320,1024]{1,0:T(8,128)(2,1)S(1)} collective-permute-done((bf16[320,1024]{1,0:T(8,128)(2,1)S(1)}, bf16[320,1024]{1,0:T(8,128)(2,1)S(1)}, u32[]{:S(2)}, u32[]{:S(2)}) %collective-permute-start.10) | collective-permute-done | bytes 655392 | tf_op jit(solution)/shard_map/ppermute | solution.py:462
  55.8 0.2 add.9
  55.9 1.5 %collective-permute-start.16 = (bf16[160,1024]{1,0:T(8,128)(2,1)S(1)}, bf16[160,1024]{1,0:T(8,128)(2,1)S(1)}, u32[]{:S(2)}, u32[]{:S(2)}) collective-permute-start(bf16[160,1024]{1,0:T(8,128)(2,1)S(1)} %get-tuple-element.79.refs_6_), channel_id=1, source_target_pairs={{0,8},{4,20},{8,0},{12,28},{16,24},{20,4},{24,16},{28,12},{1,9},{5... | collective-permute-start | bytes 983048 | tf_op jit(solution)/shard_map/ppermute | solution.py:462
  57.5 2.7 %grads_given.1 = (bf16[3,1024,512]{2,1,0:T(8,128)(2,1)S(1)}, bf16[16,128]{1,0:T(8,128)(2,1)S(1)}) custom-call(s32[1]{0:T(128)} %bitcast.3.refs_0_.refs_2_, bf16[640,1024]{1,0:T(8,128)(2,1)S(1)} %get-tuple-element.82.refs_1_, bf16[640,1024]{1,0:T(8,128)(2,1)S(1)} %get-tuple-element.77.refs_2_, bf16[2,640,512]{2,1,0:T(8,128)(2,1)S(1)} %get-tuple-element.83.refs_3_, ...), custom_call_target="tpu_custom_call" | custom-call | flops 2013265920 | tf_op jit(solution)/shard_map/grads_given/pallas_call | solution.py:53
  60.2 3.9 %grads_kept.1 = (bf16[2,1024,512]{2,1,0:T(8,128)(2,1)}, bf16[2,1024,512]{2,1,0:T(8,128)(2,1)}, bf16[2,512,1024]{2,1,0:T(8,128)(2,1)}, bf16[16,128]{1,0:T(8,128)(2,1)S(1)}) custom-call(s32[1]{0:T(128)} %bitcast.3.refs_0_.refs_2_, bf16[640,1024]{1,0:T(8,128)(2,1)S(1)} %get-tuple-element.82.refs_1_, bf16[640,1024]{1,0:T(8,128)(2,1)S(1)} %get-tuple-element.77.refs_2_, ...), custom_call_target="tpu_custom_call" | custom-call | flops 2013265920 | tf_op jit(solution)/shard_map/grads_kept/pallas_call | solution.py:53
  64.1 1.5 %collective-permute-done.17.refs_1_ = bf16[320,1024]{1,0:T(8,128)(2,1)S(1)} collective-permute-done((bf16[320,1024]{1,0:T(8,128)(2,1)S(1)}, bf16[320,1024]{1,0:T(8,128)(2,1)S(1)}, u32[]{:S(2)}, u32[]{:S(2)}) %collective-permute-start.17) | collective-permute-done | bytes 655392 | tf_op jit(solution)/shard_map/ppermute | solution.py:462
  65.6 0.2 add.10
  65.8 0.9 collective-permute-done.16.refs_1_
  66.7 0.1 add.11.refs_1_
  66.7 1.1 %collective-permute-start.18 = (bf16[160,1024]{1,0:T(8,128)(2,1)S(1)}, bf16[160,1024]{1,0:T(8,128)(2,1)S(1)}, u32[]{:S(2)}, u32[]{:S(2)}) collective-permute-start(bf16[160,1024]{1,0:T(8,128)(2,1)S(1)} %add.11.refs_1_), channel_id=1, source_target_pairs={{0,4},{4,0},{8,12},{12,8},{16,20},{20,16},{24,28},{28,24},{1,5},{5... | collective-permute-start | bytes 983048 | tf_op jit(solution)/shard_map/ppermute | solution.py:453
  67.9 1.2 %collective-permute-start.22 = (bf16[160,1024]{1,0:T(8,128)(2,1)S(1)}, bf16[160,1024]{1,0:T(8,128)(2,1)S(1)}, u32[]{:S(2)}, u32[]{:S(2)}) collective-permute-start(bf16[160,1024]{1,0:T(8,128)(2,1)S(1)} %get-tuple-element.88.refs_2_), channel_id=1, source_target_pairs={{0,8},{4,20},{8,0},{12,28},{16,24},{20,4},{24,16},{28,12},{1,9},{5... | collective-permute-start | bytes 983048 | tf_op jit(solution)/shard_map/ppermute | solution.py:462
  69.0 0.1 collective-permute-done.18.refs_2_
  69.1 0.3 blend.6
  69.5 1.1 %collective-permute-start.19 = (bf16[40,1024]{1,0:T(8,128)(2,1)S(1)}, bf16[40,1024]{1,0:T(8,128)(2,1)S(1)}, u32[]{:S(2)}, u32[]{:S(2)}) collective-permute-start(bf16[40,1024]{1,0:T(8,128)(2,1)S(1)} %get-tuple-element.90), channel_id=1, source_target_pairs={{0,1},{1,0},{2,3},{3,2},{4,5},{5,4},{6,7},{7,6},{8,9},{9,8},{10,11... | collective-permute-start | bytes 245768 | tf_op jit(solution)/shard_map/ppermute | solution.py:456
  70.5 2.1 %collective-permute-start.20 = (bf16[40,1024]{1,0:T(8,128)(2,1)S(1)}, bf16[40,1024]{1,0:T(8,128)(2,1)S(1)}, u32[]{:S(2)}, u32[]{:S(2)}) collective-permute-start(bf16[40,1024]{1,0:T(8,128)(2,1)S(1)} %get-tuple-element.91), channel_id=1, source_target_pairs={{0,2},{1,3},{2,0},{3,1},{4,6},{5,7},{6,4},{7,5},{8,10},{9,11},{10,... | collective-permute-start | bytes 245768 | tf_op jit(solution)/shard_map/ppermute | solution.py:456
  72.6 2.4 %collective-permute-done.22.refs_1_ = bf16[160,1024]{1,0:T(8,128)(2,1)S(1)} collective-permute-done((bf16[160,1024]{1,0:T(8,128)(2,1)S(1)}, bf16[160,1024]{1,0:T(8,128)(2,1)S(1)}, u32[]{:S(2)}, u32[]{:S(2)}) %collective-permute-start.22) | collective-permute-done | bytes 327712 | tf_op jit(solution)/shard_map/ppermute | solution.py:462
  75.0 0.1 add.12.refs_3_.refs_1_
  75.0 0.1 collective-permute-start.23
  75.1 0.2 collective-permute-done.19.refs_1_.refs_4_
  75.3 2.1 %collective-permute-done.20.refs_2_.refs_5_ = bf16[40,1024]{1,0:T(8,128)(2,1)S(1)} collective-permute-done((bf16[40,1024]{1,0:T(8,128)(2,1)S(1)}, bf16[40,1024]{1,0:T(8,128)(2,1)S(1)}, u32[]{:S(2)}, u32[]{:S(2)}) %collective-permute-start.20) | collective-permute-done | bytes 81952 | tf_op jit(solution)/shard_map/ppermute | solution.py:456
  77.4 0.3 blend.7
  77.8 0.1 collective-permute-start.27
  77.9 2.1 %collective-permute-start.21 = (bf16[40,1024]{1,0:T(8,128)(2,1)S(1)}, bf16[40,1024]{1,0:T(8,128)(2,1)S(1)}, u32[]{:S(2)}, u32[]{:S(2)}) collective-permute-start(bf16[40,1024]{1,0:T(8,128)(2,1)S(1)} %get-tuple-element.92), channel_id=1, source_target_pairs={{0,3},{1,2},{2,1},{3,0},{4,7},{5,6},{6,5},{7,4},{8,11},{9,10},{10,... | collective-permute-start | bytes 245768 | tf_op jit(solution)/shard_map/ppermute | solution.py:456
  80.0 2.3 %collective-permute-start.25 = (bf16[40,1024]{1,0:T(8,128)(2,1)S(1)}, bf16[40,1024]{1,0:T(8,128)(2,1)S(1)}, u32[]{:S(2)}, u32[]{:S(2)}) collective-permute-start(bf16[40,1024]{1,0:T(8,128)(2,1)S(1)} %get-tuple-element.96), channel_id=1, source_target_pairs={{0,2},{1,3},{2,0},{3,1},{4,6},{5,7},{6,4},{7,5},{8,10},{9,11},{10,... | collective-permute-start | bytes 245768 | tf_op jit(solution)/shard_map/ppermute | solution.py:456
  82.3 2.1 %collective-permute-start.26 = (bf16[40,1024]{1,0:T(8,128)(2,1)S(1)}, bf16[40,1024]{1,0:T(8,128)(2,1)S(1)}, u32[]{:S(2)}, u32[]{:S(2)}) collective-permute-start(bf16[40,1024]{1,0:T(8,128)(2,1)S(1)} %get-tuple-element.97), channel_id=1, source_target_pairs={{0,3},{1,2},{2,1},{3,0},{4,7},{5,6},{6,5},{7,4},{8,11},{9,10},{10,... | collective-permute-start | bytes 245768 | tf_op jit(solution)/shard_map/ppermute | solution.py:456
  84.4 1.7 %finish.1 = (bf16[2,1024,512]{2,1,0:T(8,128)(2,1)}, bf16[2,1024,512]{2,1,0:T(8,128)(2,1)}, bf16[2,512,1024]{2,1,0:T(8,128)(2,1)}, bf16[16,128]{1,0:T(8,128)(2,1)S(1)}) custom-call(s32[1]{0:T(128)} %bitcast.3.refs_0_.refs_2_, bf16[3,1024,512]{2,1,0:T(8,128)(2,1)S(1)} %collective-permute-done.27.refs_1_, ...), custom_call_target="tpu_custom_call", output_to_operand_aliasing={{0}: (2, {}), {1}: (3, {}), {2}: (4, {})} | custom-call | tf_op jit(solution)/shard_map/finish/pallas_call | solution.py:53
  86.1 2.2 %collective-permute-done.24.refs_8_ = bf16[40,1024]{1,0:T(8,128)(2,1)S(1)} collective-permute-done((bf16[40,1024]{1,0:T(8,128)(2,1)S(1)}, bf16[40,1024]{1,0:T(8,128)(2,1)S(1)}, u32[]{:S(2)}, u32[]{:S(2)}) %collective-permute-start.24) | collective-permute-done | bytes 81952 | tf_op jit(solution)/shard_map/ppermute | solution.py:456
  88.3 1.7 %collective-permute-done.25.refs_9_ = bf16[40,1024]{1,0:T(8,128)(2,1)S(1)} collective-permute-done((bf16[40,1024]{1,0:T(8,128)(2,1)S(1)}, bf16[40,1024]{1,0:T(8,128)(2,1)S(1)}, u32[]{:S(2)}, u32[]{:S(2)}) %collective-permute-start.25) | collective-permute-done | bytes 81952 | tf_op jit(solution)/shard_map/ppermute | solution.py:456
  90.0 1.0 %combine_both.1 = (bf16[64,1024]{1,0:T(8,128)(2,1)}, bf16[64,1024]{1,0:T(8,128)(2,1)}) custom-call(bf16[160,64]{1,0:T(8,128)(2,1)S(1)} %get-tuple-element.58.refs_0_, bf16[160,64]{1,0:T(8,128)(2,1)S(1)} %get-tuple-element.59.refs_1_, bf16[160,64]{1,0:T(8,128)(2,1)S(1)} %get-tuple-element.60.refs_2_, ...), custom_call_target="tpu_custom_call" | custom-call | tf_op jit(solution)/shard_map/combine_both/pallas_call | solution.py:53
  (27 shorter events, 0.2 us)
Async XLA Ops:
  0.6 27.0 %copy-start = (bf16[2,1024,512]{2,1,0:T(8,128)(2,1)S(1)}, bf16[2,1024,512]{2,1,0:T(8,128)(2,1)}, u32[]{:S(2)}) copy-start(bf16[2,1024,512]{2,1,0:T(8,128)(2,1)} %refs_3_.5) | copy-start | bytes 6291460
  0.6 1.1 %copy-start.3 = (bf16[64,1024]{1,0:T(8,128)(2,1)S(1)}, bf16[64,1024]{1,0:T(8,128)(2,1)}, u32[]{:S(2)}) copy-start(bf16[64,1024]{1,0:T(8,128)(2,1)} %refs_2_.1) | copy-start | bytes 393220
  1.7 0.7 copy-start.5
  2.9 2.8 %collective-permute-start = (bf16[160,1024]{1,0:T(8,128)(2,1)S(1)}, bf16[160,1024]{1,0:T(8,128)(2,1)S(1)}, u32[]{:S(2)}, u32[]{:S(2)}) collective-permute-start(bf16[160,1024]{1,0:T(8,128)(2,1)S(1)} %get-tuple-element.57.refs_4_.refs_1_), channel_id=1, source_target_pairs={{0,4},{4,0},{8,12},{12,8},{16,20},{20,16},{24,28},{28,24},{1,5},{5... | collective-permute-start | bytes 983048 | tf_op jit(solution)/shard_map/ppermute | solution.py:453
  3.5 0.9 copy-start.4
  4.4 0.7 copy-start.6
  5.6 6.2 %collective-permute-start.4 = (bf16[160,1024]{1,0:T(8,128)(2,1)S(1)}, bf16[160,1024]{1,0:T(8,128)(2,1)S(1)}, u32[]{:S(2)}, u32[]{:S(2)}) collective-permute-start(bf16[160,1024]{1,0:T(8,128)(2,1)S(1)} %get-tuple-element.65.refs_1_), channel_id=1, source_target_pairs={{0,4},{4,0},{8,12},{12,8},{16,20},{20,16},{24,28},{28,24},{1,5},{5... | collective-permute-start | bytes 983048 | tf_op jit(solution)/shard_map/ppermute | solution.py:453
  6.1 6.0 %collective-permute-start.1 = (bf16[40,1024]{1,0:T(8,128)(2,1)S(1)}, bf16[40,1024]{1,0:T(8,128)(2,1)S(1)}, u32[]{:S(2)}, u32[]{:S(2)}) collective-permute-start(bf16[40,1024]{1,0:T(8,128)(2,1)S(1)} %get-tuple-element.62), channel_id=1, source_target_pairs={{0,1},{1,0},{2,3},{3,2},{4,5},{5,4},{6,7},{7,6},{8,9},{9,8},{10,11... | collective-permute-start | bytes 245768 | tf_op jit(solution)/shard_map/ppermute | solution.py:456
  9.2 9.4 %collective-permute-start.2 = (bf16[40,1024]{1,0:T(8,128)(2,1)S(1)}, bf16[40,1024]{1,0:T(8,128)(2,1)S(1)}, u32[]{:S(2)}, u32[]{:S(2)}) collective-permute-start(bf16[40,1024]{1,0:T(8,128)(2,1)S(1)} %get-tuple-element.63), channel_id=1, source_target_pairs={{0,2},{1,3},{2,0},{3,1},{4,6},{5,7},{6,4},{7,5},{8,10},{9,11},{10,... | collective-permute-start | bytes 245768 | tf_op jit(solution)/shard_map/ppermute | solution.py:456
  11.8 6.8 %collective-permute-start.3 = (bf16[40,1024]{1,0:T(8,128)(2,1)S(1)}, bf16[40,1024]{1,0:T(8,128)(2,1)S(1)}, u32[]{:S(2)}, u32[]{:S(2)}) collective-permute-start(bf16[40,1024]{1,0:T(8,128)(2,1)S(1)} %get-tuple-element.64), channel_id=1, source_target_pairs={{0,3},{1,2},{2,1},{3,0},{4,7},{5,6},{6,5},{7,4},{8,11},{9,10},{10,... | collective-permute-start | bytes 245768 | tf_op jit(solution)/shard_map/ppermute | solution.py:456
  18.6 7.3 %collective-permute-start.5 = (bf16[160,1024]{1,0:T(8,128)(2,1)S(1)}, bf16[160,1024]{1,0:T(8,128)(2,1)S(1)}, u32[]{:S(2)}, u32[]{:S(2)}) collective-permute-start(bf16[160,1024]{1,0:T(8,128)(2,1)S(1)} %join.5.refs_0_.refs_4_), channel_id=1, source_target_pairs={{0,8},{4,20},{8,0},{12,28},{16,24},{20,4},{24,16},{28,12},{1,9},{5... | collective-permute-start | bytes 983048 | tf_op jit(solution)/shard_map/ppermute | solution.py:462
  20.2 7.4 %collective-permute-start.11 = (bf16[40,1024]{1,0:T(8,128)(2,1)S(1)}, bf16[40,1024]{1,0:T(8,128)(2,1)S(1)}, u32[]{:S(2)}, u32[]{:S(2)}) collective-permute-start(bf16[40,1024]{1,0:T(8,128)(2,1)S(1)} %get-tuple-element.72), channel_id=1, source_target_pairs={{0,1},{1,0},{2,3},{3,2},{4,5},{5,4},{6,7},{7,6},{8,9},{9,8},{10,11... | collective-permute-start | bytes 245768 | tf_op jit(solution)/shard_map/ppermute | solution.py:456
  21.7 8.2 %collective-permute-start.12 = (bf16[40,1024]{1,0:T(8,128)(2,1)S(1)}, bf16[40,1024]{1,0:T(8,128)(2,1)S(1)}, u32[]{:S(2)}, u32[]{:S(2)}) collective-permute-start(bf16[40,1024]{1,0:T(8,128)(2,1)S(1)} %get-tuple-element.73), channel_id=1, source_target_pairs={{0,2},{1,3},{2,0},{3,1},{4,6},{5,7},{6,4},{7,5},{8,10},{9,11},{10,... | collective-permute-start | bytes 245768 | tf_op jit(solution)/shard_map/ppermute | solution.py:456
  23.2 6.7 %collective-permute-start.13 = (bf16[40,1024]{1,0:T(8,128)(2,1)S(1)}, bf16[40,1024]{1,0:T(8,128)(2,1)S(1)}, u32[]{:S(2)}, u32[]{:S(2)}) collective-permute-start(bf16[40,1024]{1,0:T(8,128)(2,1)S(1)} %get-tuple-element.74), channel_id=1, source_target_pairs={{0,3},{1,2},{2,1},{3,0},{4,7},{5,6},{6,5},{7,4},{8,11},{9,10},{10,... | collective-permute-start | bytes 245768 | tf_op jit(solution)/shard_map/ppermute | solution.py:456
  26.0 14.2 %copy-start.1 = (bf16[2,1024,512]{2,1,0:T(8,128)(2,1)S(1)}, bf16[2,1024,512]{2,1,0:T(8,128)(2,1)}, u32[]{:S(2)}) copy-start(bf16[2,1024,512]{2,1,0:T(8,128)(2,1)} %refs_4_.3) | copy-start | bytes 6291460
  26.0 14.2 %copy-start.2 = (bf16[2,512,1024]{2,1,0:T(8,128)(2,1)S(1)}, bf16[2,512,1024]{2,1,0:T(8,128)(2,1)}, u32[]{:S(2)}) copy-start(bf16[2,512,1024]{2,1,0:T(8,128)(2,1)} %refs_5_.3) | copy-start | bytes 6291460
  26.0 14.2 %collective-permute-start.6 = (bf16[320,1024]{1,0:T(8,128)(2,1)S(1)}, bf16[320,1024]{1,0:T(8,128)(2,1)S(1)}, u32[]{:S(2)}, u32[]{:S(2)}) collective-permute-start(bf16[320,1024]{1,0:T(8,128)(2,1)S(1)} %join.6.refs_0_.refs_2_), channel_id=1, source_target_pairs={{0,16},{4,12},{8,24},{12,4},{16,0},{20,28},{24,8},{28,20},{1,17},{... | collective-permute-start | bytes 1966088 | tf_op jit(solution)/shard_map/ppermute | solution.py:462
  27.6 12.6 %collective-permute-start.7 = (bf16[2,1024,512]{2,1,0:T(8,128)(2,1)S(1)}, bf16[2,1024,512]{2,1,0:T(8,128)(2,1)S(1)}, u32[]{:S(2)}, u32[]{:S(2)}) collective-permute-start(bf16[2,1024,512]{2,1,0:T(8,128)(2,1)S(1)} %copy-done), channel_id=1, source_target_pairs={{0,4},{4,0},{8,12},{12,8},{16,20},{20,16},{24,28},{28,24},{1,5},{5... | collective-permute-start | bytes 6291464 | tf_op jit(solution)/shard_map/ppermute | solution.py:453
  27.6 12.6 %collective-permute-start.8 = (bf16[2,1024,512]{2,1,0:T(8,128)(2,1)}, bf16[2,1024,512]{2,1,0:T(8,128)(2,1)S(1)}, u32[]{:S(2)}, u32[]{:S(2)}) collective-permute-start(bf16[2,1024,512]{2,1,0:T(8,128)(2,1)} %refs_4_.3), channel_id=1, source_target_pairs={{0,4},{4,0},{8,12},{12,8},{16,20},{20,16},{24,28},{28,24},{1,5},{5... | collective-permute-start | bytes 6291464 | tf_op jit(solution)/shard_map/ppermute | solution.py:453
  29.9 10.3 %collective-permute-start.9 = (bf16[2,512,1024]{2,1,0:T(8,128)(2,1)}, bf16[2,512,1024]{2,1,0:T(8,128)(2,1)S(1)}, u32[]{:S(2)}, u32[]{:S(2)}) collective-permute-start(bf16[2,512,1024]{2,1,0:T(8,128)(2,1)} %refs_5_.3), channel_id=1, source_target_pairs={{0,4},{4,0},{8,12},{12,8},{16,20},{20,16},{24,28},{28,24},{1,5},{5... | collective-permute-start | bytes 6291464 | tf_op jit(solution)/shard_map/ppermute | solution.py:453
  29.9 7.1 %collective-permute-start.14 = (bf16[160,1024]{1,0:T(8,128)(2,1)S(1)}, bf16[160,1024]{1,0:T(8,128)(2,1)S(1)}, u32[]{:S(2)}, u32[]{:S(2)}) collective-permute-start(bf16[160,1024]{1,0:T(8,128)(2,1)S(1)} %join.7.refs_0_), channel_id=1, source_target_pairs={{0,8},{4,20},{8,0},{12,28},{16,24},{20,4},{24,16},{28,12},{1,9},{5... | collective-permute-start | bytes 983048 | tf_op jit(solution)/shard_map/ppermute | solution.py:462
  37.1 10.7 %collective-permute-start.15 = (bf16[320,1024]{1,0:T(8,128)(2,1)S(1)}, bf16[320,1024]{1,0:T(8,128)(2,1)S(1)}, u32[]{:S(2)}, u32[]{:S(2)}) collective-permute-start(bf16[320,1024]{1,0:T(8,128)(2,1)S(1)} %join.8.refs_0_), channel_id=1, source_target_pairs={{0,16},{4,12},{8,24},{12,4},{16,0},{20,28},{24,8},{28,20},{1,17},{... | collective-permute-start | bytes 1966088 | tf_op jit(solution)/shard_map/ppermute | solution.py:462
  45.1 10.7 %collective-permute-start.10 = (bf16[320,1024]{1,0:T(8,128)(2,1)S(1)}, bf16[320,1024]{1,0:T(8,128)(2,1)S(1)}, u32[]{:S(2)}, u32[]{:S(2)}) collective-permute-start(bf16[320,1024]{1,0:T(8,128)(2,1)S(1)} %get-tuple-element.71), channel_id=1, source_target_pairs={{0,16},{4,12},{8,24},{12,4},{16,0},{20,28},{24,8},{28,20},{1,17},{... | collective-permute-start | bytes 1966088 | tf_op jit(solution)/shard_map/ppermute | solution.py:462
  52.2 13.4 %collective-permute-start.17 = (bf16[320,1024]{1,0:T(8,128)(2,1)S(1)}, bf16[320,1024]{1,0:T(8,128)(2,1)S(1)}, u32[]{:S(2)}, u32[]{:S(2)}) collective-permute-start(bf16[320,1024]{1,0:T(8,128)(2,1)S(1)} %get-tuple-element.81), channel_id=1, source_target_pairs={{0,16},{4,12},{8,24},{12,4},{16,0},{20,28},{24,8},{28,20},{1,17},{... | collective-permute-start | bytes 1966088 | tf_op jit(solution)/shard_map/ppermute | solution.py:462
  55.9 10.7 %collective-permute-start.16 = (bf16[160,1024]{1,0:T(8,128)(2,1)S(1)}, bf16[160,1024]{1,0:T(8,128)(2,1)S(1)}, u32[]{:S(2)}, u32[]{:S(2)}) collective-permute-start(bf16[160,1024]{1,0:T(8,128)(2,1)S(1)} %get-tuple-element.79.refs_6_), channel_id=1, source_target_pairs={{0,8},{4,20},{8,0},{12,28},{16,24},{20,4},{24,16},{28,12},{1,9},{5... | collective-permute-start | bytes 983048 | tf_op jit(solution)/shard_map/ppermute | solution.py:462
  66.7 2.4 %collective-permute-start.18 = (bf16[160,1024]{1,0:T(8,128)(2,1)S(1)}, bf16[160,1024]{1,0:T(8,128)(2,1)S(1)}, u32[]{:S(2)}, u32[]{:S(2)}) collective-permute-start(bf16[160,1024]{1,0:T(8,128)(2,1)S(1)} %add.11.refs_1_), channel_id=1, source_target_pairs={{0,4},{4,0},{8,12},{12,8},{16,20},{20,16},{24,28},{28,24},{1,5},{5... | collective-permute-start | bytes 983048 | tf_op jit(solution)/shard_map/ppermute | solution.py:453
  67.9 7.1 %collective-permute-start.22 = (bf16[160,1024]{1,0:T(8,128)(2,1)S(1)}, bf16[160,1024]{1,0:T(8,128)(2,1)S(1)}, u32[]{:S(2)}, u32[]{:S(2)}) collective-permute-start(bf16[160,1024]{1,0:T(8,128)(2,1)S(1)} %get-tuple-element.88.refs_2_), channel_id=1, source_target_pairs={{0,8},{4,20},{8,0},{12,28},{16,24},{20,4},{24,16},{28,12},{1,9},{5... | collective-permute-start | bytes 983048 | tf_op jit(solution)/shard_map/ppermute | solution.py:462
  69.5 5.8 %collective-permute-start.19 = (bf16[40,1024]{1,0:T(8,128)(2,1)S(1)}, bf16[40,1024]{1,0:T(8,128)(2,1)S(1)}, u32[]{:S(2)}, u32[]{:S(2)}) collective-permute-start(bf16[40,1024]{1,0:T(8,128)(2,1)S(1)} %get-tuple-element.90), channel_id=1, source_target_pairs={{0,1},{1,0},{2,3},{3,2},{4,5},{5,4},{6,7},{7,6},{8,9},{9,8},{10,11... | collective-permute-start | bytes 245768 | tf_op jit(solution)/shard_map/ppermute | solution.py:456
  70.5 6.9 %collective-permute-start.20 = (bf16[40,1024]{1,0:T(8,128)(2,1)S(1)}, bf16[40,1024]{1,0:T(8,128)(2,1)S(1)}, u32[]{:S(2)}, u32[]{:S(2)}) collective-permute-start(bf16[40,1024]{1,0:T(8,128)(2,1)S(1)} %get-tuple-element.91), channel_id=1, source_target_pairs={{0,2},{1,3},{2,0},{3,1},{4,6},{5,7},{6,4},{7,5},{8,10},{9,11},{10,... | collective-permute-start | bytes 245768 | tf_op jit(solution)/shard_map/ppermute | solution.py:456
  75.0 2.4 %collective-permute-start.23 = (bf16[160,1024]{1,0:T(8,128)(2,1)S(1)}, bf16[160,1024]{1,0:T(8,128)(2,1)S(1)}, u32[]{:S(2)}, u32[]{:S(2)}) collective-permute-start(bf16[160,1024]{1,0:T(8,128)(2,1)S(1)} %add.12.refs_3_.refs_1_), channel_id=1, source_target_pairs={{0,4},{4,0},{8,12},{12,8},{16,20},{20,16},{24,28},{28,24},{1,5},{5... | collective-permute-start | bytes 983048 | tf_op jit(solution)/shard_map/ppermute | solution.py:453
  77.8 6.6 %collective-permute-start.27 = (bf16[3,1024,512]{2,1,0:T(8,128)(2,1)S(1)}, bf16[3,1024,512]{2,1,0:T(8,128)(2,1)S(1)}, u32[]{:S(2)}, u32[]{:S(2)}) collective-permute-start(bf16[3,1024,512]{2,1,0:T(8,128)(2,1)S(1)} %get-tuple-element.99), channel_id=1, source_target_pairs={{0,4},{4,0},{8,12},{12,8},{16,20},{20,16},{24,28},{28,24},{1,5},{5... | collective-permute-start | bytes 9437192 | tf_op jit(solution)/shard_map/ppermute | solution.py:453
  77.9 8.2 %collective-permute-start.21 = (bf16[40,1024]{1,0:T(8,128)(2,1)S(1)}, bf16[40,1024]{1,0:T(8,128)(2,1)S(1)}, u32[]{:S(2)}, u32[]{:S(2)}) collective-permute-start(bf16[40,1024]{1,0:T(8,128)(2,1)S(1)} %get-tuple-element.92), channel_id=1, source_target_pairs={{0,3},{1,2},{2,1},{3,0},{4,7},{5,6},{6,5},{7,4},{8,11},{9,10},{10,... | collective-permute-start | bytes 245768 | tf_op jit(solution)/shard_map/ppermute | solution.py:456
  80.0 8.3 %collective-permute-start.24 = (bf16[40,1024]{1,0:T(8,128)(2,1)S(1)}, bf16[40,1024]{1,0:T(8,128)(2,1)S(1)}, u32[]{:S(2)}, u32[]{:S(2)}) collective-permute-start(bf16[40,1024]{1,0:T(8,128)(2,1)S(1)} %get-tuple-element.95), channel_id=1, source_target_pairs={{0,1},{1,0},{2,3},{3,2},{4,5},{5,4},{6,7},{7,6},{8,9},{9,8},{10,11... | collective-permute-start | bytes 245768 | tf_op jit(solution)/shard_map/ppermute | solution.py:456
  80.0 10.0 %collective-permute-start.25 = (bf16[40,1024]{1,0:T(8,128)(2,1)S(1)}, bf16[40,1024]{1,0:T(8,128)(2,1)S(1)}, u32[]{:S(2)}, u32[]{:S(2)}) collective-permute-start(bf16[40,1024]{1,0:T(8,128)(2,1)S(1)} %get-tuple-element.96), channel_id=1, source_target_pairs={{0,2},{1,3},{2,0},{3,1},{4,6},{5,7},{6,4},{7,5},{8,10},{9,11},{10,... | collective-permute-start | bytes 245768 | tf_op jit(solution)/shard_map/ppermute | solution.py:456
  82.3 7.7 %collective-permute-start.26 = (bf16[40,1024]{1,0:T(8,128)(2,1)S(1)}, bf16[40,1024]{1,0:T(8,128)(2,1)S(1)}, u32[]{:S(2)}, u32[]{:S(2)}) collective-permute-start(bf16[40,1024]{1,0:T(8,128)(2,1)S(1)} %get-tuple-element.97), channel_id=1, source_target_pairs={{0,3},{1,2},{2,1},{3,0},{4,7},{5,6},{6,5},{7,4},{8,11},{9,10},{10,... | collective-permute-start | bytes 245768 | tf_op jit(solution)/shard_map/ppermute | solution.py:456
